TPU v7x, 32 devices: a whole 2x2x4 slice. The times are simulated.
32 devices in a mesh: parts: 2 (over x), sec: 8 (over z, y), tile: 2 (over core).
Axes of the slice: x: 2, y: 2, z: 4, core: 2. Of those that a mesh axis runs over, the one named last changes fastest.
Arguments:
- source: bfloat16 [16, 50, 256, 256], P(('parts', 'sec'), 'tile'), parts along dimension 0, may hold values from -6 to 6
- pull_ids: int32 [16, 50, 3], P(('parts', 'sec'), 'tile'), parts along dimension 0, may hold values from 0 to 49, as said below
- interp_idx: int32 [16, 50, 3, 2], P(('parts', 'sec'), 'tile'), parts along dimension 0, may hold values from 0 to 15
- interp_table: bfloat16 [16, 256, 256], replicated, may hold values from -0.375 to 0.375
- patch_pos: int32 [16, 50, 2], P(('parts', 'sec'), 'tile'), parts along dimension 0, may hold values from 0 to 1152
Outputs:
- warped: bfloat16 [16, 2560, 1280], P(('parts', 'sec'), 'tile'), parts along dimension 0
- correlations: float32 [16, 50, 128, 128], P(('parts', 'sec'), 'tile'), parts along dimension 0
There are 2 independent parts, one for each index of `parts`. A program takes and returns all parts, laid end to end along the dimension named above; an argument that names none is the same for every part. Nothing has to cross between parts.
Inputs may be any that keep to these rules, and one draw needn't show every extreme that they name: `pull_ids`: the tile that holds block id b is b // 25. In every tile at least 6 and at most 12 of its 75 pulls name blocks of the other tile of its section, and some tile of every part has exactly 12; the other pulls name its own blocks.
All inputs are finite; a program needn't handle non-finite values.
Results may differ from a plain program's by a relative error of at most 0.012.
Values may be sent and summed in bfloat16 or wider, within the bound.
No kernel may reach another device: no remote copies, remote signals or barrier semaphores. Data moves between devices by JAX's collectives and lax.ppermute only.
A program may use at most 128 MiB of HBM per device.

v0:
```python
import math

import jax
import jax.numpy as jnp
from jax import lax
from jax.sharding import PartitionSpec as P

BS = 256
PS = 128
GRID = 5
KP = 3


EPSILON = 1e-06


def from_behind(array, axis, by):
    size = lax.axis_size(axis)
    pairs = [(i, i + by) for i in range(size) if 0 <= i + by < size]
    return lax.ppermute(array, axis, pairs)


def extract(picture, corners):
    count = corners.shape[0]
    width = picture.shape[1]
    offsets = jnp.arange(PS, dtype=jnp.int32)
    row_index = (corners[:, 0:1] + offsets[None, :]).reshape(-1)
    band = jnp.take(picture, row_index, axis=0).reshape(count, PS, width)
    column_index = corners[:, 1:2] + offsets[None, :]
    columns_all = jnp.arange(width, dtype=jnp.int32)
    picker = (columns_all[None, :, None] == column_index[:, None, :]).astype(jnp.bfloat16)
    windows = jnp.einsum("prc,pcq->prq", band, picker, preferred_element_type=jnp.float32)
    return windows.astype(jnp.bfloat16)


def product(left_matrix, right_matrix):
    return jnp.matmul(left_matrix, right_matrix, precision=lax.Precision.HIGH)


def correlate(own_patches, previous):
    first = own_patches.astype(jnp.float32)
    first = first - jnp.mean(first, axis=(1, 2), keepdims=True)
    second = previous.astype(jnp.float32)
    second = second - jnp.mean(second, axis=(1, 2), keepdims=True)
    count = first.shape[0]
    index_range = jnp.arange(PS, dtype=jnp.int32)
    phase = index_range[:, None] * index_range[None, :] % PS
    angle = 2.0 * math.pi / PS * phase.astype(jnp.float32)
    cosine = jnp.cos(angle)
    sine_table = jnp.sin(angle)
    row_stack = jnp.concatenate([cosine, sine_table], axis=0)
    column_stack = jnp.concatenate([cosine, sine_table], axis=1)
    fields = jnp.concatenate([first, second], axis=0)
    halves = product(row_stack, fields)
    quarters = product(halves, column_stack)
    real_part = quarters[:, :PS, :PS] - quarters[:, PS:, PS:]
    imag_part = -(quarters[:, :PS, PS:] + quarters[:, PS:, :PS])
    real_one, real_two = (real_part[:count], real_part[count:])
    imag_one, imag_two = (imag_part[:count], imag_part[count:])
    cross_real = real_one * real_two + imag_one * imag_two
    cross_imag = imag_one * real_two - real_one * imag_two
    inverse_left = jnp.concatenate(
        [
            jnp.concatenate([cosine, -sine_table], axis=1),
            jnp.concatenate([sine_table, cosine], axis=1),
        ],
        axis=0,
    )
    stacked_cross = jnp.concatenate([cross_real, cross_imag], axis=1)
    mixed = product(inverse_left, stacked_cross)
    side_by_side = jnp.concatenate([mixed[:, :PS], mixed[:, PS:]], axis=2)
    inverse_right = jnp.concatenate([cosine, -sine_table], axis=0)
    circular = product(side_by_side, inverse_right) / (PS * PS)
    scale = PS * jnp.sqrt(
        (jnp.mean(first * first, axis=(1, 2)) + EPSILON)
        * (jnp.mean(second * second, axis=(1, 2)) + EPSILON)
    )
    return circular / scale[:, None, None]


def shards(source, pull_ids, interp_idx, interp_table, patch_pos):
    blocks = source[0]
    block_ids = pull_ids[0].reshape(-1)
    section = lax.all_gather(blocks, "tile", axis=0, tiled=True)
    pulled = section[block_ids]
    matrix_index = interp_idx[0].reshape(-1, 2)
    left_product = jnp.einsum(
        "rij,rjk->rik", interp_table[matrix_index[:, 0]], pulled, preferred_element_type=jnp.float32
    ).astype(jnp.bfloat16)
    summed_terms = jnp.einsum(
        "rik,rlk->ril",
        left_product,
        interp_table[matrix_index[:, 1]],
        preferred_element_type=jnp.float32,
    )
    blocks_out = summed_terms.reshape(GRID * GRID, KP, BS, BS).sum(axis=1).astype(jnp.bfloat16)
    warped_tile = (
        blocks_out.reshape(GRID, GRID, BS, BS).transpose(0, 2, 1, 3).reshape(GRID * BS, GRID * BS)
    )
    positions = patch_pos[0]
    own_patches = extract(warped_tile, positions)
    earlier_tile = from_behind(warped_tile, "sec", 1)
    previous = extract(earlier_tile, positions)
    correlations = correlate(own_patches, previous)
    return (warped_tile[None], correlations[None])


def solution(mesh):
    return jax.shard_map(
        shards,
        mesh=mesh,
        in_specs=(
            P(("parts", "sec"), "tile", None, None),
            P(("parts", "sec"), "tile", None),
            P(("parts", "sec"), "tile", None, None),
            P(),
            P(("parts", "sec"), "tile", None),
        ),
        out_specs=(P(("parts", "sec"), "tile", None), P(("parts", "sec"), "tile", None, None)),
        check_vma=False,
    )
```

profile of v0, /device:TPU:10, one launch (start us, length us, event | category | flops | bytes accessed | tf_op | source)
XLA Modules:
  0.0 223.3 jit_solution(5426929600169359905)
XLA Ops:
  8.8 6.0 %gather_fusion = bf16[75,256,256]{2,1,0:T(8,128)(2,1)} fusion(bf16[16,256,256]{2,1,0:T(8,128)(2,1)S(1)} %copy-done, s32[1024]{0:T(1024)S(1)} %get-tuple-element.24), kind=kCustom, calls=%fused_computation.2 | custom fusion | bytes 19661100 | tf_op jit(solution)/shard_map/gather | solution.py:88
  14.8 7.2 %gather_fusion.2 = bf16[75,256,256]{2,1,0:T(8,128)(2,1)} fusion(bf16[16,256,256]{2,1,0:T(8,128)(2,1)S(1)} %copy-done, s32[1024]{0:T(1024)S(1)} %get-tuple-element.23), kind=kCustom, calls=%fused_computation.4 | custom fusion | bytes 19661100 | tf_op jit(solution)/shard_map/gather | solution.py:93
  22.2 5.9 %all-gather.3.cloned.1.call-done = bf16[1,50,256,256]{3,2,0,1:T(8,128)(2,1)} async-done(((bf16[1,25,256,256]{3,2,0,1:T(8,128)(2,1)}), bf16[1,50,256,256]{3,2,0,1:T(8,128)(2,1)}) %all-gather.3.cloned.1.call-update) | async-done | bytes 6553616 | tf_op jit(solution)/shard_map/all_gather | solution.py:84
  28.1 8.9 %gather_fusion.1 = bf16[75,256,256]{2,1,0:T(8,128)(2,1)} fusion(bf16[50,256,256]{2,1,0:T(8,128)(2,1)} %bitcast.58, s32[1024]{0:T(1024)S(1)} %pad_clamp_fusion.2), kind=kCustom, calls=%fused_computation.3 | custom fusion | bytes 19661100 | tf_op jit(solution)/shard_map/gather | solution.py:85
  37.0 19.1 %fusion.2 = f32[75,256,256]{2,1,0:T(8,128)} fusion(bf16[75,256,256]{2,1,0:T(8,128)(2,1)} %gather_fusion.2, bf16[75,256,256]{2,1,0:T(8,128)(2,1)} %gather_fusion, bf16[75,256,256]{2,1,0:T(8,128)(2,1)} %gather_fusion.1), kind=kOutput, calls=%fused_computation.8 | convolution fusion | flops 5038080000 | bytes 49152000 | tf_op jit(solution)/shard_map/rik,rlk->ril/dot_general | solution.py:90
  56.1 8.6 %reduce_sum.45 = bf16[25,256,256]{2,1,0:T(8,128)(2,1)S(1)} reduce(f32[25,3,256,256]{3,2,1,0:T(8,128)} %bitcast.56, f32[]{:T(128)} %constant.40.clone.1), dimensions={1}, to_apply=%region_0.0 | reduce | flops 3276800 | bytes 22937604 | tf_op jit(solution)/shard_map/reduce_sum | solution.py:96
  64.7 2.2 copy.20
  66.9 1.5 copy.25
  68.4 0.8 copy-done.2
  69.2 3.6 %collective-permute-start = (bf16[1280,1280]{1,0:T(8,128)(2,1)S(1)}, bf16[1280,1280]{1,0:T(8,128)(2,1)}, u32[]{:S(2)}, u32[]{:S(2)}) collective-permute-start(bf16[1280,1280]{1,0:T(8,128)(2,1)S(1)} %bitcast.54), channel_id=1, source_target_pairs={{0,2},{2,4},{4,6},{6,8},{8,10},{10,12},{12,14},{1,3},{3,5},{5,7},{... | collective-permute-start | bytes 9830408 | tf_op jit(solution)/shard_map/ppermute | solution.py:20
  73.6 8.2 %broadcast_in_dim_reshape.3 = bf16[1,1280,1280]{2,1,0:T(8,128)(2,1)} reshape(bf16[5,256,5,256]{3,2,1,0:T(8,128)(2,1)} %copy-done.2) | data formatting | bytes 6553600 | tf_op jit(solution)/shard_map/broadcast_in_dim;reshape | solution.py:105
  81.8 11.6 %gather_fusion.3 = bf16[3200,1280]{1,0:T(8,128)(2,1)} fusion(bf16[1280,1280]{1,0:T(8,128)(2,1)S(1)} %bitcast.55, s32[4096]{0:T(1024)S(1)} %pad_clamp_fusion), kind=kCustom, calls=%fused_computation.clone | custom fusion | bytes 16396800 | tf_op jit(solution)/shard_map/jit(_take)/gather | solution.py:28
  93.3 51.9 %collective-permute-done = bf16[1280,1280]{1,0:T(8,128)(2,1)} collective-permute-done((bf16[1280,1280]{1,0:T(8,128)(2,1)S(1)}, bf16[1280,1280]{1,0:T(8,128)(2,1)}, u32[]{:S(2)}, u32[]{:S(2)}) %collective-permute-start) | collective-permute-done | bytes 3276832 | tf_op jit(solution)/shard_map/ppermute | solution.py:20
  145.2 20.2 %gather_fusion.4 = bf16[3200,1280]{1,0:T(8,128)(2,1)} fusion(bf16[1280,1280]{1,0:T(8,128)(2,1)} %collective-permute-done, s32[4096]{0:T(1024)S(1)} %pad_clamp_fusion), kind=kCustom, calls=%fused_computation.1.clone | custom fusion | bytes 16396800 | tf_op jit(solution)/shard_map/jit(_take)/gather | solution.py:28
  165.4 7.1 %broadcast_select_fusion.1 = (bf16[3200,1280]{1,0:T(8,128)(2,1)S(1)}, bf16[3200,1280]{1,0:T(8,128)(2,1)S(1)}) fusion(bf16[3200,1280]{1,0:T(8,128)(2,1)} %gather_fusion.3, pred[3200]{0:T(1024)(128)(4,1)S(1)} %compare_and_fusion, bf16[3200,1280]{1,0:T(8,128)(2,1)} %gather_fusion.4), kind=kLoop, calls=%fused_computation.14 | loop fusion | flops 8192000 | bytes 32771200 | tf_op jit(solution)/shard_map/jit(_take)/select_n | solution.py:28
  172.5 4.8 %convert_reduce_fusion.1 = (f32[25]{0:T(128)S(1)}, bf16[25,128,128]{2,1,0:T(8,128)(2,1)S(1)}) fusion(bf16[25,128,1280]{2,1,0:T(8,128)(2,1)S(1)} %bitcast.63, s32[25,128]{1,0:T(8,128)S(1)} %iota_add_fusion), kind=kOutput, calls=%fused_computation.32 | convolution fusion | flops 1053900800 | bytes 9024100 | tf_op jit(solution)/shard_map/prc,pcq->prq/dot_general | solution.py:32
  177.2 4.8 %convert_reduce_fusion = (f32[25]{0:T(128)S(1)}, bf16[25,128,128]{2,1,0:T(8,128)(2,1)S(1)}) fusion(bf16[25,128,1280]{2,1,0:T(8,128)(2,1)S(1)} %bitcast.62, s32[25,128]{1,0:T(8,128)S(1)} %iota_add_fusion), kind=kOutput, calls=%fused_computation.30 | convolution fusion | flops 1053900800 | bytes 9024100 | tf_op jit(solution)/shard_map/prc,pcq->prq/dot_general | solution.py:32
  182.9 3.1 %fusion.11 = f32[256,50,128]{2,0,1:T(8,128)S(1)} fusion(f32[25,128,128]{2,1,0:T(8,128)S(1)} %get-tuple-element.12, f32[25,128,128]{2,1,0:T(8,128)S(1)} %get-tuple-element.10, f32[128,128]{1,0:T(8,128)S(1)} %get-tuple-element.26, f32[128,128]{1,0:T(8,128)S(1)} %get-tuple-element.25), kind=kOutput, calls=%fused_computation.20 | convolution fusion | flops 1259143168 | bytes 9961472 | tf_op jit(solution)/shard_map/dot_general | solution.py:37
  186.0 13.5 %fusion.8 = f32[50,256,256]{2,1,0:T(8,128)S(1)} fusion(f32[256,50,128]{2,0,1:T(8,128)S(1)} %fusion.11, f32[128,128]{1,0:T(8,128)S(1)} %get-tuple-element.25, f32[128,128]{1,0:T(8,128)S(1)} %get-tuple-element.26), kind=kOutput, calls=%fused_computation.15 | convolution fusion | flops 2516615168 | bytes 19791872 | tf_op jit(solution)/shard_map/dot_general | solution.py:37
  199.5 2.6 %slice_subtract_fusion = (f32[50,128,128]{2,1,0:T(8,128)S(1)}, f32[50,128,128]{2,1,0:T(8,128)}) fusion(f32[50,256,256]{2,1,0:T(8,128)S(1)} %fusion.8), kind=kLoop, calls=%fused_computation.19 | loop fusion | flops 2457600 | bytes 19660800 | tf_op jit(solution)/shard_map/sub | solution.py:56
  202.1 2.6 %multiply_add_fusion = (f32[25,128,128]{2,1,0:T(8,128)S(1)}, f32[25,128,128]{2,1,0:T(8,128)S(1)}) fusion(f32[50,128,128]{2,1,0:T(8,128)} %get-tuple-element.4, f32[50,128,128]{2,1,0:T(8,128)S(1)} %get-tuple-element.3), kind=kLoop, calls=%fused_computation.37 | loop fusion | flops 2457600 | bytes 9830400 | tf_op jit(solution)/shard_map/add | solution.py:60
  205.1 3.2 %copy.22 = f32[25,256,128]{1,2,0:T(8,128)} copy(f32[25,256,128]{2,1,0:T(8,128)S(1)} %pad_maximum_fusion) | data formatting | bytes 6553600 | tf_op jit(solution)/shard_map/concatenate | solution.py:69
  208.3 3.4 %fusion.23 = f32[256,3200]{0,1:S(1)} fusion(f32[256,3200]{0,1:T(8,128)} %bitcast.61, f32[128,128]{1,0:T(8,128)S(1)} %get-tuple-element.26, f32[128,128]{1,0:T(8,128)S(1)} %get-tuple-element.25, f32[128,128]{1,0:T(8,128)S(1)} %fusion.47), kind=kOutput, calls=%fused_computation.40 | convolution fusion | flops 1258487808 | bytes 6750208
  212.2 4.0 %divide_bitcast_fusion = f32[1,25,128,128]{3,2,1,0:T(8,128)} fusion(f32[25,128,128]{1,2,0:T(8,128)S(1)} %get-tuple-element.8, f32[25,128,128]{1,2,0:T(8,128)S(1)} %get-tuple-element.7, f32[25]{0:T(128)S(1)} %sqrt_multiply_fusion, f32[128,128]{1,0:T(8,128)S(1)} %get-tuple-element.26, f32[128,128]{1,0:T(8,128)S(1)} %fusion.47), kind=kOutput, calls=%fused_computation.33 | convolution fusion | flops 630816768 | bytes 5046372 | tf_op jit(solution)/shard_map/dot_general | solution.py:37
  (35 shorter events, 4.2 us)
Async XLA Ops:
  7.2 1.6 copy-start
  7.2 0.8 copy-start.3
  7.2 21.0 %all-gather.3.cloned.1.call-start = ((), (), s32[]{:S(2)}) async-start(), calls=%async_computation | async-start | bytes 9830400 | tf_op jit(solution)/shard_map/all_gather | solution.py:84
  14.8 7.2 %copy-start.4 = (s32[1,25,3]{1,0,2:T(1,128)S(1)}, s32[1,25,3]{1,0,2:T(1,128)}, u32[]{:S(2)}) copy-start(s32[1,25,3]{1,0,2:T(1,128)} %param.8) | copy-start | bytes 904
  66.9 2.3 %copy-start.2 = (bf16[5,256,5,256]{3,2,1,0:T(8,128)(2,1)}, bf16[5,256,5,256]{3,2,1,0:T(8,128)(2,1)S(1)}, u32[]{:S(2)}) copy-start(bf16[5,256,5,256]{3,2,1,0:T(8,128)(2,1)S(1)} %copy.20) | copy-start | bytes 9830404
  66.9 5.9 %copy-start.5 = (s32[1,25,2]{1,2,0:T(2,128)S(1)}, s32[1,25,2]{1,2,0:T(2,128)}, u32[]{:S(2)}) copy-start(s32[1,25,2]{1,2,0:T(2,128)} %param.11) | copy-start | bytes 604
  69.2 76.0 %collective-permute-start = (bf16[1280,1280]{1,0:T(8,128)(2,1)S(1)}, bf16[1280,1280]{1,0:T(8,128)(2,1)}, u32[]{:S(2)}, u32[]{:S(2)}) collective-permute-start(bf16[1280,1280]{1,0:T(8,128)(2,1)S(1)} %bitcast.54), channel_id=1, source_target_pairs={{0,2},{2,4},{4,6},{6,8},{8,10},{10,12},{12,14},{1,3},{3,5},{5,7},{... | collective-permute-start | bytes 9830408 | tf_op jit(solution)/shard_map/ppermute | solution.py:20
  212.2 4.1 %copy-start.1 = (bf16[16,256,256]{2,1,0:T(8,128)(2,1)S(1)}, bf16[16,256,256]{2,1,0:T(8,128)(2,1)}, u32[]{:S(2)}) copy-start(bf16[16,256,256]{2,1,0:T(8,128)(2,1)} %param.10) | copy-start | bytes 6291460
Sparse Core Ops, SparseCore 0:
  9.6 18.5 all-gather.2
where the time goes:
time: 227 us; the launch traced here: 223 us
  local copies, waits for them, and re-layouts  71.1 us (31%)
  waiting for transfers between devices  58.5 us (26%)
  matrix products  52.7 us (23%)
  other arithmetic  22.9 us (10%)
  between operations  14.4 us (6%)
  starting transfers between devices  3.68 us (2%)
    ppermute x1, waiting for transfers between devices, from_behind(): return lax.ppermute(array, axis, pairs)  51.9 us
    gather x2, local copies, waits for them, and re-layouts, extract(): band = jnp.take(picture, row_index, axis=0).reshape(count, PS, width)  31.7 us
    dot_general x3, matrix products, product(): return jnp.matmul(left_matrix, right_matrix, precision=lax.Precision.HIGH)  20.6 us
    dot_general x1, matrix products, shards(): jnp.einsum('rik,rlk->ril', left_product, interp_table[matrix_index[:, 1]]...  19.1 us
    dot_general x2, matrix products, extract(): jnp.einsum('prc,pcq->prq', band, picker, preferred_element_type=jnp.float32)  9.52 us
    gather x1, local copies, waits for them, and re-layouts, shards(): pulled = section[block_ids]  8.89 us
    reduce_sum x1, other arithmetic, shards(): summed_terms.reshape(GRID * GRID, KP, BS, BS).sum(axis=1)  8.57 us
    another operation x1, local copies, waits for them, and re-layouts, shards(): return (warped_tile[None], correlations[None])  8.15 us
  transfers between devices with their start and end apart: 2, of which 2 were waited for; matrix products, arithmetic and copies ran while one was open for 15% of the time, Pallas kernels for 0%

commit v1 on v0

v1 whole, which is shorter than its diff:
```python
import functools

import jax
import jax.numpy as jnp
import ml_dtypes
import numpy as np
from jax import lax
from jax.experimental import pallas as pl
from jax.experimental.pallas import tpu as pltpu
from jax.sharding import PartitionSpec as P

BS = 256
PS = 128
KP = 3
EPSILON = 1e-06
CAP = 12
ROWS = PS + 16
COLS = 2 * PS

SMEM = pl.BlockSpec(memory_space=pltpu.SMEM)
VMEM = pl.BlockSpec(memory_space=pltpu.VMEM)
ANY = pl.BlockSpec(memory_space=pl.ANY)
F32 = jnp.float32
BF16 = jnp.bfloat16


def tables():
    grid = np.arange(PS)
    angle = 2.0 * np.pi / PS * (grid[:, None] * grid[None, :] % PS)
    cosine, sine = np.cos(angle), np.sin(angle)
    across = np.concatenate([cosine, sine], axis=1)
    high = across.astype(ml_dtypes.bfloat16)
    low = (across - high.astype(np.float64)).astype(ml_dtypes.bfloat16)
    forward = np.concatenate([high, low], axis=0)
    constant = forward.astype(np.float64).sum(axis=0, keepdims=True).astype(np.float32)
    down = np.block([[cosine, -sine], [sine, cosine]]).astype(ml_dtypes.bfloat16)
    back = np.concatenate([cosine, -sine], axis=0).astype(ml_dtypes.bfloat16)
    return forward, constant, down, back


def dot(a, b):
    return jnp.dot(a, b, preferred_element_type=F32)


def block_order(ids, order, tile, count):
    first, last = jnp.int32(0), jnp.int32(count - 1)
    for b in range(count):
        away = (ids[b, 0] // count != tile) | (ids[b, 1] // count != tile) | (ids[b, 2] // count != tile)
        order[jnp.where(away, last, first)] = b
        first = first + jnp.where(away, 0, 1)
        last = last - jnp.where(away, 1, 0)


def place(block, grid):
    row = pl.multiple_of(block // grid * BS, BS)
    col = pl.multiple_of(block % grid * BS, BS)
    return pl.ds(row, BS), pl.ds(col, BS)


def warp_blocks(blocks, ids, mats, table, slots, arrived, finish):
    for n, block in enumerate(blocks):
        for k in range(KP):
            arrived(n, k)
        total = None
        for k in range(KP):
            left = dot(table[mats[block, 2 * k]], slots[n * KP + k]).astype(BF16)
            term = lax.dot_general(
                left, table[mats[block, 2 * k + 1]], (((1,), (1,)), ((), ())), preferred_element_type=F32
            )
            total = term if total is None else total + term
        finish(n, block, total.astype(BF16))


def near_kernel(count, grid, ids, mats, source, table, warped, order, slots, done, in_sem, out_sem):
    tile = lax.axis_index("tile")
    near = count - CAP
    block_order(ids, order, tile, count)
    blocks = [order[n] for n in range(near)]

    def fetch(n, k):
        index = ids[blocks[n], k] - tile * count
        return pltpu.make_async_copy(source.at[index], slots.at[n * KP + k], in_sem.at[n * KP + k])

    for n in range(near):
        for k in range(KP):
            fetch(n, k).start()
    writes = []

    def finish(n, block, value):
        done[n] = value
        writes.append(pltpu.make_async_copy(done.at[n], warped.at[place(block, grid)], out_sem.at[n]))
        writes[-1].start()

    warp_blocks(blocks, ids, mats, table, slots, lambda n, k: fetch(n, k).wait(), finish)
    for write in writes:
        write.wait()


def window(picture, y, x):
    top = pl.multiple_of(jnp.minimum(y // 16 * 16, picture.shape[0] - ROWS), 16)
    left = pl.multiple_of(jnp.minimum(x // PS * PS, picture.shape[1] - COLS), PS)
    area = picture[pl.ds(top, ROWS), pl.ds(left, COLS)]
    i = lax.broadcasted_iota(jnp.int32, (PS, ROWS), 0)
    r = lax.broadcasted_iota(jnp.int32, (PS, ROWS), 1)
    pick_rows = (r - i == y - top).astype(F32).astype(BF16)
    c = lax.broadcasted_iota(jnp.int32, (COLS, PS), 0)
    j = lax.broadcasted_iota(jnp.int32, (COLS, PS), 1)
    pick_cols = (c - j == x - left).astype(F32).astype(BF16)
    return dot(dot(pick_rows, area).astype(BF16), pick_cols).astype(BF16)


def far_kernel(
    count, grid, patches, ids, mats, corners, source, other, table, begun, warped, out,
    order, slots, picture, in_sem, near_sem, out_sem,
):
    tile = lax.axis_index("tile")
    near = count - CAP
    block_order(ids, order, tile, count)
    blocks = [order[near + n] for n in range(CAP)]

    def fetch(n, k, act):
        index = ids[blocks[n], k]
        home = index // count
        slot, sem = slots.at[n * KP + k], in_sem.at[n * KP + k]

        @pl.when(home == tile)
        def _():
            act(pltpu.make_async_copy(source.at[index - home * count], slot, sem))

        @pl.when(home != tile)
        def _():
            act(pltpu.make_async_copy(other.at[index - home * count], slot, sem))

    for n in range(CAP):
        for k in range(KP):
            fetch(n, k, lambda copy: copy.start())
    loads = []
    for n in range(near):
        at = place(order[n], grid)
        loads.append(pltpu.make_async_copy(begun.at[at], picture.at[at], near_sem.at[n]))
        loads[-1].start()
    writes = []

    def arrived(n, k):
        pltpu.make_async_copy(source.at[0], slots.at[n * KP + k], in_sem.at[n * KP + k]).wait()

    def finish(n, block, value):
        at = place(block, grid)
        picture[at] = value
        writes.append(pltpu.make_async_copy(picture.at[at], warped.at[at], out_sem.at[n]))
        writes[-1].start()

    warp_blocks(blocks, ids, mats, table, slots, arrived, finish)
    for load in loads:
        load.wait()
    for p in range(patches):
        out[p] = window(picture, corners[p, 0], corners[p, 1])
    for write in writes:
        write.wait()


def spectrum_columns(patch, forward, constant):
    values = patch.astype(F32)
    mean = jnp.sum(values, keepdims=True) * (1.0 / (PS * PS))
    centred = values - mean
    power = jnp.sum(centred * centred, keepdims=True) * (1.0 / (PS * PS))
    halves = dot(jnp.concatenate([patch, patch], axis=1), forward[...]) - mean * constant[...]
    halves = halves.astype(BF16)
    return halves[:, :PS], halves[:, PS:], power


def own_kernel(patches, corners, picture, forward, constant, down, out, power_out):
    for p in range(patches):
        patch = window(picture, corners[p, 0], corners[p, 1])
        cosine_part, sine_part, power = spectrum_columns(patch, forward, constant)
        out[p] = dot(down[...], jnp.concatenate([cosine_part, sine_part], axis=0))
        power_out[pl.ds(p, 1), :] = jnp.broadcast_to(power, (1, PS))


def match_kernel(patches, previous, spectra, powers, forward, constant, down, back, out):
    for start in range(0, patches, 2):
        pair = range(start, min(start + 2, patches))
        parts = [spectrum_columns(previous[p], forward, constant) for p in pair]
        stacked = jnp.concatenate(
            [jnp.concatenate([part[h] for part in parts], axis=1) for h in range(2)], axis=0
        )
        second = dot(down[...], stacked)
        crosses = []
        for n, p in enumerate(pair):
            one_real, one_imag = spectra[p, :PS, :], spectra[p, PS:, :]
            two_real, two_imag = second[:PS, n * PS : (n + 1) * PS], second[PS:, n * PS : (n + 1) * PS]
            real = one_real * two_real + one_imag * two_imag
            imag = one_real * two_imag - one_imag * two_real
            crosses.append(jnp.concatenate([real.astype(BF16), imag.astype(BF16)], axis=0))
        mixed = dot(down[...], jnp.concatenate(crosses, axis=1)).astype(BF16)
        for n, p in enumerate(pair):
            real, imag = mixed[:PS, n * PS : (n + 1) * PS], mixed[PS:, n * PS : (n + 1) * PS]
            circular = dot(jnp.concatenate([real, imag], axis=1), back[...])
            product = (powers[pl.ds(p, 1), :] + EPSILON) * (parts[n][2] + EPSILON)
            out[p] = circular * (lax.rsqrt(product) * (1.0 / (PS * PS * PS)))


def params(megabytes, flops, moved):
    return dict(
        compiler_params=pltpu.CompilerParams(vmem_limit_bytes=megabytes << 20),
        cost_estimate=pl.CostEstimate(flops=flops, bytes_accessed=moved, transcendentals=0),
    )


def shards(source, pull_ids, interp_idx, interp_table, patch_pos):
    blocks = source[0]
    count = blocks.shape[0]
    grid = int(round(count**0.5))
    patches = patch_pos.shape[1]
    side = grid * BS
    near = count - CAP
    ids = pull_ids[0]
    mats = interp_idx[0].reshape(count, 2 * KP)
    positions = patch_pos[0]
    sections = lax.axis_size("sec")
    tiles = lax.axis_size("tile")
    other = lax.ppermute(blocks, "tile", [(i, (i + 1) % tiles) for i in range(tiles)])
    wanted = lax.ppermute(positions, "sec", [(i + 1, i) for i in range(sections - 1)])
    forward, constant, down, back = tables()

    begun = pl.pallas_call(
        functools.partial(near_kernel, count, grid),
        out_shape=jax.ShapeDtypeStruct((side, side), BF16),
        in_specs=[SMEM, SMEM, ANY, VMEM],
        out_specs=ANY,
        scratch_shapes=[
            pltpu.SMEM((count,), jnp.int32),
            pltpu.VMEM((near * KP, BS, BS), BF16),
            pltpu.VMEM((near, BS, BS), BF16),
            pltpu.SemaphoreType.DMA((near * KP,)),
            pltpu.SemaphoreType.DMA((near,)),
        ],
        **params(20, near * KP * 4 * BS**3, near * (KP + 1) * BS * BS * 2),
    )(ids, mats, blocks, interp_table)

    warped, sent = pl.pallas_call(
        functools.partial(far_kernel, count, grid, patches),
        out_shape=(
            jax.ShapeDtypeStruct((side, side), BF16),
            jax.ShapeDtypeStruct((patches, PS, PS), BF16),
        ),
        in_specs=[SMEM, SMEM, SMEM, ANY, ANY, VMEM, ANY],
        out_specs=(ANY, VMEM),
        scratch_shapes=[
            pltpu.SMEM((count,), jnp.int32),
            pltpu.VMEM((CAP * KP, BS, BS), BF16),
            pltpu.VMEM((side, side), BF16),
            pltpu.SemaphoreType.DMA((CAP * KP,)),
            pltpu.SemaphoreType.DMA((near,)),
            pltpu.SemaphoreType.DMA((CAP,)),
        ],
        input_output_aliases={6: 0},
        **params(24, CAP * KP * 4 * BS**3, CAP * (KP + 1) * BS * BS * 2),
    )(ids, mats, wanted, blocks, other, interp_table, begun)

    previous = lax.ppermute(sent, "sec", [(i, i + 1) for i in range(sections - 1)])

    spectra, powers = pl.pallas_call(
        functools.partial(own_kernel, patches),
        out_shape=(
            jax.ShapeDtypeStruct((patches, 2 * PS, PS), F32),
            jax.ShapeDtypeStruct((patches, PS), F32),
        ),
        in_specs=[SMEM] + [VMEM] * 4,
        out_specs=(VMEM, VMEM),
        **params(20, patches * 12 * PS**3, side * side * 2),
    )(positions, warped, forward, constant, down)

    correlations = pl.pallas_call(
        functools.partial(match_kernel, patches),
        out_shape=jax.ShapeDtypeStruct((patches, PS, PS), F32),
        in_specs=[VMEM] * 7,
        out_specs=VMEM,
        **params(20, patches * 16 * PS**3, patches * PS * PS * 14),
    )(previous, spectra, powers, forward, constant, down, back)
    return warped[None], correlations[None]


def solution(mesh):
    return jax.shard_map(
        shards,
        mesh=mesh,
        in_specs=(
            P(("parts", "sec"), "tile", None, None),
            P(("parts", "sec"), "tile", None),
            P(("parts", "sec"), "tile", None, None),
            P(),
            P(("parts", "sec"), "tile", None),
        ),
        out_specs=(P(("parts", "sec"), "tile", None), P(("parts", "sec"), "tile", None, None)),
        check_vma=False,
    )
```

time: 227 us -> 76.4 us (0.34); the launches traced: 223 us -> 76 us
  local copies, waits for them, and re-layouts: 71.1 us -> 7.81 us
  matrix products: 52.7 us -> 0 us
  Pallas kernels: 0 us -> 51.1 us
  waiting for transfers between devices: 58.5 us -> 10.2 us
  other arithmetic: 22.9 us -> 0 us
  between operations: 14.4 us -> 0.77 us
  starting transfers between devices: 3.68 us -> 6.12 us
    gather x5 -> x0, local copies, waits for them, and re-layouts: 53.8 us -> none  [the longest x2 31.7 us: extract(): band = jnp.take(picture, row_index, axis=0).reshape(count, PS, width)]
    pallas_call x0 -> x4, Pallas kernels: none -> 51.1 us  [the longest x1 17.4 us: shards(): pl.pallas_call(functools.partial(far_kernel, count, grid, patches), out_s...]
    dot_general x6 -> x0, matrix products: 49.2 us -> none  [the longest x3 20.6 us: product(): return jnp.matmul(left_matrix, right_matrix, precision=lax.Precision.HIGH)]
    ppermute x1 -> x3, waiting for transfers between devices: 51.9 us -> 10.2 us  [the longest x1 10.2 us: shards(): lax.ppermute(sent, 'sec', [(i, i + 1) for i in range(sections - 1)])]
    reduce_sum x3 -> x0, other arithmetic: 9.45 us -> none  [the longest x1 8.57 us: shards(): summed_terms.reshape(GRID * GRID, KP, BS, BS).sum(axis=1)]
    another operation x3 -> x2, local copies, waits for them, and re-layouts: 8.34 us -> 0.8 us  [shards(): mats = interp_idx[0].reshape(count, 2 * KP)]
    select_n x4 -> x0, other arithmetic: 7.19 us -> none  [the longest x2 7.18 us: extract(): band = jnp.take(picture, row_index, axis=0).reshape(count, PS, width)]
    all_gather x1 -> x0, waiting for transfers between devices: 5.95 us -> none  [shards(): section = lax.all_gather(blocks, 'tile', axis=0, tiled=True)]
  transfers between devices with their start and end apart: 2 -> 3, of which waited for: 2 -> 1; matrix products, arithmetic and copies ran while one was open for 15% -> 3% of each run, Pallas kernels for 0% -> 33%
where the time goes in v1:
time: 76.4 us; the launch traced here: 76 us
  Pallas kernels  51.1 us (67%)
  waiting for transfers between devices  10.2 us (13%)
  local copies, waits for them, and re-layouts  7.81 us (10%)
  starting transfers between devices  6.12 us (8%)
  between operations  0.77 us (1%)
    pallas_call x1, Pallas kernels, shards(): pl.pallas_call(functools.partial(far_kernel, count, grid, patches), out_s...  17.4 us
    pallas_call x1, Pallas kernels, shards(): pl.pallas_call(functools.partial(near_kernel, count, grid), out_shape=jax...  16.6 us
    ppermute x1, waiting for transfers between devices, shards(): lax.ppermute(sent, 'sec', [(i, i + 1) for i in range(sections - 1)])  10.2 us
    pallas_call x1, Pallas kernels, shards(): pl.pallas_call(functools.partial(match_kernel, patches), out_shape=jax.Sh...  8.92 us
    pallas_call x1, Pallas kernels, shards(): pl.pallas_call(functools.partial(own_kernel, patches), out_shape=(jax.Sha...  8.2 us
    unnamed x18, local copies, waits for them, and re-layouts  5.47 us
    ppermute x1, starting transfers between devices, shards(): lax.ppermute(positions, 'sec', [(i + 1, i) for i in range(sections - 1)])  3.3 us
    ppermute x1, starting transfers between devices, shards(): lax.ppermute(sent, 'sec', [(i, i + 1) for i in range(sections - 1)])  2.75 us
  transfers between devices with their start and end apart: 3, of which 1 were waited for; matrix products, arithmetic and copies ran while one was open for 3% of the time, Pallas kernels for 33%

profile of v1, /device:TPU:10, one launch (start us, length us, event | category | flops | bytes accessed | tf_op | source)
XLA Modules:
  0.0 76.0 jit_solution(1782419721733514052)
XLA Ops:
  0.6 0.1 collective-permute-start.1
  0.7 0.8 %copy.17.corners = s32[25,2]{1,0:T(8,128)S(1)} copy(s32[25,2]{0,1:T(2,128)} %bitcast.14) | data formatting | bytes 400 | tf_op jit(solution)/shard_map/squeeze | solution.py:219
  1.5 3.3 %collective-permute-start = (s32[25,2]{1,0:T(8,128)S(1)}, s32[25,2]{1,0:T(8,128)S(1)}, u32[]{:S(2)}, u32[]{:S(2)}) collective-permute-start(s32[25,2]{1,0:T(8,128)S(1)} %copy.17.corners), channel_id=1, source_target_pairs={{2,0},{4,2},{6,4},{8,6},{10,8},{12,10},{14,12},{3,1},{5,3},{7,5},{... | collective-permute-start | bytes 608 | tf_op jit(solution)/shard_map/ppermute | solution.py:223
  4.8 0.7 reshape_squeeze.3
  5.5 0.1 copy.21.mats
  5.6 0.8 %copy.23 = s32[1,25,3]{2,1,0:T(8,128)S(1)} copy(s32[1,25,3]{1,0,2:T(1,128)} %param.10) | data formatting | bytes 600 | tf_op jit(solution)/shard_map/squeeze | solution.py:217
  6.4 1.9 %copy-done.1 = bf16[1,25,256,256]{3,2,1,0:T(8,128)(2,1)S(1)} copy-done((bf16[1,25,256,256]{3,2,1,0:T(8,128)(2,1)S(1)}, bf16[1,25,256,256]{3,2,1,0:T(8,128)(2,1)}, u32[]{:S(2)}) %copy-start.1) | copy-done | bytes 3276824
  8.3 1.6 %copy-done.3 = bf16[16,256,256]{2,1,0:T(8,128)(2,1)S(1)} copy-done((bf16[16,256,256]{2,1,0:T(8,128)(2,1)S(1)}, bf16[16,256,256]{2,1,0:T(8,128)(2,1)}, u32[]{:S(2)}) %copy-start.3) | copy-done | bytes 2097176
  9.9 16.6 %shard_map.104.begun = bf16[1280,1280]{1,0:T(8,128)(2,1)} custom-call(s32[25,3]{1,0:T(8,128)S(1)} %bitcast.11, s32[25,6]{1,0:T(8,128)S(1)} %copy.21.mats, bf16[25,256,256]{2,1,0:T(8,128)(2,1)S(1)} %bitcast.9, bf16[16,256,256]{2,1,0:T(8,128)(2,1)S(1)} %copy-done.3), custom_call_target="tpu_custom_call" | custom-call | flops 2617245696 | bytes 6815744 | tf_op jit(solution)/shard_map/pallas_call | solution.py:226
  26.4 0.0 copy-start.5
  26.5 0.0 copy-start.6
  26.5 0.0 copy-start.8
  26.5 0.0 collective-permute-done.corners
  26.5 0.0 collective-permute-done.1.other
  26.5 0.0 copy-start.7
  26.5 17.4 %shard_map.105 = (bf16[1280,1280]{1,0:T(8,128)(2,1)}, bf16[25,128,128]{2,1,0:T(8,128)(2,1)S(1)}) custom-call(s32[25,3]{1,0:T(8,128)S(1)} %bitcast.12, s32[25,6]{1,0:T(8,128)S(1)} %copy.21.mats, s32[25,2]{1,0:T(8,128)S(1)} %collective-permute-done.corners, bf16[25,256,256]{2,1,0:T(8,128)(2,1)S(1)} %bitcast.10, ...), custom_call_target="tpu_custom_call", output_to_operand_aliasing={{0}: (6, {})} | custom-call | flops 2415919104 | bytes 6291456 | tf_op jit(solution)/shard_map/pallas_call | solution.py:241
  44.0 2.7 %collective-permute-start.2 = (bf16[25,128,128]{2,1,0:T(8,128)(2,1)S(1)}, bf16[25,128,128]{2,1,0:T(8,128)(2,1)S(1)}, u32[]{:S(2)}, u32[]{:S(2)}) collective-permute-start(bf16[25,128,128]{2,1,0:T(8,128)(2,1)S(1)} %get-tuple-element.7), channel_id=1, source_target_pairs={{0,2},{2,4},{4,6},{6,8},{8,10},{10,12},{12,14},{1,3},{3,5},{5,7},{... | collective-permute-start | bytes 2457608 | tf_op jit(solution)/shard_map/ppermute | solution.py:261
  46.7 0.0 copy-done.5
  46.7 0.0 copy-done.6
  46.8 0.0 copy-start
  46.8 1.9 %copy-done = bf16[1280,1280]{1,0:T(8,128)(2,1)S(1)} copy-done((bf16[1280,1280]{1,0:T(8,128)(2,1)S(1)}, bf16[1280,1280]{1,0:T(8,128)(2,1)}, u32[]{:S(2)}) %copy-start) | copy-done | bytes 3276824
  48.7 8.2 %shard_map.106 = (f32[25,256,128]{2,1,0:T(8,128)S(1)}, f32[25,128]{1,0:T(8,128)S(1)}) custom-call(s32[25,2]{1,0:T(8,128)S(1)} %copy.17.corners, bf16[1280,1280]{1,0:T(8,128)(2,1)S(1)} %copy-done, bf16[256,256]{1,0:T(8,128)(2,1)S(1)} %copy-done.6, f32[1,256]{1,0:T(1,128)S(1)} %copy-done.8, bf16[256,256]{1,0:T(8,128)(2,1)S(1)} %copy-done.5), custom_call_target="tpu_custom_call" | custom-call | flops 629145600 | bytes 3276800 | tf_op jit(solution)/shard_map/pallas_call | solution.py:263
  56.9 10.2 %collective-permute-done.2.previous = bf16[25,128,128]{2,1,0:T(8,128)(2,1)S(1)} collective-permute-done((bf16[25,128,128]{2,1,0:T(8,128)(2,1)S(1)}, bf16[25,128,128]{2,1,0:T(8,128)(2,1)S(1)}, u32[]{:S(2)}, u32[]{:S(2)}) %collective-permute-start.2) | collective-permute-done | bytes 819232 | tf_op jit(solution)/shard_map/ppermute | solution.py:261
  67.1 8.9 %shard_map.107 = f32[25,128,128]{2,1,0:T(8,128)} custom-call(bf16[25,128,128]{2,1,0:T(8,128)(2,1)S(1)} %collective-permute-done.2.previous, f32[25,256,128]{2,1,0:T(8,128)S(1)} %get-tuple-element.8.spectra, f32[25,128]{1,0:T(8,128)S(1)} %get-tuple-element.9.powers, bf16[256,256]{1,0:T(8,128)(2,1)S(1)} %copy-done.6, f32[1,256]{1,0:T(1,128)S(1)} %copy-done.8, ...), custom_call_target="tpu_custom_call" | custom-call | flops 838860800 | bytes 5734400 | tf_op jit(solution)/shard_map/pallas_call | solution.py:274
  (8 shorter events, 0.0 us)
Async XLA Ops:
  0.6 25.9 %collective-permute-start.1 = (bf16[25,256,256]{2,1,0:T(8,128)(2,1)}, bf16[25,256,256]{2,1,0:T(8,128)(2,1)S(1)}, u32[]{:S(2)}, u32[]{:S(2)}) collective-permute-start(bf16[25,256,256]{2,1,0:T(8,128)(2,1)} %bitcast.8), channel_id=1, source_target_pairs={{0,1},{1,0},{2,3},{3,2},{4,5},{5,4},{6,7},{7,6},{8,9},{9,8},{10,11... | collective-permute-start | bytes 9830408 | tf_op jit(solution)/shard_map/ppermute | solution.py:222
  1.5 25.0 %collective-permute-start = (s32[25,2]{1,0:T(8,128)S(1)}, s32[25,2]{1,0:T(8,128)S(1)}, u32[]{:S(2)}, u32[]{:S(2)}) collective-permute-start(s32[25,2]{1,0:T(8,128)S(1)} %copy.17.corners), channel_id=1, source_target_pairs={{2,0},{4,2},{6,4},{8,6},{10,8},{12,10},{14,12},{3,1},{5,3},{7,5},{... | collective-permute-start | bytes 608 | tf_op jit(solution)/shard_map/ppermute | solution.py:223
  6.4 1.9 %copy-start.1 = (bf16[1,25,256,256]{3,2,1,0:T(8,128)(2,1)S(1)}, bf16[1,25,256,256]{3,2,1,0:T(8,128)(2,1)}, u32[]{:S(2)}) copy-start(bf16[1,25,256,256]{3,2,1,0:T(8,128)(2,1)} %param.9) | copy-start | bytes 9830404
  8.3 1.6 %copy-start.3 = (bf16[16,256,256]{2,1,0:T(8,128)(2,1)S(1)}, bf16[16,256,256]{2,1,0:T(8,128)(2,1)}, u32[]{:S(2)}) copy-start(bf16[16,256,256]{2,1,0:T(8,128)(2,1)} %table.3) | copy-start | bytes 6291460
  9.9 16.6 %copy-start.2 = (bf16[1,25,256,256]{3,2,1,0:T(8,128)(2,1)S(1)}, bf16[1,25,256,256]{3,2,1,0:T(8,128)(2,1)}, u32[]{:S(2)}) copy-start(bf16[1,25,256,256]{3,2,1,0:T(8,128)(2,1)} %param.9) | copy-start | bytes 9830404
  9.9 16.6 %copy-start.4 = (bf16[16,256,256]{2,1,0:T(8,128)(2,1)S(1)}, bf16[16,256,256]{2,1,0:T(8,128)(2,1)}, u32[]{:S(2)}) copy-start(bf16[16,256,256]{2,1,0:T(8,128)(2,1)} %table.3) | copy-start | bytes 6291460
  26.4 20.3 %copy-start.5 = (bf16[256,256]{1,0:T(8,128)(2,1)S(1)}, bf16[256,256]{1,0:T(8,128)(2,1)}, u32[]{:S(2)}) copy-start(bf16[256,256]{1,0:T(8,128)(2,1)} %constant.12.clone.down) | copy-start | bytes 393220
  26.5 20.3 %copy-start.6 = (bf16[256,256]{1,0:T(8,128)(2,1)S(1)}, bf16[256,256]{1,0:T(8,128)(2,1)}, u32[]{:S(2)}) copy-start(bf16[256,256]{1,0:T(8,128)(2,1)} %constant.10.clone.forward) | copy-start | bytes 393220
  26.5 20.3 %copy-start.8 = (f32[1,256]{1,0:T(1,128)S(1)}, f32[1,256]{1,0:T(1,128)}, u32[]{:S(2)}) copy-start(f32[1,256]{1,0:T(1,128)} %constant.11.clone) | copy-start | bytes 3076
  26.5 40.6 %copy-start.7 = (bf16[256,128]{1,0:T(8,128)(2,1)S(1)}, bf16[256,128]{1,0:T(8,128)(2,1)}, u32[]{:S(2)}) copy-start(bf16[256,128]{1,0:T(8,128)(2,1)} %constant.13.clone.back) | copy-start | bytes 196612
  44.0 23.1 %collective-permute-start.2 = (bf16[25,128,128]{2,1,0:T(8,128)(2,1)S(1)}, bf16[25,128,128]{2,1,0:T(8,128)(2,1)S(1)}, u32[]{:S(2)}, u32[]{:S(2)}) collective-permute-start(bf16[25,128,128]{2,1,0:T(8,128)(2,1)S(1)} %get-tuple-element.7), channel_id=1, source_target_pairs={{0,2},{2,4},{4,6},{6,8},{8,10},{10,12},{12,14},{1,3},{3,5},{5,7},{... | collective-permute-start | bytes 2457608 | tf_op jit(solution)/shard_map/ppermute | solution.py:261
  46.8 1.9 %copy-start = (bf16[1280,1280]{1,0:T(8,128)(2,1)S(1)}, bf16[1280,1280]{1,0:T(8,128)(2,1)}, u32[]{:S(2)}) copy-start(bf16[1280,1280]{1,0:T(8,128)(2,1)} %get-tuple-element.6.picture) | copy-start | bytes 9830404

commit v2 on v1

v2 whole, which is shorter than its diff:
```python
import functools

import jax
import jax.numpy as jnp
import ml_dtypes
import numpy as np
from jax import lax
from jax.experimental import pallas as pl
from jax.experimental.pallas import tpu as pltpu
from jax.sharding import PartitionSpec as P

BS = 256
PS = 128
KP = 3
EPSILON = 1e-06
CAP = 12
ROWS = PS + 16
COLS = 2 * PS

SMEM = pl.BlockSpec(memory_space=pltpu.SMEM)
VMEM = pl.BlockSpec(memory_space=pltpu.VMEM)
ANY = pl.BlockSpec(memory_space=pl.ANY)
F32 = jnp.float32
BF16 = jnp.bfloat16


def tables():
    grid = np.arange(PS)
    angle = 2.0 * np.pi / PS * (grid[:, None] * grid[None, :] % PS)
    cosine, sine = np.cos(angle), np.sin(angle)
    across = np.concatenate([cosine, sine], axis=1)
    high = across.astype(ml_dtypes.bfloat16)
    low = (across - high.astype(np.float64)).astype(ml_dtypes.bfloat16)
    forward = np.concatenate([high, low], axis=0)
    constant = forward.astype(np.float64).sum(axis=0, keepdims=True).astype(np.float32)
    down = np.block([[cosine, -sine], [sine, cosine]]).astype(ml_dtypes.bfloat16)
    back = np.concatenate([cosine, -sine], axis=0).astype(ml_dtypes.bfloat16)
    return forward, constant, down, back


def dot(a, b):
    return jnp.dot(a, b, preferred_element_type=F32)


def block_order(ids, order, low, count):
    first, last = jnp.int32(0), jnp.int32(count - 1)
    for b in range(count):
        near = None
        for k in range(KP):
            local = ids[k, b] - low
            here = (local >= 0) & (local < count)
            near = here if near is None else near & here
        order[jnp.where(near, first, last)] = b
        step = near.astype(jnp.int32)
        first = first + step
        last = last + step - 1


def place(block, grid):
    row = pl.multiple_of(block // grid * BS, BS)
    col = pl.multiple_of(block % grid * BS, BS)
    return pl.ds(row, BS), pl.ds(col, BS)


def warp_block(block, mats, table, pulled):
    total = None
    for k in range(KP):
        left = dot(table[mats[k, 0, block]], pulled(k)).astype(BF16)
        term = lax.dot_general(
            left, table[mats[k, 1, block]], (((1,), (1,)), ((), ())), preferred_element_type=F32
        )
        total = term if total is None else total + term
    return total.astype(BF16)


def near_kernel(count, ids, mats, source, table, begun, order):
    low = lax.axis_index("tile") * count
    block_order(ids, order, low, count)
    for n in range(count - CAP):
        block = order[n]
        begun[n] = warp_block(block, mats, table, lambda k: source[ids[k, block] - low])


def window(picture, y, x):
    top = pl.multiple_of(jnp.minimum(y // 16 * 16, picture.shape[0] - ROWS), 16)
    left = pl.multiple_of(jnp.minimum(x // PS * PS, picture.shape[1] - COLS), PS)
    area = picture[pl.ds(top, ROWS), pl.ds(left, COLS)]
    i = lax.broadcasted_iota(jnp.int32, (PS, ROWS), 0)
    r = lax.broadcasted_iota(jnp.int32, (PS, ROWS), 1)
    pick_rows = (r - i == y - top).astype(F32).astype(BF16)
    c = lax.broadcasted_iota(jnp.int32, (COLS, PS), 0)
    j = lax.broadcasted_iota(jnp.int32, (COLS, PS), 1)
    pick_cols = (c - j == x - left).astype(F32).astype(BF16)
    return dot(dot(pick_rows, area).astype(BF16), pick_cols).astype(BF16)


def far_kernel(
    count, grid, patches, ids, mats, corners, source, other, table, begun, picture, out, order
):
    tile = lax.axis_index("tile")
    low = tile * count
    there = (1 - tile) * count
    near = count - CAP
    block_order(ids, order, low, count)
    for n in range(near):
        picture[place(order[n], grid)] = begun[n]
    for n in range(near, count):
        block = order[n]

        def pulled(k):
            index = ids[k, block]
            local = index - low
            here = (local >= 0) & (local < count)
            own = source[jnp.where(here, local, 0)]
            return jnp.where(here, own, other[jnp.where(here, 0, index - there)])

        picture[place(block, grid)] = warp_block(block, mats, table, pulled)
    for p in range(patches):
        out[p] = window(picture, corners[0, p], corners[1, p])


def spectrum_columns(patch, forward, constant):
    values = patch.astype(F32)
    mean = jnp.sum(values, keepdims=True) * (1.0 / (PS * PS))
    centred = values - mean
    power = jnp.sum(centred * centred, keepdims=True) * (1.0 / (PS * PS))
    halves = dot(jnp.concatenate([patch, patch], axis=1), forward[...]) - mean * constant[...]
    halves = halves.astype(BF16)
    return halves[:, :PS], halves[:, PS:], power


def own_kernel(patches, corners, picture, forward, constant, down, out, power_out):
    for p in range(patches):
        patch = window(picture, corners[0, p], corners[1, p])
        cosine_part, sine_part, power = spectrum_columns(patch, forward, constant)
        out[p] = dot(down[...], jnp.concatenate([cosine_part, sine_part], axis=0))
        power_out[pl.ds(p, 1), :] = jnp.broadcast_to(power, (1, PS))


def match_kernel(patches, previous, spectra, powers, forward, constant, down, back, out, halves, crosses, mixed, scales):
    for p in range(patches):
        cosine_part, sine_part, power = spectrum_columns(previous[p], forward, constant)
        at = pl.ds(p % 2 * PS, PS)
        halves[p // 2, :PS, at] = cosine_part
        halves[p // 2, PS:, at] = sine_part
        product = (powers[pl.ds(p, 1), :] + EPSILON) * (power + EPSILON)
        scales[pl.ds(p, 1), :] = lax.rsqrt(product) * (1.0 / (PS * PS * PS))
    pairs = [range(start, min(start + 2, patches)) for start in range(0, patches, 2)]
    for q, pair in enumerate(pairs):
        width = PS * len(pair)
        second = dot(down[...], halves[q, :, :width])
        for n, p in enumerate(pair):
            one_real, one_imag = spectra[p, :PS, :], spectra[p, PS:, :]
            two_real, two_imag = second[:PS, n * PS : (n + 1) * PS], second[PS:, n * PS : (n + 1) * PS]
            real = one_real * two_real + one_imag * two_imag
            imag = one_real * two_imag - one_imag * two_real
            crosses[q, :PS, pl.ds(n * PS, PS)] = real.astype(BF16)
            crosses[q, PS:, pl.ds(n * PS, PS)] = imag.astype(BF16)
    for q, pair in enumerate(pairs):
        width = PS * len(pair)
        both = dot(down[...], crosses[q, :, :width]).astype(BF16)
        for n, p in enumerate(pair):
            mixed[p, :, :PS] = both[:PS, n * PS : (n + 1) * PS]
            mixed[p, :, PS:] = both[PS:, n * PS : (n + 1) * PS]
    for p in range(patches):
        out[p] = dot(mixed[p], back[...]) * scales[pl.ds(p, 1), :]


def params(megabytes, flops, moved):
    return dict(
        compiler_params=pltpu.CompilerParams(vmem_limit_bytes=megabytes << 20),
        cost_estimate=pl.CostEstimate(flops=flops, bytes_accessed=moved, transcendentals=0),
    )


def shards(source, pull_ids, interp_idx, interp_table, patch_pos):
    blocks = source[0]
    count = blocks.shape[0]
    grid = int(round(count**0.5))
    patches = patch_pos.shape[1]
    side = grid * BS
    near = count - CAP
    ids = pull_ids[0].T
    mats = interp_idx[0].transpose(1, 2, 0)
    positions = patch_pos[0].T
    sections = lax.axis_size("sec")
    tiles = lax.axis_size("tile")
    other = lax.ppermute(blocks, "tile", [(i, (i + 1) % tiles) for i in range(tiles)])
    wanted = lax.ppermute(positions, "sec", [(i + 1, i) for i in range(sections - 1)])
    forward, constant, down, back = tables()

    begun = pl.pallas_call(
        functools.partial(near_kernel, count),
        out_shape=jax.ShapeDtypeStruct((near, BS, BS), BF16),
        in_specs=[SMEM, SMEM, VMEM, VMEM],
        out_specs=VMEM,
        scratch_shapes=[pltpu.SMEM((count,), jnp.int32)],
        **params(16, near * KP * 4 * BS**3, near * (KP + 1) * BS * BS * 2),
    )(ids, mats, blocks, interp_table)

    warped, sent = pl.pallas_call(
        functools.partial(far_kernel, count, grid, patches),
        out_shape=(
            jax.ShapeDtypeStruct((side, side), BF16),
            jax.ShapeDtypeStruct((patches, PS, PS), BF16),
        ),
        in_specs=[SMEM] * 3 + [VMEM] * 4,
        out_specs=(VMEM, VMEM),
        scratch_shapes=[pltpu.SMEM((count,), jnp.int32)],
        **params(16, CAP * KP * 4 * BS**3, CAP * (KP + 1) * BS * BS * 2),
    )(ids, mats, wanted, blocks, other, interp_table, begun)

    previous = lax.ppermute(sent, "sec", [(i, i + 1) for i in range(sections - 1)])

    spectra, powers = pl.pallas_call(
        functools.partial(own_kernel, patches),
        out_shape=(
            jax.ShapeDtypeStruct((patches, 2 * PS, PS), F32),
            jax.ShapeDtypeStruct((patches, PS), F32),
        ),
        in_specs=[SMEM] + [VMEM] * 4,
        out_specs=(VMEM, VMEM),
        **params(20, patches * 12 * PS**3, side * side * 2),
    )(positions, warped, forward, constant, down)

    correlations = pl.pallas_call(
        functools.partial(match_kernel, patches),
        out_shape=jax.ShapeDtypeStruct((patches, PS, PS), F32),
        in_specs=[VMEM] * 7,
        out_specs=VMEM,
        scratch_shapes=[
            pltpu.VMEM(((patches + 1) // 2, 2 * PS, 2 * PS), BF16),
            pltpu.VMEM(((patches + 1) // 2, 2 * PS, 2 * PS), BF16),
            pltpu.VMEM((patches, PS, 2 * PS), BF16),
            pltpu.VMEM((patches, PS), F32),
        ],
        **params(20, patches * 16 * PS**3, patches * PS * PS * 14),
    )(previous, spectra, powers, forward, constant, down, back)
    return warped[None], correlations[None]


def solution(mesh):
    return jax.shard_map(
        shards,
        mesh=mesh,
        in_specs=(
            P(("parts", "sec"), "tile", None, None),
            P(("parts", "sec"), "tile", None),
            P(("parts", "sec"), "tile", None, None),
            P(),
            P(("parts", "sec"), "tile", None),
        ),
        out_specs=(P(("parts", "sec"), "tile", None), P(("parts", "sec"), "tile", None, None)),
        check_vma=False,
    )
```

time: 76.4 us -> 49.2 us (0.64)
  Pallas kernels: 51.1 us -> 24.7 us
  local copies, waits for them, and re-layouts: 7.81 us -> 6.84 us
    pallas_call x1, Pallas kernels: 16.6 us -> 3.93 us  [shards(): pl.pallas_call(functools.partial(near_kernel, count), out_shape=jax.Shape...]
    pallas_call x1, Pallas kernels: 17.4 us -> 6.7 us  [shards(): pl.pallas_call(functools.partial(far_kernel, count, grid, patches), out_s...]
    pallas_call x1, Pallas kernels: 8.92 us -> 6.14 us  [shards(): pl.pallas_call(functools.partial(match_kernel, patches), out_shape=jax.Sh...]
    squeeze x2 -> x0, local copies, waits for them, and re-layouts: 1.54 us -> none  [the longest x1 0.77 us: shards(): positions = patch_pos[0]]
    unnamed x18 -> x19, local copies, waits for them, and re-layouts: 5.47 us -> 6.84 us
    another operation x2 -> x0, local copies, waits for them, and re-layouts: 0.8 us -> none  [shards(): mats = interp_idx[0].reshape(count, 2 * KP)]
  transfers between devices with their start and end apart: 3 -> 3, of which waited for: 1 -> 1; matrix products, arithmetic and copies ran while one was open for 3% -> 1% of each run, Pallas kernels for 33% -> 24%
where the time goes in v2:
time: 49.2 us; the launch traced here: 48.9 us
  Pallas kernels  24.7 us (50%)
  waiting for transfers between devices  10.5 us (21%)
  local copies, waits for them, and re-layouts  6.84 us (14%)
  starting transfers between devices  6.1 us (12%)
  between operations  0.76 us (2%)
    ppermute x1, waiting for transfers between devices, shards(): lax.ppermute(sent, 'sec', [(i, i + 1) for i in range(sections - 1)])  10.5 us
    pallas_call x1, Pallas kernels, shards(): pl.pallas_call(functools.partial(own_kernel, patches), out_shape=(jax.Sha...  7.95 us
    unnamed x19, local copies, waits for them, and re-layouts  6.84 us
    pallas_call x1, Pallas kernels, shards(): pl.pallas_call(functools.partial(far_kernel, count, grid, patches), out_s...  6.7 us
    pallas_call x1, Pallas kernels, shards(): pl.pallas_call(functools.partial(match_kernel, patches), out_shape=jax.Sh...  6.14 us
    pallas_call x1, Pallas kernels, shards(): pl.pallas_call(functools.partial(near_kernel, count), out_shape=jax.Shape...  3.93 us
    ppermute x1, starting transfers between devices, shards(): lax.ppermute(positions, 'sec', [(i + 1, i) for i in range(sections - 1)])  3.32 us
    ppermute x1, starting transfers between devices, shards(): lax.ppermute(sent, 'sec', [(i, i + 1) for i in range(sections - 1)])  2.71 us
  transfers between devices with their start and end apart: 3, of which 1 were waited for; matrix products, arithmetic and copies ran while one was open for 1% of the time, Pallas kernels for 24%

profile of v2, /device:TPU:10, one launch (start us, length us, event | category | flops | bytes accessed | tf_op | source)
XLA Modules:
  0.0 48.9 jit_solution(15788856954516775870)
XLA Ops:
  0.6 0.1 collective-permute-start.1
  0.7 3.3 %collective-permute-start = (s32[2,25]{1,0:T(2,128)}, s32[2,25]{1,0:T(2,128)S(1)}, u32[]{:S(2)}, u32[]{:S(2)}) collective-permute-start(s32[2,25]{1,0:T(2,128)} %bitcast.22), channel_id=1, source_target_pairs={{2,0},{4,2},{6,4},{8,6},{10,8},{12,10},{14,12},{3,1},{5,3},{7,5},{... | collective-permute-start | bytes 608 | tf_op jit(solution)/shard_map/ppermute | solution.py:189
  4.0 0.7 %copy.13 = s32[1,25,3]{1,2,0:T(4,128)S(1)} copy(s32[1,25,3]{1,0,2:T(1,128)} %param.10) | data formatting | bytes 600
  4.7 1.9 %copy-done.1 = bf16[1,25,256,256]{3,2,1,0:T(8,128)(2,1)S(1)} copy-done((bf16[1,25,256,256]{3,2,1,0:T(8,128)(2,1)S(1)}, bf16[1,25,256,256]{3,2,1,0:T(8,128)(2,1)}, u32[]{:S(2)}) %copy-start.1) | copy-done | bytes 3276824
  6.6 1.6 %copy-done.2 = bf16[16,256,256]{2,1,0:T(8,128)(2,1)S(1)} copy-done((bf16[16,256,256]{2,1,0:T(8,128)(2,1)S(1)}, bf16[16,256,256]{2,1,0:T(8,128)(2,1)}, u32[]{:S(2)}) %copy-start.2) | copy-done | bytes 2097176
  8.2 0.7 %copy-done.7 = s32[1,25,3,2]{1,3,2,0:T(2,128)S(1)} copy-done((s32[1,25,3,2]{1,3,2,0:T(2,128)S(1)}, s32[1,25,3,2]{1,3,2,0:T(2,128)}, u32[]{:S(2)}) %copy-start.7) | copy-done | bytes 624
  8.9 3.9 %shard_map.104.begun = bf16[13,256,256]{2,1,0:T(8,128)(2,1)S(1)} custom-call(s32[3,25]{1,0:T(4,128)S(1)} %bitcast.18, s32[3,2,25]{2,1,0:T(2,128)S(1)} %bitcast.20, bf16[25,256,256]{2,1,0:T(8,128)(2,1)S(1)} %bitcast.16, bf16[16,256,256]{2,1,0:T(8,128)(2,1)S(1)} %copy-done.2), custom_call_target="tpu_custom_call" | custom-call | flops 2617245696 | bytes 6815744 | tf_op jit(solution)/shard_map/pallas_call | solution.py:192
  12.9 0.0 copy-start.3
  12.9 0.0 copy-start.4
  12.9 0.0 copy-start.6
  12.9 0.0 copy-start.8
  12.9 0.0 collective-permute-done.corners
  12.9 0.0 collective-permute-done.1.other
  12.9 0.0 copy-start.5
  12.9 6.7 %shard_map.105 = (bf16[1280,1280]{1,0:T(8,128)(2,1)}, bf16[25,128,128]{2,1,0:T(8,128)(2,1)S(1)}) custom-call(s32[3,25]{1,0:T(4,128)S(1)} %bitcast.19, s32[3,2,25]{2,1,0:T(2,128)S(1)} %bitcast.21, s32[2,25]{1,0:T(2,128)S(1)} %collective-permute-done.corners, bf16[25,256,256]{2,1,0:T(8,128)(2,1)S(1)} %bitcast.17, ...), custom_call_target="tpu_custom_call" | custom-call | flops 2415919104 | bytes 6291456 | tf_op jit(solution)/shard_map/pallas_call | solution.py:201
  19.6 2.7 %collective-permute-start.2 = (bf16[25,128,128]{2,1,0:T(8,128)(2,1)S(1)}, bf16[25,128,128]{2,1,0:T(8,128)(2,1)S(1)}, u32[]{:S(2)}, u32[]{:S(2)}) collective-permute-start(bf16[25,128,128]{2,1,0:T(8,128)(2,1)S(1)} %get-tuple-element.7), channel_id=1, source_target_pairs={{0,2},{2,4},{4,6},{6,8},{8,10},{10,12},{12,14},{1,3},{3,5},{5,7},{... | collective-permute-start | bytes 2457608 | tf_op jit(solution)/shard_map/ppermute | solution.py:213
  22.4 0.0 copy-done.3
  22.4 0.0 copy-done.4
  22.4 0.0 copy-done.6
  22.4 0.0 copy-start
  22.4 1.9 %copy-done = bf16[1280,1280]{1,0:T(8,128)(2,1)S(1)} copy-done((bf16[1280,1280]{1,0:T(8,128)(2,1)S(1)}, bf16[1280,1280]{1,0:T(8,128)(2,1)}, u32[]{:S(2)}) %copy-start) | copy-done | bytes 3276824
  24.3 8.0 %shard_map.106 = (f32[25,256,128]{2,1,0:T(8,128)S(1)}, f32[25,128]{1,0:T(8,128)S(1)}) custom-call(s32[2,25]{1,0:T(2,128)S(1)} %bitcast.23, bf16[1280,1280]{1,0:T(8,128)(2,1)S(1)} %copy-done, bf16[256,256]{1,0:T(8,128)(2,1)S(1)} %copy-done.4, f32[1,256]{1,0:T(1,128)S(1)} %copy-done.6, bf16[256,256]{1,0:T(8,128)(2,1)S(1)} %copy-done.3), custom_call_target="tpu_custom_call" | custom-call | flops 629145600 | bytes 3276800 | tf_op jit(solution)/shard_map/pallas_call | solution.py:215
  32.3 10.5 %collective-permute-done.2.previous = bf16[25,128,128]{2,1,0:T(8,128)(2,1)S(1)} collective-permute-done((bf16[25,128,128]{2,1,0:T(8,128)(2,1)S(1)}, bf16[25,128,128]{2,1,0:T(8,128)(2,1)S(1)}, u32[]{:S(2)}, u32[]{:S(2)}) %collective-permute-start.2) | collective-permute-done | bytes 819232 | tf_op jit(solution)/shard_map/ppermute | solution.py:213
  42.8 6.1 %shard_map.107 = f32[25,128,128]{2,1,0:T(8,128)} custom-call(bf16[25,128,128]{2,1,0:T(8,128)(2,1)S(1)} %collective-permute-done.2.previous, f32[25,256,128]{2,1,0:T(8,128)S(1)} %get-tuple-element.8.spectra, f32[25,128]{1,0:T(8,128)S(1)} %get-tuple-element.9.powers, bf16[256,256]{1,0:T(8,128)(2,1)S(1)} %copy-done.4, f32[1,256]{1,0:T(1,128)S(1)} %copy-done.6, ...), custom_call_target="tpu_custom_call" | custom-call | flops 838860800 | bytes 5734400 | tf_op jit(solution)/shard_map/pallas_call | solution.py:226
  (5 shorter events, 0.0 us)
Async XLA Ops:
  0.6 12.3 %collective-permute-start.1 = (bf16[25,256,256]{2,1,0:T(8,128)(2,1)}, bf16[25,256,256]{2,1,0:T(8,128)(2,1)S(1)}, u32[]{:S(2)}, u32[]{:S(2)}) collective-permute-start(bf16[25,256,256]{2,1,0:T(8,128)(2,1)} %bitcast.15), channel_id=1, source_target_pairs={{0,1},{1,0},{2,3},{3,2},{4,5},{5,4},{6,7},{7,6},{8,9},{9,8},{10,11... | collective-permute-start | bytes 9830408 | tf_op jit(solution)/shard_map/ppermute | solution.py:188
  0.7 12.2 %collective-permute-start = (s32[2,25]{1,0:T(2,128)}, s32[2,25]{1,0:T(2,128)S(1)}, u32[]{:S(2)}, u32[]{:S(2)}) collective-permute-start(s32[2,25]{1,0:T(2,128)} %bitcast.22), channel_id=1, source_target_pairs={{2,0},{4,2},{6,4},{8,6},{10,8},{12,10},{14,12},{3,1},{5,3},{7,5},{... | collective-permute-start | bytes 608 | tf_op jit(solution)/shard_map/ppermute | solution.py:189
  4.7 1.9 %copy-start.1 = (bf16[1,25,256,256]{3,2,1,0:T(8,128)(2,1)S(1)}, bf16[1,25,256,256]{3,2,1,0:T(8,128)(2,1)}, u32[]{:S(2)}) copy-start(bf16[1,25,256,256]{3,2,1,0:T(8,128)(2,1)} %param.9) | copy-start | bytes 9830404
  6.6 1.6 %copy-start.2 = (bf16[16,256,256]{2,1,0:T(8,128)(2,1)S(1)}, bf16[16,256,256]{2,1,0:T(8,128)(2,1)}, u32[]{:S(2)}) copy-start(bf16[16,256,256]{2,1,0:T(8,128)(2,1)} %table.3) | copy-start | bytes 6291460
  8.2 0.7 %copy-start.7 = (s32[1,25,3,2]{1,3,2,0:T(2,128)S(1)}, s32[1,25,3,2]{1,3,2,0:T(2,128)}, u32[]{:S(2)}) copy-start(s32[1,25,3,2]{1,3,2,0:T(2,128)} %param.11) | copy-start | bytes 1804
  12.9 9.5 %copy-start.3 = (bf16[256,256]{1,0:T(8,128)(2,1)S(1)}, bf16[256,256]{1,0:T(8,128)(2,1)}, u32[]{:S(2)}) copy-start(bf16[256,256]{1,0:T(8,128)(2,1)} %constant.12.clone.down) | copy-start | bytes 393220
  12.9 9.5 %copy-start.4 = (bf16[256,256]{1,0:T(8,128)(2,1)S(1)}, bf16[256,256]{1,0:T(8,128)(2,1)}, u32[]{:S(2)}) copy-start(bf16[256,256]{1,0:T(8,128)(2,1)} %constant.10.clone.forward) | copy-start | bytes 393220
  12.9 9.5 %copy-start.6 = (f32[1,256]{1,0:T(1,128)S(1)}, f32[1,256]{1,0:T(1,128)}, u32[]{:S(2)}) copy-start(f32[1,256]{1,0:T(1,128)} %constant.11.clone) | copy-start | bytes 3076
  12.9 9.5 %copy-start.8 = (s32[1,25,2]{1,2,0:T(2,128)S(1)}, s32[1,25,2]{1,2,0:T(2,128)}, u32[]{:S(2)}) copy-start(s32[1,25,2]{1,2,0:T(2,128)} %param.13) | copy-start | bytes 604
  12.9 29.9 %copy-start.5 = (bf16[256,128]{1,0:T(8,128)(2,1)S(1)}, bf16[256,128]{1,0:T(8,128)(2,1)}, u32[]{:S(2)}) copy-start(bf16[256,128]{1,0:T(8,128)(2,1)} %constant.13.clone.back) | copy-start | bytes 196612
  19.6 23.2 %collective-permute-start.2 = (bf16[25,128,128]{2,1,0:T(8,128)(2,1)S(1)}, bf16[25,128,128]{2,1,0:T(8,128)(2,1)S(1)}, u32[]{:S(2)}, u32[]{:S(2)}) collective-permute-start(bf16[25,128,128]{2,1,0:T(8,128)(2,1)S(1)} %get-tuple-element.7), channel_id=1, source_target_pairs={{0,2},{2,4},{4,6},{6,8},{8,10},{10,12},{12,14},{1,3},{3,5},{5,7},{... | collective-permute-start | bytes 2457608 | tf_op jit(solution)/shard_map/ppermute | solution.py:213
  22.4 1.9 %copy-start = (bf16[1280,1280]{1,0:T(8,128)(2,1)S(1)}, bf16[1280,1280]{1,0:T(8,128)(2,1)}, u32[]{:S(2)}) copy-start(bf16[1280,1280]{1,0:T(8,128)(2,1)} %get-tuple-element.6.picture) | copy-start | bytes 9830404

commit v3 on v2

v3 whole, which is shorter than its diff:
```python
import functools

import jax
import jax.numpy as jnp
import ml_dtypes
import numpy as np
from jax import lax
from jax.experimental import pallas as pl
from jax.experimental.pallas import tpu as pltpu
from jax.sharding import PartitionSpec as P

BS = 256
PS = 128
KP = 3
EPSILON = 1e-06
CAP = 12
ROWS = PS + 16
COLS = 2 * PS
PARTS = (0.64,)

SMEM = pl.BlockSpec(memory_space=pltpu.SMEM)
VMEM = pl.BlockSpec(memory_space=pltpu.VMEM)
ANY = pl.BlockSpec(memory_space=pl.ANY)
F32 = jnp.float32
BF16 = jnp.bfloat16


def tables():
    grid = np.arange(PS)
    angle = 2.0 * np.pi / PS * (grid[:, None] * grid[None, :] % PS)
    cosine, sine = np.cos(angle), np.sin(angle)
    across = np.concatenate([cosine, sine], axis=1)
    high = across.astype(ml_dtypes.bfloat16)
    low = (across - high.astype(np.float64)).astype(ml_dtypes.bfloat16)
    forward = np.concatenate([high, low], axis=0)
    constant = forward.astype(np.float64).sum(axis=0, keepdims=True).astype(np.float32)
    down = np.block([[cosine, -sine], [sine, cosine]]).astype(ml_dtypes.bfloat16)
    back = np.concatenate([cosine, -sine], axis=0).astype(ml_dtypes.bfloat16)
    return forward, constant, down, back


def dot(a, b):
    return jnp.dot(a, b, preferred_element_type=F32)


FIELDS = 1 + 3 * KP


def plan_kernel(count, tiles, ids_from, mats_from, plan, ids, mats, sems):
    copies = [
        pltpu.make_async_copy(ids_from, ids, sems.at[0]),
        pltpu.make_async_copy(mats_from, mats, sems.at[1]),
    ]
    for copy in copies:
        copy.start()
    for copy in copies:
        copy.wait()
    low = lax.axis_index("tile") * count
    first, last = jnp.int32(0), jnp.int32(count - 1)
    for b in range(count):
        near, pulls = None, []
        for k in range(KP):
            local = ids[k, 0, b] - low
            here = (local >= 0) & (local < count)
            near = here if near is None else near & here
            pulls.append(jnp.where(local < 0, local + tiles * count, local))
        step = near.astype(jnp.int32)
        at = (last + step * (first - last)) * FIELDS
        first = first + step
        last = last + step - 1
        plan[at] = b
        for k in range(KP):
            plan[at + 1 + 3 * k] = pulls[k]
            plan[at + 2 + 3 * k] = mats[k, 0, b]
            plan[at + 3 + 3 * k] = mats[k, 1, b]


def place(block, grid):
    row = pl.multiple_of(block // grid * BS, BS)
    col = pl.multiple_of(block % grid * BS, BS)
    return pl.ds(row, BS), pl.ds(col, BS)


def warp_block(n, plan, table, pulled):
    total = None
    for k in range(KP):
        at = n * FIELDS + 3 * k
        left = dot(table[plan[at + 2]], pulled(plan[at + 1])).astype(BF16)
        term = lax.dot_general(
            left, table[plan[at + 3]], (((1,), (1,)), ((), ())), preferred_element_type=F32
        )
        total = term if total is None else total + term
    return total.astype(BF16)


def near_kernel(count, plan, source, table, begun):
    for n in range(count - CAP):
        begun[n] = warp_block(n, plan, table, lambda index: source[index])


def window(picture, y, x):
    top = pl.multiple_of(jnp.minimum(y // 16 * 16, picture.shape[0] - ROWS), 16)
    left = pl.multiple_of(jnp.minimum(x // PS * PS, picture.shape[1] - COLS), PS)
    area = picture[pl.ds(top, ROWS), pl.ds(left, COLS)]
    i = lax.broadcasted_iota(jnp.int32, (PS, ROWS), 0)
    r = lax.broadcasted_iota(jnp.int32, (PS, ROWS), 1)
    pick_rows = (r - i == y - top).astype(F32).astype(BF16)
    c = lax.broadcasted_iota(jnp.int32, (COLS, PS), 0)
    j = lax.broadcasted_iota(jnp.int32, (COLS, PS), 1)
    pick_cols = (c - j == x - left).astype(F32).astype(BF16)
    return dot(dot(pick_rows, area).astype(BF16), pick_cols).astype(BF16)


def cut_windows(share, corners, picture, out):
    for n, p in enumerate(share):
        out[n] = window(picture, corners[0, p], corners[1, p])


def far_kernel(count, grid, share, plan, corners, source, other, table, begun, picture, out):
    near = count - CAP

    def pulled(index):
        here = index < count
        own = source[jnp.where(here, index, 0)]
        return jnp.where(here, own, other[jnp.where(here, 0, index - count)])

    for n in range(near):
        picture[place(plan[n * FIELDS], grid)] = begun[n]
    for n in range(near, count):
        picture[place(plan[n * FIELDS], grid)] = warp_block(n, plan, table, pulled)
    cut_windows(share, corners, picture, out)


def spectrum_columns(patch, forward, constant):
    values = patch.astype(F32)
    mean = jnp.sum(values, keepdims=True) * (1.0 / (PS * PS))
    centred = values - mean
    power = jnp.sum(centred * centred, keepdims=True) * (1.0 / (PS * PS))
    halves = dot(jnp.concatenate([patch, patch], axis=1), forward[...]) - mean * constant[...]
    halves = halves.astype(BF16)
    return halves[:, :PS], halves[:, PS:], power


def own_kernel(patches, corners, picture, forward, constant, down, out, power_out, warped, bands, halves, sem):
    write = pltpu.make_async_copy(picture, warped, sem)
    write.start()
    cut_windows(range(patches), corners, picture, bands)
    for p in range(patches):
        cosine_part, sine_part, power = spectrum_columns(bands[p], forward, constant)
        halves[p, :PS] = cosine_part
        halves[p, PS:] = sine_part
        power_out[pl.ds(p, 1), :] = jnp.broadcast_to(power, (1, PS))
    for p in range(patches):
        out[p] = dot(down[...], halves[p])
    write.wait()


def match_kernel(
    share, previous, spectra, powers, forward, constant, down, back, *rest
):
    out, halves, crosses, mixed, scales, done, sems = rest[-7:]
    pairs = [share[start : start + 2] for start in range(0, len(share), 2)]
    for n, p in enumerate(share):
        cosine_part, sine_part, power = spectrum_columns(previous[n], forward, constant)
        at = pl.ds(n % 2 * PS, PS)
        halves[n // 2, :PS, at] = cosine_part
        halves[n // 2, PS:, at] = sine_part
        product = (powers[pl.ds(p, 1), :] + EPSILON) * (power + EPSILON)
        scales[pl.ds(n, 1), :] = lax.rsqrt(product) * (1.0 / (PS * PS * PS))
    for q, pair in enumerate(pairs):
        width = PS * len(pair)
        second = dot(down[...], halves[q, :, :width])
        for n, p in enumerate(pair):
            one_real, one_imag = spectra[p, :PS, :], spectra[p, PS:, :]
            two_real, two_imag = second[:PS, n * PS : (n + 1) * PS], second[PS:, n * PS : (n + 1) * PS]
            real = one_real * two_real + one_imag * two_imag
            imag = one_real * two_imag - one_imag * two_real
            crosses[q, :PS, pl.ds(n * PS, PS)] = real.astype(BF16)
            crosses[q, PS:, pl.ds(n * PS, PS)] = imag.astype(BF16)
    for q, pair in enumerate(pairs):
        width = PS * len(pair)
        both = dot(down[...], crosses[q, :, :width]).astype(BF16)
        for n, p in enumerate(pair):
            mixed[2 * q + n, :, :PS] = both[:PS, n * PS : (n + 1) * PS]
            mixed[2 * q + n, :, PS:] = both[PS:, n * PS : (n + 1) * PS]
    writes = []
    group = 5
    for n, p in enumerate(share):
        done[n] = dot(mixed[n], back[...]) * scales[pl.ds(n, 1), :]
        if n % group == group - 1 or n == len(share) - 1:
            first = n // group * group
            size = n + 1 - first
            writes.append(
                pltpu.make_async_copy(
                    done.at[pl.ds(first, size)],
                    out.at[pl.ds(share[0] + first, size)],
                    sems.at[n // group],
                )
            )
            writes[-1].start()
    for write in writes:
        write.wait()


def shares_of(patches):
    cuts = [0] + [round(patches * part) for part in PARTS] + [patches]
    return [range(a, b) for a, b in zip(cuts, cuts[1:])]


def params(megabytes, flops, moved):
    return dict(
        compiler_params=pltpu.CompilerParams(vmem_limit_bytes=megabytes << 20),
        cost_estimate=pl.CostEstimate(flops=flops, bytes_accessed=moved, transcendentals=0),
    )


def shards(source, pull_ids, interp_idx, interp_table, patch_pos):
    blocks = source[0]
    count = blocks.shape[0]
    grid = int(round(count**0.5))
    patches = patch_pos.shape[1]
    side = grid * BS
    near = count - CAP
    ids = pull_ids.transpose(2, 0, 1)
    mats = interp_idx[0].transpose(1, 2, 0)
    positions = patch_pos[0].T
    shares = shares_of(patches)
    sections = lax.axis_size("sec")
    tiles = lax.axis_size("tile")
    other = lax.ppermute(blocks, "tile", [(i, (i + 1) % tiles) for i in range(tiles)])
    plan = pl.pallas_call(
        functools.partial(plan_kernel, count, tiles),
        out_shape=jax.ShapeDtypeStruct((count * FIELDS,), jnp.int32),
        in_specs=[ANY] * 2,
        out_specs=SMEM,
        scratch_shapes=[
            pltpu.SMEM(ids.shape, jnp.int32),
            pltpu.SMEM(mats.shape, jnp.int32),
            pltpu.SemaphoreType.DMA((3,)),
        ],
        **params(16, 2 << 30, 16 << 20),
    )(ids, mats)
    plan, asked = lax.optimization_barrier((plan, positions))
    wanted = lax.ppermute(asked, "sec", [(i + 1, i) for i in range(sections - 1)])
    forward, constant, down, back = tables()

    begun = pl.pallas_call(
        functools.partial(near_kernel, count),
        out_shape=jax.ShapeDtypeStruct((near, BS, BS), BF16),
        in_specs=[SMEM, VMEM, VMEM],
        out_specs=VMEM,
        **params(16, near * KP * 4 * BS**3, near * (KP + 1) * BS * BS * 2),
    )(plan, blocks, interp_table)

    picture, sent = pl.pallas_call(
        functools.partial(far_kernel, count, grid, shares[0]),
        out_shape=(
            jax.ShapeDtypeStruct((side, side), BF16),
            jax.ShapeDtypeStruct((len(shares[0]), PS, PS), BF16),
        ),
        in_specs=[SMEM] * 2 + [VMEM] * 4,
        out_specs=(VMEM, VMEM),
        **params(16, CAP * KP * 4 * BS**3, CAP * (KP + 1) * BS * BS * 2),
    )(plan, wanted, blocks, other, interp_table, begun)

    onward = [(i, i + 1) for i in range(sections - 1)]
    arrivals = [lax.ppermute(sent, "sec", onward)]
    for share in shares[1:]:
        sent = pl.pallas_call(
            functools.partial(cut_windows, share),
            out_shape=jax.ShapeDtypeStruct((len(share), PS, PS), BF16),
            in_specs=[SMEM, VMEM],
            out_specs=VMEM,
            **params(16, len(share) * 10 * PS**3, len(share) * PS * PS * 8),
        )(wanted, picture)
        arrivals.append(lax.ppermute(sent, "sec", onward))

    spectra, powers, warped = pl.pallas_call(
        functools.partial(own_kernel, patches),
        out_shape=(
            jax.ShapeDtypeStruct((patches, 2 * PS, PS), F32),
            jax.ShapeDtypeStruct((patches, PS), F32),
            jax.ShapeDtypeStruct((side, side), BF16),
        ),
        in_specs=[SMEM] + [VMEM] * 4,
        out_specs=(VMEM, VMEM, ANY),
        scratch_shapes=[
            pltpu.VMEM((patches, PS, PS), BF16),
            pltpu.VMEM((patches, 2 * PS, PS), BF16),
            pltpu.SemaphoreType.DMA,
        ],
        **params(20, patches * 12 * PS**3, side * side * 2),
    )(positions, picture, forward, constant, down)

    correlations = ()
    for share, previous in zip(shares, arrivals):
        size = len(share)
        correlations = (
            pl.pallas_call(
                functools.partial(match_kernel, share),
                out_shape=jax.ShapeDtypeStruct((patches, PS, PS), F32),
                in_specs=[VMEM] * 7 + [ANY] * len(correlations),
                out_specs=ANY,
                scratch_shapes=[
                    pltpu.VMEM(((size + 1) // 2, 2 * PS, 2 * PS), BF16),
                    pltpu.VMEM(((size + 1) // 2, 2 * PS, 2 * PS), BF16),
                    pltpu.VMEM((size, PS, 2 * PS), BF16),
                    pltpu.VMEM((size, PS), F32),
                    pltpu.VMEM((size, PS, PS), F32),
                    pltpu.SemaphoreType.DMA(((size + 4) // 5,)),
                ],
                input_output_aliases={7: 0} if correlations else {},
                **params(16, size * 16 * PS**3, size * PS * PS * 14),
            )(previous, spectra, powers, forward, constant, down, back, *correlations),
        )
    (correlations,) = correlations
    return warped[None], correlations[None]


def solution(mesh):
    return jax.shard_map(
        shards,
        mesh=mesh,
        in_specs=(
            P(("parts", "sec"), "tile", None, None),
            P(("parts", "sec"), "tile", None),
            P(("parts", "sec"), "tile", None, None),
            P(),
            P(("parts", "sec"), "tile", None),
        ),
        out_specs=(P(("parts", "sec"), "tile", None), P(("parts", "sec"), "tile", None, None)),
        check_vma=False,
    )
```

time: 49.2 us -> 41.8 us (0.85)
  local copies, waits for them, and re-layouts: 6.84 us -> 1.4 us
  waiting for transfers between devices: 10.5 us -> 5.5 us
  starting transfers between devices: 6.1 us -> 10.6 us
  Pallas kernels: 24.7 us -> 23.1 us
    unnamed x19 -> x18, local copies, waits for them, and re-layouts: 6.84 us -> 1.4 us
    ppermute x2 -> x3, waiting for transfers between devices: 10.5 us -> 5.5 us  [the longest x1 4.01 us: shards(): arrivals = [lax.ppermute(sent, 'sec', onward)]]
    ppermute x2 -> x3, starting transfers between devices: 6.02 us -> 10.5 us  [the longest x1 4.28 us: shards(): arrivals.append(lax.ppermute(sent, 'sec', onward))]
    pallas_call x1, Pallas kernels: 7.95 us -> 5.18 us  [shards(): pl.pallas_call(functools.partial(own_kernel, patches), out_shape=(jax.Sha...]
    pallas_call x2 -> x5, Pallas kernels: 12.8 us -> 14.3 us  [the longest x2 6.87 us: shards(): pl.pallas_call(functools.partial(match_kernel, share), out_shape=jax.Shap...]
  transfers between devices with their start and end apart: 3 -> 4, of which waited for: 1 -> 2; matrix products, arithmetic and copies ran while one was open for 1% -> 0% of each run, Pallas kernels for 24% -> 38%
where the time goes in v3:
time: 41.8 us; the launch traced here: 41.5 us
  Pallas kernels  23.1 us (55%)
  starting transfers between devices  10.6 us (25%)
  waiting for transfers between devices  5.5 us (13%)
  local copies, waits for them, and re-layouts  1.4 us (3%)
  between operations  0.97 us (2%)
    pallas_call x2, Pallas kernels, shards(): pl.pallas_call(functools.partial(match_kernel, share), out_shape=jax.Shap...  6.87 us
    pallas_call x1, Pallas kernels, shards(): pl.pallas_call(functools.partial(own_kernel, patches), out_shape=(jax.Sha...  5.18 us
    pallas_call x1, Pallas kernels, shards(): pl.pallas_call(functools.partial(far_kernel, count, grid, shares[0]), out...  4.48 us
    ppermute x1, starting transfers between devices, shards(): arrivals.append(lax.ppermute(sent, 'sec', onward))  4.28 us
    ppermute x1, waiting for transfers between devices, shards(): arrivals = [lax.ppermute(sent, 'sec', onward)]  4.01 us
    pallas_call x1, Pallas kernels, shards(): pl.pallas_call(functools.partial(near_kernel, count), out_shape=jax.Shape...  3.66 us
    ppermute x1, starting transfers between devices, shards(): lax.ppermute(asked, 'sec', [(i + 1, i) for i in range(sections - 1)])  3.31 us
    ppermute x1, starting transfers between devices, shards(): arrivals = [lax.ppermute(sent, 'sec', onward)]  2.89 us
  transfers between devices with their start and end apart: 4, of which 2 were waited for; matrix products, arithmetic and copies ran while one was open for 0% of the time, Pallas kernels for 38%

profile of v3, /device:TPU:10, one launch (start us, length us, event | category | flops | bytes accessed | tf_op | source)
XLA Modules:
  0.0 41.5 jit_solution(14579110467344082194)
XLA Ops:
  0.6 0.1 collective-permute-start.1
  0.7 0.7 %copy-done.7 = s32[1,25,3,2]{1,3,2,0:T(2,128)S(1)} copy-done((s32[1,25,3,2]{1,3,2,0:T(2,128)S(1)}, s32[1,25,3,2]{1,3,2,0:T(2,128)}, u32[]{:S(2)}) %copy-start.7) | copy-done | bytes 624
  1.4 0.7 %copy-done.8 = s32[1,25,3]{1,0,2:T(1,128)S(1)} copy-done((s32[1,25,3]{1,0,2:T(1,128)S(1)}, s32[1,25,3]{1,0,2:T(1,128)}, u32[]{:S(2)}) %copy-start.8) | copy-done | bytes 324
  2.1 1.7 %shard_map.104.plan = s32[250]{0:T(256)S(1)} custom-call(s32[3,1,25]{2,1,0:T(1,128)S(1)} %bitcast.16, s32[3,2,25]{2,1,0:T(2,128)S(1)} %bitcast.15), custom_call_target="tpu_custom_call" | custom-call | flops 2147483648 | bytes 16777216 | tf_op jit(solution)/shard_map/pallas_call | solution.py:231
  3.8 0.0 copy-done.6
  3.8 3.3 %collective-permute-start = (s32[2,25]{1,0:T(2,128)S(1)}, s32[2,25]{1,0:T(2,128)S(1)}, u32[]{:S(2)}, u32[]{:S(2)}) collective-permute-start(s32[2,25]{1,0:T(2,128)S(1)} %bitcast.13), channel_id=1, source_target_pairs={{2,0},{4,2},{6,4},{8,6},{10,8},{12,10},{14,12},{3,1},{5,3},{7,5},{... | collective-permute-start | bytes 608 | tf_op jit(solution)/shard_map/ppermute | solution.py:244
  7.1 0.0 copy-done
  7.1 0.0 copy-done.1
  7.1 3.7 %shard_map.105.begun = bf16[13,256,256]{2,1,0:T(8,128)(2,1)S(1)} custom-call(s32[250]{0:T(256)S(1)} %shard_map.104.plan, bf16[25,256,256]{2,1,0:T(8,128)(2,1)S(1)} %bitcast.11, bf16[16,256,256]{2,1,0:T(8,128)(2,1)S(1)} %copy-done.1), custom_call_target="tpu_custom_call" | custom-call | flops 2617245696 | bytes 6815744 | tf_op jit(solution)/shard_map/pallas_call | solution.py:247
  10.8 0.0 collective-permute-done.corners
  10.8 0.0 collective-permute-done.1.other
  10.8 4.5 %shard_map.106 = (bf16[1280,1280]{1,0:T(8,128)(2,1)S(1)}, bf16[16,128,128]{2,1,0:T(8,128)(2,1)S(1)}) custom-call(s32[250]{0:T(256)S(1)} %shard_map.104.plan, s32[2,25]{1,0:T(2,128)S(1)} %collective-permute-done.corners, bf16[25,256,256]{2,1,0:T(8,128)(2,1)S(1)} %bitcast.12, bf16[25,256,256]{2,1,0:T(8,128)(2,1)S(1)} %collective-permute-done.1.other, ...), custom_call_target="tpu_custom_call" | custom-call | flops 2415919104 | bytes 6291456 | tf_op jit(solution)/shard_map/pallas_call | solution.py:255
  15.3 0.0 copy-start.2
  15.3 0.0 copy-start.3
  15.3 0.0 copy-start.5
  15.3 2.9 %collective-permute-start.3 = (bf16[16,128,128]{2,1,0:T(8,128)(2,1)S(1)}, bf16[16,128,128]{2,1,0:T(8,128)(2,1)S(1)}, u32[]{:S(2)}, u32[]{:S(2)}) collective-permute-start(bf16[16,128,128]{2,1,0:T(8,128)(2,1)S(1)} %get-tuple-element.15), channel_id=1, source_target_pairs={{0,2},{2,4},{4,6},{6,8},{8,10},{10,12},{12,14},{1,3},{3,5},{5,7},{... | collective-permute-start | bytes 1572872 | tf_op jit(solution)/shard_map/ppermute | solution.py:267
  18.2 0.0 copy-start.4
  18.2 1.2 %shard_map.108 = bf16[9,128,128]{2,1,0:T(8,128)(2,1)S(1)} custom-call(s32[2,25]{1,0:T(2,128)S(1)} %collective-permute-done.corners, bf16[1280,1280]{1,0:T(8,128)(2,1)S(1)} %get-tuple-element.11.picture), custom_call_target="tpu_custom_call" | custom-call | flops 188743680 | bytes 1179648 | tf_op jit(solution)/shard_map/pallas_call | solution.py:269
  19.5 4.3 %collective-permute-start.2 = (bf16[9,128,128]{2,1,0:T(8,128)(2,1)S(1)}, bf16[9,128,128]{2,1,0:T(8,128)(2,1)S(1)}, u32[]{:S(2)}, u32[]{:S(2)}) collective-permute-start(bf16[9,128,128]{2,1,0:T(8,128)(2,1)S(1)} %shard_map.108), channel_id=1, source_target_pairs={{0,2},{2,4},{4,6},{6,8},{8,10},{10,12},{12,14},{1,3},{3,5},{5,7},{... | collective-permute-start | bytes 884744 | tf_op jit(solution)/shard_map/ppermute | solution.py:276
  23.8 5.2 %shard_map.107 = (f32[25,256,128]{2,1,0:T(8,128)S(1)}, f32[25,128]{1,0:T(8,128)S(1)}, bf16[1280,1280]{1,0:T(8,128)(2,1)}) custom-call(s32[2,25]{1,0:T(2,128)S(1)} %bitcast.14, bf16[1280,1280]{1,0:T(8,128)(2,1)S(1)} %get-tuple-element.11.picture, bf16[256,256]{1,0:T(8,128)(2,1)S(1)} %copy-done.3, f32[1,256]{1,0:T(1,128)S(1)} %copy-done.5, ...), custom_call_target="tpu_custom_call" | custom-call | flops 629145600 | bytes 3276800 | tf_op jit(solution)/shard_map/pallas_call | solution.py:278
  29.0 4.0 %collective-permute-done.3.previous = bf16[16,128,128]{2,1,0:T(8,128)(2,1)S(1)} collective-permute-done((bf16[16,128,128]{2,1,0:T(8,128)(2,1)S(1)}, bf16[16,128,128]{2,1,0:T(8,128)(2,1)S(1)}, u32[]{:S(2)}, u32[]{:S(2)}) %collective-permute-start.3) | collective-permute-done | bytes 524320 | tf_op jit(solution)/shard_map/ppermute | solution.py:267
  33.0 4.1 %shard_map.109.rest_0_ = f32[25,128,128]{2,1,0:T(8,128)} custom-call(bf16[16,128,128]{2,1,0:T(8,128)(2,1)S(1)} %collective-permute-done.3.previous, f32[25,256,128]{2,1,0:T(8,128)S(1)} %get-tuple-element.13.spectra, f32[25,128]{1,0:T(8,128)S(1)} %get-tuple-element.14.powers, bf16[256,256]{1,0:T(8,128)(2,1)S(1)} %copy-done.3, f32[1,256]{1,0:T(1,128)S(1)} %copy-done.5, ...), custom_call_target="tpu_custom_call" | custom-call | flops 536870912 | bytes 3670016 | tf_op jit(solution)/shard_map/pallas_call | solution.py:299
  37.1 1.5 %collective-permute-done.2.previous = bf16[9,128,128]{2,1,0:T(8,128)(2,1)S(1)} collective-permute-done((bf16[9,128,128]{2,1,0:T(8,128)(2,1)S(1)}, bf16[9,128,128]{2,1,0:T(8,128)(2,1)S(1)}, u32[]{:S(2)}, u32[]{:S(2)}) %collective-permute-start.2) | collective-permute-done | bytes 294944 | tf_op jit(solution)/shard_map/ppermute | solution.py:276
  38.6 2.7 %shard_map.110 = f32[25,128,128]{2,1,0:T(8,128)} custom-call(bf16[9,128,128]{2,1,0:T(8,128)(2,1)S(1)} %collective-permute-done.2.previous, f32[25,256,128]{2,1,0:T(8,128)S(1)} %get-tuple-element.13.spectra, f32[25,128]{1,0:T(8,128)S(1)} %get-tuple-element.14.powers, bf16[256,256]{1,0:T(8,128)(2,1)S(1)} %copy-done.3, ...), custom_call_target="tpu_custom_call", output_to_operand_aliasing={{}: (7, {})} | custom-call | flops 301989888 | bytes 2064384 | tf_op jit(solution)/shard_map/pallas_call | solution.py:299
  (9 shorter events, 0.0 us)
Async XLA Ops:
  0.6 10.2 %collective-permute-start.1 = (bf16[25,256,256]{2,1,0:T(8,128)(2,1)}, bf16[25,256,256]{2,1,0:T(8,128)(2,1)S(1)}, u32[]{:S(2)}, u32[]{:S(2)}) collective-permute-start(bf16[25,256,256]{2,1,0:T(8,128)(2,1)} %bitcast.10), channel_id=1, source_target_pairs={{0,1},{1,0},{2,3},{3,2},{4,5},{5,4},{6,7},{7,6},{8,9},{9,8},{10,11... | collective-permute-start | bytes 9830408 | tf_op jit(solution)/shard_map/ppermute | solution.py:230
  0.7 0.7 %copy-start.7 = (s32[1,25,3,2]{1,3,2,0:T(2,128)S(1)}, s32[1,25,3,2]{1,3,2,0:T(2,128)}, u32[]{:S(2)}) copy-start(s32[1,25,3,2]{1,3,2,0:T(2,128)} %param.11) | copy-start | bytes 1804
  1.4 0.7 %copy-start.8 = (s32[1,25,3]{1,0,2:T(1,128)S(1)}, s32[1,25,3]{1,0,2:T(1,128)}, u32[]{:S(2)}) copy-start(s32[1,25,3]{1,0,2:T(1,128)} %param.10) | copy-start | bytes 904
  2.1 1.7 %copy-start.6 = (s32[1,25,2]{1,2,0:T(2,128)S(1)}, s32[1,25,2]{1,2,0:T(2,128)}, u32[]{:S(2)}) copy-start(s32[1,25,2]{1,2,0:T(2,128)} %param.13) | copy-start | bytes 604
  2.1 5.0 %copy-start = (bf16[1,25,256,256]{3,2,1,0:T(8,128)(2,1)S(1)}, bf16[1,25,256,256]{3,2,1,0:T(8,128)(2,1)}, u32[]{:S(2)}) copy-start(bf16[1,25,256,256]{3,2,1,0:T(8,128)(2,1)} %param.9) | copy-start | bytes 9830404
  2.1 5.0 %copy-start.1 = (bf16[16,256,256]{2,1,0:T(8,128)(2,1)S(1)}, bf16[16,256,256]{2,1,0:T(8,128)(2,1)}, u32[]{:S(2)}) copy-start(bf16[16,256,256]{2,1,0:T(8,128)(2,1)} %table.3) | copy-start | bytes 6291460
  3.8 7.0 %collective-permute-start = (s32[2,25]{1,0:T(2,128)S(1)}, s32[2,25]{1,0:T(2,128)S(1)}, u32[]{:S(2)}, u32[]{:S(2)}) collective-permute-start(s32[2,25]{1,0:T(2,128)S(1)} %bitcast.13), channel_id=1, source_target_pairs={{2,0},{4,2},{6,4},{8,6},{10,8},{12,10},{14,12},{3,1},{5,3},{7,5},{... | collective-permute-start | bytes 608 | tf_op jit(solution)/shard_map/ppermute | solution.py:244
  15.3 8.5 %copy-start.2 = (bf16[256,256]{1,0:T(8,128)(2,1)S(1)}, bf16[256,256]{1,0:T(8,128)(2,1)}, u32[]{:S(2)}) copy-start(bf16[256,256]{1,0:T(8,128)(2,1)} %constant.13.clone.down) | copy-start | bytes 393220
  15.3 8.5 %copy-start.3 = (bf16[256,256]{1,0:T(8,128)(2,1)S(1)}, bf16[256,256]{1,0:T(8,128)(2,1)}, u32[]{:S(2)}) copy-start(bf16[256,256]{1,0:T(8,128)(2,1)} %constant.11.clone.forward) | copy-start | bytes 393220
  15.3 8.5 %copy-start.5 = (f32[1,256]{1,0:T(1,128)S(1)}, f32[1,256]{1,0:T(1,128)}, u32[]{:S(2)}) copy-start(f32[1,256]{1,0:T(1,128)} %constant.12.clone) | copy-start | bytes 3076
  15.3 17.7 %collective-permute-start.3 = (bf16[16,128,128]{2,1,0:T(8,128)(2,1)S(1)}, bf16[16,128,128]{2,1,0:T(8,128)(2,1)S(1)}, u32[]{:S(2)}, u32[]{:S(2)}) collective-permute-start(bf16[16,128,128]{2,1,0:T(8,128)(2,1)S(1)} %get-tuple-element.15), channel_id=1, source_target_pairs={{0,2},{2,4},{4,6},{6,8},{8,10},{10,12},{12,14},{1,3},{3,5},{5,7},{... | collective-permute-start | bytes 1572872 | tf_op jit(solution)/shard_map/ppermute | solution.py:267
  18.2 14.8 %copy-start.4 = (bf16[256,128]{1,0:T(8,128)(2,1)S(1)}, bf16[256,128]{1,0:T(8,128)(2,1)}, u32[]{:S(2)}) copy-start(bf16[256,128]{1,0:T(8,128)(2,1)} %constant.14.clone.back) | copy-start | bytes 196612
  19.5 19.1 %collective-permute-start.2 = (bf16[9,128,128]{2,1,0:T(8,128)(2,1)S(1)}, bf16[9,128,128]{2,1,0:T(8,128)(2,1)S(1)}, u32[]{:S(2)}, u32[]{:S(2)}) collective-permute-start(bf16[9,128,128]{2,1,0:T(8,128)(2,1)S(1)} %shard_map.108), channel_id=1, source_target_pairs={{0,2},{2,4},{4,6},{6,8},{8,10},{10,12},{12,14},{1,3},{3,5},{5,7},{... | collective-permute-start | bytes 884744 | tf_op jit(solution)/shard_map/ppermute | solution.py:276

commit v4 on v3

--- a/solution.py
+++ b/solution.py
@@ -27,16 +27,19 @@
 
 def tables():
     grid = np.arange(PS)
-    angle = 2.0 * np.pi / PS * (grid[:, None] * grid[None, :] % PS)
-    cosine, sine = np.cos(angle), np.sin(angle)
+    folded = np.minimum(grid, PS - grid)
+    quarter = np.minimum(folded, PS // 2 - folded)
+    wave = np.sign(PS // 4 - folded) * np.cos(2.0 * np.pi / PS * quarter)
+    phase = grid[:, None] * grid[None, :] % PS
+    cosine, sine = wave[phase], wave[(phase + 3 * PS // 4) % PS]
     across = np.concatenate([cosine, sine], axis=1)
     high = across.astype(ml_dtypes.bfloat16)
     low = (across - high.astype(np.float64)).astype(ml_dtypes.bfloat16)
     forward = np.concatenate([high, low], axis=0)
-    constant = forward.astype(np.float64).sum(axis=0, keepdims=True).astype(np.float32)
+    lowest = (grid[None, :] == 0).astype(np.float32) / PS
     down = np.block([[cosine, -sine], [sine, cosine]]).astype(ml_dtypes.bfloat16)
     back = np.concatenate([cosine, -sine], axis=0).astype(ml_dtypes.bfloat16)
-    return forward, constant, down, back
+    return forward, lowest, down, back
 
 
 def dot(a, b):
@@ -46,15 +49,11 @@
 FIELDS = 1 + 3 * KP
 
 
-def plan_kernel(count, tiles, ids_from, mats_from, plan, ids, mats, sems):
-    copies = [
-        pltpu.make_async_copy(ids_from, ids, sems.at[0]),
-        pltpu.make_async_copy(mats_from, mats, sems.at[1]),
-    ]
-    for copy in copies:
-        copy.start()
-    for copy in copies:
-        copy.wait()
+def gate_kernel(out):
+    out[...] = jnp.zeros(out.shape, out.dtype)
+
+
+def make_plan(count, tiles, ids, mats, plan):
     low = lax.axis_index("tile") * count
     first, last = jnp.int32(0), jnp.int32(count - 1)
     for b in range(count):
@@ -93,7 +92,8 @@
     return total.astype(BF16)
 
 
-def near_kernel(count, plan, source, table, begun):
+def near_kernel(count, tiles, ids, mats, source, table, gate, begun, plan):
+    make_plan(count, tiles, ids, mats, plan)
     for n in range(count - CAP):
         begun[n] = warp_block(n, plan, table, lambda index: source[index])
 
@@ -116,8 +116,11 @@
         out[n] = window(picture, corners[0, p], corners[1, p])
 
 
-def far_kernel(count, grid, share, plan, corners, source, other, table, begun, picture, out):
+def far_kernel(
+    count, tiles, grid, share, ids, mats, corners, source, other, table, begun, picture, out, plan
+):
     near = count - CAP
+    make_plan(count, tiles, ids, mats, plan)
 
     def pulled(index):
         here = index < count
@@ -131,48 +134,50 @@
     cut_windows(share, corners, picture, out)
 
 
-def spectrum_columns(patch, forward, constant):
-    values = patch.astype(F32)
-    mean = jnp.sum(values, keepdims=True) * (1.0 / (PS * PS))
-    centred = values - mean
-    power = jnp.sum(centred * centred, keepdims=True) * (1.0 / (PS * PS))
-    halves = dot(jnp.concatenate([patch, patch], axis=1), forward[...]) - mean * constant[...]
-    halves = halves.astype(BF16)
-    return halves[:, :PS], halves[:, PS:], power
-
-
-def own_kernel(patches, corners, picture, forward, constant, down, out, power_out, warped, bands, halves, sem):
+def spectrum_columns(patch, forward, lowest):
+    halves = dot(jnp.concatenate([patch, patch], axis=1), forward[...])
+    cosine_part, sine_part = halves[:, :PS], halves[:, PS:]
+    cosine_part = cosine_part - jnp.sum(cosine_part, axis=0, keepdims=True) * lowest[...]
+    return cosine_part.astype(BF16), sine_part.astype(BF16)
+
+
+def energy(real, imag):
+    return jnp.sum(real * real + imag * imag, axis=0, keepdims=True)
+
+
+def mean_square(energies):
+    return jnp.sum(energies, axis=1, keepdims=True) * (1.0 / PS**4)
+
+
+def own_kernel(patches, corners, picture, forward, lowest, down, out, power_out, warped, bands, halves, sem):
     write = pltpu.make_async_copy(picture, warped, sem)
     write.start()
     cut_windows(range(patches), corners, picture, bands)
     for p in range(patches):
-        cosine_part, sine_part, power = spectrum_columns(bands[p], forward, constant)
-        halves[p, :PS] = cosine_part
-        halves[p, PS:] = sine_part
-        power_out[pl.ds(p, 1), :] = jnp.broadcast_to(power, (1, PS))
+        halves[p, :PS], halves[p, PS:] = spectrum_columns(bands[p], forward, lowest)
     for p in range(patches):
-        out[p] = dot(down[...], halves[p])
+        both = dot(down[...], halves[p])
+        out[p] = both
+        power_out[pl.ds(p, 1), :] = energy(both[:PS], both[PS:])
+    power_out[...] = jnp.broadcast_to(mean_square(power_out[...]), power_out.shape)
     write.wait()
 
 
 def match_kernel(
-    share, previous, spectra, powers, forward, constant, down, back, *rest
+    share, previous, spectra, powers, forward, lowest, down, back, *rest
 ):
     out, halves, crosses, mixed, scales, done, sems = rest[-7:]
     pairs = [share[start : start + 2] for start in range(0, len(share), 2)]
-    for n, p in enumerate(share):
-        cosine_part, sine_part, power = spectrum_columns(previous[n], forward, constant)
+    for n in range(len(share)):
         at = pl.ds(n % 2 * PS, PS)
-        halves[n // 2, :PS, at] = cosine_part
-        halves[n // 2, PS:, at] = sine_part
-        product = (powers[pl.ds(p, 1), :] + EPSILON) * (power + EPSILON)
-        scales[pl.ds(n, 1), :] = lax.rsqrt(product) * (1.0 / (PS * PS * PS))
+        halves[n // 2, :PS, at], halves[n // 2, PS:, at] = spectrum_columns(previous[n], forward, lowest)
     for q, pair in enumerate(pairs):
         width = PS * len(pair)
         second = dot(down[...], halves[q, :, :width])
         for n, p in enumerate(pair):
             one_real, one_imag = spectra[p, :PS, :], spectra[p, PS:, :]
             two_real, two_imag = second[:PS, n * PS : (n + 1) * PS], second[PS:, n * PS : (n + 1) * PS]
+            scales[pl.ds(2 * q + n, 1), :] = energy(two_real, two_imag)
             real = one_real * two_real + one_imag * two_imag
             imag = one_real * two_imag - one_imag * two_real
             crosses[q, :PS, pl.ds(n * PS, PS)] = real.astype(BF16)
@@ -183,9 +188,11 @@
         for n, p in enumerate(pair):
             mixed[2 * q + n, :, :PS] = both[:PS, n * PS : (n + 1) * PS]
             mixed[2 * q + n, :, PS:] = both[PS:, n * PS : (n + 1) * PS]
+    product = (powers[pl.ds(share[0], len(share)), :] + EPSILON) * (mean_square(scales[...]) + EPSILON)
+    scales[...] = lax.rsqrt(product) * (1.0 / (PS * PS * PS))
     writes = []
     group = 5
-    for n, p in enumerate(share):
+    for n in range(len(share)):
         done[n] = dot(mixed[n], back[...]) * scales[pl.ds(n, 1), :]
         if n % group == group - 1 or n == len(share) - 1:
             first = n // group * group
@@ -228,40 +235,36 @@
     sections = lax.axis_size("sec")
     tiles = lax.axis_size("tile")
     other = lax.ppermute(blocks, "tile", [(i, (i + 1) % tiles) for i in range(tiles)])
-    plan = pl.pallas_call(
-        functools.partial(plan_kernel, count, tiles),
-        out_shape=jax.ShapeDtypeStruct((count * FIELDS,), jnp.int32),
-        in_specs=[ANY] * 2,
-        out_specs=SMEM,
-        scratch_shapes=[
-            pltpu.SMEM(ids.shape, jnp.int32),
-            pltpu.SMEM(mats.shape, jnp.int32),
-            pltpu.SemaphoreType.DMA((3,)),
-        ],
+    gate = pl.pallas_call(
+        gate_kernel,
+        out_shape=jax.ShapeDtypeStruct((8, 128), F32),
+        out_specs=VMEM,
         **params(16, 2 << 30, 16 << 20),
-    )(ids, mats)
-    plan, asked = lax.optimization_barrier((plan, positions))
+    )()
+    gate, asked = lax.optimization_barrier((gate, positions))
     wanted = lax.ppermute(asked, "sec", [(i + 1, i) for i in range(sections - 1)])
-    forward, constant, down, back = tables()
+    forward, lowest, down, back = tables()
 
     begun = pl.pallas_call(
-        functools.partial(near_kernel, count),
+        functools.partial(near_kernel, count, tiles),
         out_shape=jax.ShapeDtypeStruct((near, BS, BS), BF16),
-        in_specs=[SMEM, VMEM, VMEM],
+        in_specs=[SMEM, SMEM, VMEM, VMEM, ANY],
         out_specs=VMEM,
+        scratch_shapes=[pltpu.SMEM((count * FIELDS,), jnp.int32)],
         **params(16, near * KP * 4 * BS**3, near * (KP + 1) * BS * BS * 2),
-    )(plan, blocks, interp_table)
+    )(ids, mats, blocks, interp_table, gate)
 
     picture, sent = pl.pallas_call(
-        functools.partial(far_kernel, count, grid, shares[0]),
+        functools.partial(far_kernel, count, tiles, grid, shares[0]),
         out_shape=(
             jax.ShapeDtypeStruct((side, side), BF16),
             jax.ShapeDtypeStruct((len(shares[0]), PS, PS), BF16),
         ),
-        in_specs=[SMEM] * 2 + [VMEM] * 4,
+        in_specs=[SMEM] * 3 + [VMEM] * 4,
         out_specs=(VMEM, VMEM),
+        scratch_shapes=[pltpu.SMEM((count * FIELDS,), jnp.int32)],
         **params(16, CAP * KP * 4 * BS**3, CAP * (KP + 1) * BS * BS * 2),
-    )(plan, wanted, blocks, other, interp_table, begun)
+    )(ids, mats, wanted, blocks, other, interp_table, begun)
 
     onward = [(i, i + 1) for i in range(sections - 1)]
     arrivals = [lax.ppermute(sent, "sec", onward)]
@@ -290,7 +293,7 @@
             pltpu.SemaphoreType.DMA,
         ],
         **params(20, patches * 12 * PS**3, side * side * 2),
-    )(positions, picture, forward, constant, down)
+    )(positions, picture, forward, lowest, down)
 
     correlations = ()
     for share, previous in zip(shares, arrivals):
@@ -311,7 +314,7 @@
                 ],
                 input_output_aliases={7: 0} if correlations else {},
                 **params(16, size * 16 * PS**3, size * PS * PS * 14),
-            )(previous, spectra, powers, forward, constant, down, back, *correlations),
+            )(previous, spectra, powers, forward, lowest, down, back, *correlations),
         )
     (correlations,) = correlations
     return warped[None], correlations[None]

time: 41.8 us -> 39.1 us (0.935)
  Pallas kernels: 23.1 us -> 18.1 us
  waiting for transfers between devices: 5.5 us -> 8.32 us
  local copies, waits for them, and re-layouts: 1.4 us -> 0.59 us
    pallas_call x2, Pallas kernels: 6.87 us -> 4.63 us  [shards(): pl.pallas_call(functools.partial(match_kernel, share), out_shape=jax.Shap...]
    ppermute x1, waiting for transfers between devices: 4.01 us -> 6.04 us  [shards(): arrivals = [lax.ppermute(sent, 'sec', onward)]]
    pallas_call x1, Pallas kernels: 5.18 us -> 3.24 us  [shards(): pl.pallas_call(functools.partial(own_kernel, patches), out_shape=(jax.Sha...]
    unnamed x18, local copies, waits for them, and re-layouts: 1.4 us -> 0.59 us
    ppermute x1, waiting for transfers between devices: 1.48 us -> 2.28 us  [shards(): arrivals.append(lax.ppermute(sent, 'sec', onward))]
    pallas_call x3, Pallas kernels: 9.81 us -> 9.02 us  [the longest x1 4.89 us: shards(): pl.pallas_call(functools.partial(far_kernel, count, tiles, grid, shares[0...]
  transfers between devices with their start and end apart: 4 -> 4, of which waited for: 2 -> 2; matrix products, arithmetic and copies ran while one was open for 0% -> 0% of each run, Pallas kernels for 38% -> 29%
where the time goes in v4:
time: 39.1 us; the launch traced here: 38.9 us
  Pallas kernels  18.1 us (46%)
  starting transfers between devices  10.8 us (28%)
  waiting for transfers between devices  8.32 us (21%)
  between operations  1.01 us (3%)
  local copies, waits for them, and re-layouts  0.59 us (2%)
    ppermute x1, waiting for transfers between devices, shards(): arrivals = [lax.ppermute(sent, 'sec', onward)]  6.04 us
    pallas_call x1, Pallas kernels, shards(): pl.pallas_call(functools.partial(far_kernel, count, tiles, grid, shares[0...  4.89 us
    pallas_call x2, Pallas kernels, shards(): pl.pallas_call(functools.partial(match_kernel, share), out_shape=jax.Shap...  4.63 us
    ppermute x1, starting transfers between devices, shards(): arrivals.append(lax.ppermute(sent, 'sec', onward))  4.52 us
    pallas_call x1, Pallas kernels, shards(): pl.pallas_call(functools.partial(near_kernel, count, tiles), out_shape=ja...  4.14 us
    ppermute x1, starting transfers between devices, shards(): lax.ppermute(asked, 'sec', [(i + 1, i) for i in range(sections - 1)])  3.56 us
    pallas_call x1, Pallas kernels, shards(): pl.pallas_call(functools.partial(own_kernel, patches), out_shape=(jax.Sha...  3.24 us
    ppermute x1, starting transfers between devices, shards(): arrivals = [lax.ppermute(sent, 'sec', onward)]  2.64 us
  transfers between devices with their start and end apart: 4, of which 2 were waited for; matrix products, arithmetic and copies ran while one was open for 0% of the time, Pallas kernels for 29%

profile of v4, /device:TPU:10, one launch (start us, length us, event | category | flops | bytes accessed | tf_op | source)
XLA Modules:
  0.0 38.9 jit_solution(2090052552172947439)
XLA Ops:
  0.6 0.0 copy-start.8
  0.7 0.1 collective-permute-start.1
  0.8 0.5 %copy-done.8 = s32[1,25,2]{1,2,0:T(2,128)S(1)} copy-done((s32[1,25,2]{1,2,0:T(2,128)S(1)}, s32[1,25,2]{1,2,0:T(2,128)}, u32[]{:S(2)}) %copy-start.8) | copy-done | bytes 224
  1.3 3.6 %collective-permute-start = (s32[2,25]{1,0:T(2,128)S(1)}, s32[2,25]{1,0:T(2,128)S(1)}, u32[]{:S(2)}, u32[]{:S(2)}) collective-permute-start(s32[2,25]{1,0:T(2,128)S(1)} %bitcast.17), channel_id=1, source_target_pairs={{2,0},{4,2},{6,4},{8,6},{10,8},{12,10},{14,12},{3,1},{5,3},{7,5},{... | collective-permute-start | bytes 608 | tf_op jit(solution)/shard_map/ppermute | solution.py:245
  4.9 0.0 copy-done
  4.9 0.0 copy-done.1
  4.9 0.0 copy-done.6
  4.9 0.0 copy-done.7
  4.9 4.1 %shard_map.105.begun = bf16[13,256,256]{2,1,0:T(8,128)(2,1)S(1)} custom-call(s32[3,1,25]{2,1,0:T(1,128)S(1)} %bitcast.15, s32[3,2,25]{2,1,0:T(2,128)S(1)} %bitcast.13, bf16[25,256,256]{2,1,0:T(8,128)(2,1)S(1)} %bitcast.11, bf16[16,256,256]{2,1,0:T(8,128)(2,1)S(1)} %copy-done.1, f32[8,128]{1,0:T(8,128)S(1)} %shard_map.104.gate), custom_call_target="tpu_custom_call" | custom-call | flops 2617245696 | bytes 6815744 | tf_op jit(solution)/shard_map/pallas_call | solution.py:248
  9.1 0.0 collective-permute-done.corners
  9.1 0.0 collective-permute-done.1.other
  9.1 4.9 %shard_map.106 = (bf16[1280,1280]{1,0:T(8,128)(2,1)S(1)}, bf16[16,128,128]{2,1,0:T(8,128)(2,1)S(1)}) custom-call(s32[3,1,25]{2,1,0:T(1,128)S(1)} %bitcast.16, s32[3,2,25]{2,1,0:T(2,128)S(1)} %bitcast.14, s32[2,25]{1,0:T(2,128)S(1)} %collective-permute-done.corners, bf16[25,256,256]{2,1,0:T(8,128)(2,1)S(1)} %bitcast.12, ...), custom_call_target="tpu_custom_call" | custom-call | flops 2415919104 | bytes 6291456 | tf_op jit(solution)/shard_map/pallas_call | solution.py:257
  14.0 0.0 copy-start.2
  14.0 0.0 copy-start.3
  14.0 0.0 copy-start.5
  14.0 2.6 %collective-permute-start.3 = (bf16[16,128,128]{2,1,0:T(8,128)(2,1)S(1)}, bf16[16,128,128]{2,1,0:T(8,128)(2,1)S(1)}, u32[]{:S(2)}, u32[]{:S(2)}) collective-permute-start(bf16[16,128,128]{2,1,0:T(8,128)(2,1)S(1)} %get-tuple-element.15), channel_id=1, source_target_pairs={{0,2},{2,4},{4,6},{6,8},{8,10},{10,12},{12,14},{1,3},{3,5},{5,7},{... | collective-permute-start | bytes 1572872 | tf_op jit(solution)/shard_map/ppermute | solution.py:270
  16.7 0.0 copy-start.4
  16.7 1.2 %shard_map.108 = bf16[9,128,128]{2,1,0:T(8,128)(2,1)S(1)} custom-call(s32[2,25]{1,0:T(2,128)S(1)} %collective-permute-done.corners, bf16[1280,1280]{1,0:T(8,128)(2,1)S(1)} %get-tuple-element.11.picture), custom_call_target="tpu_custom_call" | custom-call | flops 188743680 | bytes 1179648 | tf_op jit(solution)/shard_map/pallas_call | solution.py:272
  17.9 4.5 %collective-permute-start.2 = (bf16[9,128,128]{2,1,0:T(8,128)(2,1)S(1)}, bf16[9,128,128]{2,1,0:T(8,128)(2,1)S(1)}, u32[]{:S(2)}, u32[]{:S(2)}) collective-permute-start(bf16[9,128,128]{2,1,0:T(8,128)(2,1)S(1)} %shard_map.108), channel_id=1, source_target_pairs={{0,2},{2,4},{4,6},{6,8},{8,10},{10,12},{12,14},{1,3},{3,5},{5,7},{... | collective-permute-start | bytes 884744 | tf_op jit(solution)/shard_map/ppermute | solution.py:279
  22.5 3.2 %shard_map.107 = (f32[25,256,128]{2,1,0:T(8,128)S(1)}, f32[25,128]{1,0:T(8,128)S(1)}, bf16[1280,1280]{1,0:T(8,128)(2,1)}) custom-call(s32[2,25]{1,0:T(2,128)S(1)} %bitcast.18, bf16[1280,1280]{1,0:T(8,128)(2,1)S(1)} %get-tuple-element.11.picture, bf16[256,256]{1,0:T(8,128)(2,1)S(1)} %copy-done.3, f32[1,128]{1,0:T(1,128)S(1)} %copy-done.5, ...), custom_call_target="tpu_custom_call" | custom-call | flops 629145600 | bytes 3276800 | tf_op jit(solution)/shard_map/pallas_call | solution.py:281
  25.7 6.0 %collective-permute-done.3.previous = bf16[16,128,128]{2,1,0:T(8,128)(2,1)S(1)} collective-permute-done((bf16[16,128,128]{2,1,0:T(8,128)(2,1)S(1)}, bf16[16,128,128]{2,1,0:T(8,128)(2,1)S(1)}, u32[]{:S(2)}, u32[]{:S(2)}) %collective-permute-start.3) | collective-permute-done | bytes 524320 | tf_op jit(solution)/shard_map/ppermute | solution.py:270
  31.8 2.7 %shard_map.109.rest_0_ = f32[25,128,128]{2,1,0:T(8,128)} custom-call(bf16[16,128,128]{2,1,0:T(8,128)(2,1)S(1)} %collective-permute-done.3.previous, f32[25,256,128]{2,1,0:T(8,128)S(1)} %get-tuple-element.13.spectra, f32[25,128]{1,0:T(8,128)S(1)} %get-tuple-element.14.powers, bf16[256,256]{1,0:T(8,128)(2,1)S(1)} %copy-done.3, f32[1,128]{1,0:T(1,128)S(1)} %copy-done.5, ...), custom_call_target="tpu_custom_call" | custom-call | flops 536870912 | bytes 3670016 | tf_op jit(solution)/shard_map/pallas_call | solution.py:302
  34.5 2.3 %collective-permute-done.2.previous = bf16[9,128,128]{2,1,0:T(8,128)(2,1)S(1)} collective-permute-done((bf16[9,128,128]{2,1,0:T(8,128)(2,1)S(1)}, bf16[9,128,128]{2,1,0:T(8,128)(2,1)S(1)}, u32[]{:S(2)}, u32[]{:S(2)}) %collective-permute-start.2) | collective-permute-done | bytes 294944 | tf_op jit(solution)/shard_map/ppermute | solution.py:279
  36.7 2.0 %shard_map.110 = f32[25,128,128]{2,1,0:T(8,128)} custom-call(bf16[9,128,128]{2,1,0:T(8,128)(2,1)S(1)} %collective-permute-done.2.previous, f32[25,256,128]{2,1,0:T(8,128)S(1)} %get-tuple-element.13.spectra, f32[25,128]{1,0:T(8,128)S(1)} %get-tuple-element.14.powers, bf16[256,256]{1,0:T(8,128)(2,1)S(1)} %copy-done.3, ...), custom_call_target="tpu_custom_call", output_to_operand_aliasing={{}: (7, {})} | custom-call | flops 301989888 | bytes 2064384 | tf_op jit(solution)/shard_map/pallas_call | solution.py:302
  (9 shorter events, 0.0 us)
Async XLA Ops:
  0.6 0.7 %copy-start.8 = (s32[1,25,2]{1,2,0:T(2,128)S(1)}, s32[1,25,2]{1,2,0:T(2,128)}, u32[]{:S(2)}) copy-start(s32[1,25,2]{1,2,0:T(2,128)} %param.13) | copy-start | bytes 604
  0.6 4.2 %copy-start = (bf16[1,25,256,256]{3,2,1,0:T(8,128)(2,1)S(1)}, bf16[1,25,256,256]{3,2,1,0:T(8,128)(2,1)}, u32[]{:S(2)}) copy-start(bf16[1,25,256,256]{3,2,1,0:T(8,128)(2,1)} %param.9) | copy-start | bytes 9830404
  0.7 4.2 %copy-start.1 = (bf16[16,256,256]{2,1,0:T(8,128)(2,1)S(1)}, bf16[16,256,256]{2,1,0:T(8,128)(2,1)}, u32[]{:S(2)}) copy-start(bf16[16,256,256]{2,1,0:T(8,128)(2,1)} %table.3) | copy-start | bytes 6291460
  0.7 4.2 %copy-start.6 = (s32[1,25,3,2]{1,3,2,0:T(2,128)S(1)}, s32[1,25,3,2]{1,3,2,0:T(2,128)}, u32[]{:S(2)}) copy-start(s32[1,25,3,2]{1,3,2,0:T(2,128)} %param.11) | copy-start | bytes 1804
  0.7 4.2 %copy-start.7 = (s32[1,25,3]{1,0,2:T(1,128)S(1)}, s32[1,25,3]{1,0,2:T(1,128)}, u32[]{:S(2)}) copy-start(s32[1,25,3]{1,0,2:T(1,128)} %param.10) | copy-start | bytes 904
  0.7 8.4 %collective-permute-start.1 = (bf16[25,256,256]{2,1,0:T(8,128)(2,1)}, bf16[25,256,256]{2,1,0:T(8,128)(2,1)S(1)}, u32[]{:S(2)}, u32[]{:S(2)}) collective-permute-start(bf16[25,256,256]{2,1,0:T(8,128)(2,1)} %bitcast.10), channel_id=1, source_target_pairs={{0,1},{1,0},{2,3},{3,2},{4,5},{5,4},{6,7},{7,6},{8,9},{9,8},{10,11... | collective-permute-start | bytes 9830408 | tf_op jit(solution)/shard_map/ppermute | solution.py:237
  1.3 7.8 %collective-permute-start = (s32[2,25]{1,0:T(2,128)S(1)}, s32[2,25]{1,0:T(2,128)S(1)}, u32[]{:S(2)}, u32[]{:S(2)}) collective-permute-start(s32[2,25]{1,0:T(2,128)S(1)} %bitcast.17), channel_id=1, source_target_pairs={{2,0},{4,2},{6,4},{8,6},{10,8},{12,10},{14,12},{3,1},{5,3},{7,5},{... | collective-permute-start | bytes 608 | tf_op jit(solution)/shard_map/ppermute | solution.py:245
  14.0 8.5 %copy-start.2 = (bf16[256,256]{1,0:T(8,128)(2,1)S(1)}, bf16[256,256]{1,0:T(8,128)(2,1)}, u32[]{:S(2)}) copy-start(bf16[256,256]{1,0:T(8,128)(2,1)} %constant.10.clone.down) | copy-start | bytes 393220
  14.0 8.5 %copy-start.3 = (bf16[256,256]{1,0:T(8,128)(2,1)S(1)}, bf16[256,256]{1,0:T(8,128)(2,1)}, u32[]{:S(2)}) copy-start(bf16[256,256]{1,0:T(8,128)(2,1)} %constant.8.clone.forward) | copy-start | bytes 393220
  14.0 8.5 %copy-start.5 = (f32[1,128]{1,0:T(1,128)S(1)}, f32[1,128]{1,0:T(1,128)}, u32[]{:S(2)}) copy-start(f32[1,128]{1,0:T(1,128)} %constant.9.clone.lowest) | copy-start | bytes 1540
  14.0 17.8 %collective-permute-start.3 = (bf16[16,128,128]{2,1,0:T(8,128)(2,1)S(1)}, bf16[16,128,128]{2,1,0:T(8,128)(2,1)S(1)}, u32[]{:S(2)}, u32[]{:S(2)}) collective-permute-start(bf16[16,128,128]{2,1,0:T(8,128)(2,1)S(1)} %get-tuple-element.15), channel_id=1, source_target_pairs={{0,2},{2,4},{4,6},{6,8},{8,10},{10,12},{12,14},{1,3},{3,5},{5,7},{... | collective-permute-start | bytes 1572872 | tf_op jit(solution)/shard_map/ppermute | solution.py:270
  16.7 15.1 %copy-start.4 = (bf16[256,128]{1,0:T(8,128)(2,1)S(1)}, bf16[256,128]{1,0:T(8,128)(2,1)}, u32[]{:S(2)}) copy-start(bf16[256,128]{1,0:T(8,128)(2,1)} %constant.11.clone.back) | copy-start | bytes 196612
  17.9 18.8 %collective-permute-start.2 = (bf16[9,128,128]{2,1,0:T(8,128)(2,1)S(1)}, bf16[9,128,128]{2,1,0:T(8,128)(2,1)S(1)}, u32[]{:S(2)}, u32[]{:S(2)}) collective-permute-start(bf16[9,128,128]{2,1,0:T(8,128)(2,1)S(1)} %shard_map.108), channel_id=1, source_target_pairs={{0,2},{2,4},{4,6},{6,8},{8,10},{10,12},{12,14},{1,3},{3,5},{5,7},{... | collective-permute-start | bytes 884744 | tf_op jit(solution)/shard_map/ppermute | solution.py:279

commit v5 on v4

v5 whole, which is shorter than its diff:
```python
import functools

import jax
import jax.numpy as jnp
import ml_dtypes
import numpy as np
from jax import lax
from jax.experimental import pallas as pl
from jax.experimental.pallas import tpu as pltpu
from jax.sharding import PartitionSpec as P

BS = 256
PS = 128
KP = 3
EPSILON = 1e-06
ROWS = PS + 16
COLS = 2 * PS

SMEM = pl.BlockSpec(memory_space=pltpu.SMEM)
VMEM = pl.BlockSpec(memory_space=pltpu.VMEM)
ANY = pl.BlockSpec(memory_space=pl.ANY)
F32 = jnp.float32
BF16 = jnp.bfloat16


def tables():
    grid = np.arange(PS)
    folded = np.minimum(grid, PS - grid)
    quarter = np.minimum(folded, PS // 2 - folded)
    wave = np.sign(PS // 4 - folded) * np.cos(2.0 * np.pi / PS * quarter)
    phase = grid[:, None] * grid[None, :] % PS
    cosine, sine = wave[phase], wave[(phase + 3 * PS // 4) % PS]
    across = np.concatenate([cosine, sine], axis=1)
    high = across.astype(ml_dtypes.bfloat16)
    low = (across - high.astype(np.float64)).astype(ml_dtypes.bfloat16)
    forward = np.concatenate([high, low], axis=0)
    lowest = (grid[None, :] == 0).astype(np.float32) / PS
    down = np.block([[cosine, -sine], [sine, cosine]]).astype(ml_dtypes.bfloat16)
    back = np.concatenate([cosine, -sine], axis=0).astype(ml_dtypes.bfloat16)
    return forward, lowest, down, back


def dot(a, b):
    return jnp.dot(a, b, preferred_element_type=F32)


def gate_kernel(out):
    out[...] = jnp.zeros(out.shape, out.dtype)


def early_rows(grid):
    return grid // 2 + 1


def from_top(corners, patches, grid):
    fitting = jnp.int32(0)
    for p in range(patches):
        fitting = fitting + (corners[0, p] <= early_rows(grid) * BS - PS).astype(jnp.int32)
    return fitting >= (patches + 1) // 2


def window_order(corners, order, patches, grid):
    down = jnp.where(from_top(corners, patches, grid), 0, grid - early_rows(grid))
    low = down * BS
    high = low + early_rows(grid) * BS - PS
    front, back = jnp.int32(0), jnp.int32(patches - 1)
    for p in range(patches):
        y = corners[0, p]
        early = ((y >= low) & (y <= high) & (front < (patches + 1) // 2)).astype(jnp.int32)
        order[back + early * (front - back)] = p
        front = front + early
        back = back + early - 1
    return down


def warp_block(block, low, count, ids, mats, source, other, table):
    total = None
    for k in range(KP):
        local = ids[k, 0, block] - low
        here = (local >= 0) & (local < count)
        away = jnp.where(local < 0, local + count, local - count)
        pulled = jnp.where(here, source[jnp.where(here, local, 0)], other[jnp.where(here, 0, away)])
        left = dot(table[mats[k, 0, block]], pulled).astype(BF16)
        term = lax.dot_general(
            left, table[mats[k, 1, block]], (((1,), (1,)), ((), ())), preferred_element_type=F32
        )
        total = term if total is None else total + term
    return total.astype(BF16)


def window(picture, y, x):
    top = pl.multiple_of(jnp.minimum(y // 16 * 16, picture.shape[0] - ROWS), 16)
    left = pl.multiple_of(jnp.minimum(x // PS * PS, picture.shape[1] - COLS), PS)
    area = picture[pl.ds(top, ROWS), pl.ds(left, COLS)]
    i = lax.broadcasted_iota(jnp.int32, (PS, ROWS), 0)
    r = lax.broadcasted_iota(jnp.int32, (PS, ROWS), 1)
    pick_rows = (r - i == y - top).astype(F32).astype(BF16)
    c = lax.broadcasted_iota(jnp.int32, (COLS, PS), 0)
    j = lax.broadcasted_iota(jnp.int32, (COLS, PS), 1)
    pick_cols = (c - j == x - left).astype(F32).astype(BF16)
    return dot(dot(pick_rows, area).astype(BF16), pick_cols).astype(BF16)


def early_kernel(
    count, grid, patches, ids, mats, corners, source, other, table, gate, early, out, order
):
    low = lax.axis_index("tile") * count
    down = window_order(corners, order, patches, grid)
    for n in range(early_rows(grid) * grid):
        block = down * grid + n
        at = pl.ds(n // grid * BS, BS), pl.ds(n % grid * BS, BS)
        early[at] = warp_block(block, low, count, ids, mats, source, other, table)
    for n in range(out.shape[0]):
        p = order[n]
        out[n] = window(early, corners[0, p] - down * BS, corners[1, p])


def late_kernel(
    count, grid, patches, ids, mats, corners, source, other, table, early, picture, out, order
):
    low = lax.axis_index("tile") * count
    rows = early_rows(grid)
    down = window_order(corners, order, patches, grid)
    for n in range(rows):
        picture[pl.ds(pl.multiple_of((down + n) * BS, BS), BS), :] = early[pl.ds(n * BS, BS), :]
    after = lax.rem(down + rows, grid)
    for n in range((grid - rows) * grid):
        row = pl.multiple_of((after + n // grid) * BS, BS)
        block = after * grid + n
        picture[pl.ds(row, BS), pl.ds(n % grid * BS, BS)] = warp_block(
            block, low, count, ids, mats, source, other, table
        )
    for n in range(out.shape[0]):
        p = order[patches - out.shape[0] + n]
        out[n] = window(picture, corners[0, p], corners[1, p])


def spectrum_columns(patch, forward, lowest):
    halves = dot(jnp.concatenate([patch, patch], axis=1), forward[...])
    cosine_part, sine_part = halves[:, :PS], halves[:, PS:]
    cosine_part = cosine_part - jnp.sum(cosine_part, axis=0, keepdims=True) * lowest[...]
    return cosine_part.astype(BF16), sine_part.astype(BF16)


def energy(real, imag):
    return jnp.sum(real * real + imag * imag, axis=0, keepdims=True)


def mean_square(energies):
    return jnp.sum(energies, axis=1, keepdims=True) * (1.0 / PS**4)


def own_kernel(
    patches, grid, corners, picture, forward, lowest, down, out, power_out, warped, order, bands, halves, sem
):
    write = pltpu.make_async_copy(picture, warped, sem)
    write.start()
    window_order(corners, order, patches, grid)
    for n in range(patches):
        p = order[n]
        bands[n] = window(picture, corners[0, p], corners[1, p])
    for p in range(patches):
        halves[p, :PS], halves[p, PS:] = spectrum_columns(bands[p], forward, lowest)
    for p in range(patches):
        both = dot(down[...], halves[p])
        out[p] = both
        power_out[pl.ds(p, 1), :] = energy(both[:PS], both[PS:])
    power_out[...] = jnp.broadcast_to(mean_square(power_out[...]), power_out.shape)
    write.wait()


def match_kernel(
    share, order, previous, spectra, powers, forward, lowest, down, back, *rest
):
    out, halves, crosses, mixed, scales, done, slots, sems, slots_sem = rest[-9:]
    fetch = pltpu.make_async_copy(order, slots, slots_sem)
    fetch.start()
    pairs = [share[start : start + 2] for start in range(0, len(share), 2)]
    for n in range(len(share)):
        at = pl.ds(n % 2 * PS, PS)
        halves[n // 2, :PS, at], halves[n // 2, PS:, at] = spectrum_columns(previous[n], forward, lowest)
    for q, pair in enumerate(pairs):
        width = PS * len(pair)
        second = dot(down[...], halves[q, :, :width])
        for n, p in enumerate(pair):
            one_real, one_imag = spectra[p, :PS, :], spectra[p, PS:, :]
            two_real, two_imag = second[:PS, n * PS : (n + 1) * PS], second[PS:, n * PS : (n + 1) * PS]
            scales[pl.ds(2 * q + n, 1), :] = energy(two_real, two_imag)
            real = one_real * two_real + one_imag * two_imag
            imag = one_real * two_imag - one_imag * two_real
            crosses[q, :PS, pl.ds(n * PS, PS)] = real.astype(BF16)
            crosses[q, PS:, pl.ds(n * PS, PS)] = imag.astype(BF16)
    for q, pair in enumerate(pairs):
        width = PS * len(pair)
        both = dot(down[...], crosses[q, :, :width]).astype(BF16)
        for n, p in enumerate(pair):
            mixed[2 * q + n, :, :PS] = both[:PS, n * PS : (n + 1) * PS]
            mixed[2 * q + n, :, PS:] = both[PS:, n * PS : (n + 1) * PS]
    product = (powers[pl.ds(share[0], len(share)), :] + EPSILON) * (mean_square(scales[...]) + EPSILON)
    scales[...] = lax.rsqrt(product) * (1.0 / (PS * PS * PS))
    fetch.wait()
    writes = []
    for n, p in enumerate(share):
        done[n] = dot(mixed[n], back[...]) * scales[pl.ds(n, 1), :]
        writes.append(pltpu.make_async_copy(done.at[n], out.at[slots[p]], sems.at[n]))
        writes[-1].start()
    for write in writes:
        write.wait()


def params(megabytes, flops, moved):
    return dict(
        compiler_params=pltpu.CompilerParams(vmem_limit_bytes=megabytes << 20),
        cost_estimate=pl.CostEstimate(flops=flops, bytes_accessed=moved, transcendentals=0),
    )


def shards(source, pull_ids, interp_idx, interp_table, patch_pos):
    blocks = source[0]
    count = blocks.shape[0]
    grid = int(round(count**0.5))
    patches = patch_pos.shape[1]
    side = grid * BS
    ids = pull_ids.transpose(2, 0, 1)
    mats = interp_idx[0].transpose(1, 2, 0)
    positions = patch_pos[0].T
    shares = range((patches + 1) // 2), range((patches + 1) // 2, patches)
    sections = lax.axis_size("sec")
    tiles = lax.axis_size("tile")
    other = lax.ppermute(blocks, "tile", [(i, (i + 1) % tiles) for i in range(tiles)])
    gate = pl.pallas_call(
        gate_kernel,
        out_shape=jax.ShapeDtypeStruct((8, 128), F32),
        out_specs=VMEM,
        **params(16, 2 << 30, 16 << 20),
    )()
    gate, asked = lax.optimization_barrier((gate, positions))
    wanted = lax.ppermute(asked, "sec", [(i + 1, i) for i in range(sections - 1)])
    forward, lowest, down, back = tables()

    onward = [(i, i + 1) for i in range(sections - 1)]

    def warp_and_cut(kernel, share, blocks_made, shape, last):
        return pl.pallas_call(
            functools.partial(kernel, count, grid, patches),
            out_shape=(
                jax.ShapeDtypeStruct(shape, BF16),
                jax.ShapeDtypeStruct((len(share), PS, PS), BF16),
            ),
            in_specs=[SMEM] * 3 + [VMEM] * 3 + [ANY if kernel is early_kernel else VMEM],
            out_specs=(VMEM, VMEM),
            scratch_shapes=[pltpu.SMEM((patches,), jnp.int32)],
            **params(16, blocks_made * KP * 4 * BS**3, blocks_made * (KP + 1) * BS * BS * 2),
        )(ids, mats, wanted, blocks, other, interp_table, last)

    rows = early_rows(grid)
    early, sent = warp_and_cut(early_kernel, shares[0], rows * grid, (rows * BS, side), gate)
    arrivals = [lax.ppermute(sent, "sec", onward)]
    picture, sent = warp_and_cut(late_kernel, shares[1], (grid - rows) * grid, (side, side), early)
    arrivals.append(lax.ppermute(sent, "sec", onward))

    spectra, powers, warped, order = pl.pallas_call(
        functools.partial(own_kernel, patches, grid),
        out_shape=(
            jax.ShapeDtypeStruct((patches, 2 * PS, PS), F32),
            jax.ShapeDtypeStruct((patches, PS), F32),
            jax.ShapeDtypeStruct((side, side), BF16),
            jax.ShapeDtypeStruct((patches,), jnp.int32),
        ),
        in_specs=[SMEM] + [VMEM] * 4,
        out_specs=(VMEM, VMEM, ANY, SMEM),
        scratch_shapes=[
            pltpu.VMEM((patches, PS, PS), BF16),
            pltpu.VMEM((patches, 2 * PS, PS), BF16),
            pltpu.SemaphoreType.DMA,
        ],
        **params(20, patches * 12 * PS**3, side * side * 2),
    )(positions, picture, forward, lowest, down)

    correlations = ()
    for share, previous in zip(shares, arrivals):
        size = len(share)
        correlations = (
            pl.pallas_call(
                functools.partial(match_kernel, share),
                out_shape=jax.ShapeDtypeStruct((patches, PS, PS), F32),
                in_specs=[ANY] + [VMEM] * 7 + [ANY] * len(correlations),
                out_specs=ANY,
                scratch_shapes=[
                    pltpu.VMEM(((size + 1) // 2, 2 * PS, 2 * PS), BF16),
                    pltpu.VMEM(((size + 1) // 2, 2 * PS, 2 * PS), BF16),
                    pltpu.VMEM((size, PS, 2 * PS), BF16),
                    pltpu.VMEM((size, PS), F32),
                    pltpu.VMEM((size, PS, PS), F32),
                    pltpu.SMEM((patches,), jnp.int32),
                    pltpu.SemaphoreType.DMA((size,)),
                    pltpu.SemaphoreType.DMA,
                ],
                input_output_aliases={8: 0} if correlations else {},
                **params(16, size * 16 * PS**3, size * PS * PS * 14),
            )(order, previous, spectra, powers, forward, lowest, down, back, *correlations),
        )
    (correlations,) = correlations
    return warped[None], correlations[None]


def solution(mesh):
    return jax.shard_map(
        shards,
        mesh=mesh,
        in_specs=(
            P(("parts", "sec"), "tile", None, None),
            P(("parts", "sec"), "tile", None),
            P(("parts", "sec"), "tile", None, None),
            P(),
            P(("parts", "sec"), "tile", None),
        ),
        out_specs=(P(("parts", "sec"), "tile", None), P(("parts", "sec"), "tile", None, None)),
        check_vma=False,
    )
```

time: 39.1 us -> 37.9 us (0.969)
  waiting for transfers between devices: 8.32 us -> 6.98 us
    ppermute x1, waiting for transfers between devices: 6.04 us -> 0.03 us  [shards(): arrivals = [lax.ppermute(sent, 'sec', onward)]]
    ppermute x1, waiting for transfers between devices: 2.28 us -> 4.8 us  [shards(): arrivals.append(lax.ppermute(sent, 'sec', onward))]
    ppermute x1, waiting for transfers between devices: 0.01 us -> 2.14 us  [shards(): lax.ppermute(asked, 'sec', [(i + 1, i) for i in range(sections - 1)])]
    ppermute x1, starting transfers between devices: 2.64 us -> 4.33 us  [shards(): arrivals = [lax.ppermute(sent, 'sec', onward)]]
    ppermute x1, starting transfers between devices: 4.52 us -> 2.85 us  [shards(): arrivals.append(lax.ppermute(sent, 'sec', onward))]
    pallas_call x4 -> x3, Pallas kernels: 13.5 us -> 13.3 us  [the longest x2 9.34 us: warp_and_cut(): pl.pallas_call(functools.partial(kernel, count, grid, patches), out_shape...]
  transfers between devices with their start and end apart: 4 -> 4, of which waited for: 2 -> 2; matrix products, arithmetic and copies ran while one was open for 0% -> 0% of each run, Pallas kernels for 29% -> 28%
where the time goes in v5:
time: 37.9 us; the launch traced here: 37.6 us
  Pallas kernels  18.3 us (48%)
  starting transfers between devices  10.8 us (28%)
  waiting for transfers between devices  6.98 us (18%)
  between operations  0.97 us (3%)
  local copies, waits for them, and re-layouts  0.59 us (2%)
    pallas_call x2, Pallas kernels, warp_and_cut(): pl.pallas_call(functools.partial(kernel, count, grid, patches), out_shape...  9.34 us
    pallas_call x2, Pallas kernels, shards(): pl.pallas_call(functools.partial(match_kernel, share), out_shape=jax.Shap...  4.97 us
    ppermute x1, waiting for transfers between devices, shards(): arrivals.append(lax.ppermute(sent, 'sec', onward))  4.8 us
    ppermute x1, starting transfers between devices, shards(): arrivals = [lax.ppermute(sent, 'sec', onward)]  4.33 us
    pallas_call x1, Pallas kernels, shards(): pl.pallas_call(functools.partial(own_kernel, patches, grid), out_shape=(j...  3.98 us
    ppermute x1, starting transfers between devices, shards(): lax.ppermute(asked, 'sec', [(i + 1, i) for i in range(sections - 1)])  3.56 us
    ppermute x1, starting transfers between devices, shards(): arrivals.append(lax.ppermute(sent, 'sec', onward))  2.85 us
    ppermute x1, waiting for transfers between devices, shards(): lax.ppermute(asked, 'sec', [(i + 1, i) for i in range(sections - 1)])  2.14 us
  transfers between devices with their start and end apart: 4, of which 2 were waited for; matrix products, arithmetic and copies ran while one was open for 0% of the time, Pallas kernels for 28%

profile of v5, /device:TPU:10, one launch (start us, length us, event | category | flops | bytes accessed | tf_op | source)
XLA Modules:
  0.0 37.6 jit_solution(1536736844653648148)
XLA Ops:
  0.6 0.0 copy-start.8
  0.6 0.0 copy-start
  0.7 0.0 copy-start.1
  0.7 0.0 copy-start.6
  0.7 0.1 collective-permute-start.1
  0.8 0.5 %copy-done.8 = s32[1,25,2]{1,2,0:T(2,128)S(1)} copy-done((s32[1,25,2]{1,2,0:T(2,128)S(1)}, s32[1,25,2]{1,2,0:T(2,128)}, u32[]{:S(2)}) %copy-start.8) | copy-done | bytes 224
  1.3 3.6 %collective-permute-start = (s32[2,25]{1,0:T(2,128)S(1)}, s32[2,25]{1,0:T(2,128)S(1)}, u32[]{:S(2)}, u32[]{:S(2)}) collective-permute-start(s32[2,25]{1,0:T(2,128)S(1)} %bitcast.17), channel_id=1, source_target_pairs={{2,0},{4,2},{6,4},{8,6},{10,8},{12,10},{14,12},{3,1},{5,3},{7,5},{... | collective-permute-start | bytes 608 | tf_op jit(solution)/shard_map/ppermute | solution.py:238
  4.9 2.1 %collective-permute-done.corners = s32[2,25]{1,0:T(2,128)S(1)} collective-permute-done((s32[2,25]{1,0:T(2,128)S(1)}, s32[2,25]{1,0:T(2,128)S(1)}, u32[]{:S(2)}, u32[]{:S(2)}) %collective-permute-start) | collective-permute-done | bytes 232 | tf_op jit(solution)/shard_map/ppermute | solution.py:238
  7.0 0.0 collective-permute-done.1.other
  7.0 0.0 copy-done.6
  7.0 0.0 copy-done.7
  7.1 5.2 %shard_map.105 = (bf16[768,1280]{1,0:T(8,128)(2,1)S(1)}, bf16[13,128,128]{2,1,0:T(8,128)(2,1)S(1)}) custom-call(s32[3,1,25]{2,1,0:T(1,128)S(1)} %bitcast.15, s32[3,2,25]{2,1,0:T(2,128)S(1)} %bitcast.13, s32[2,25]{1,0:T(2,128)S(1)} %collective-permute-done.corners, bf16[25,256,256]{2,1,0:T(8,128)(2,1)S(1)} %bitcast.11, ...), custom_call_target="tpu_custom_call" | custom-call | flops 3019898880 | bytes 7864320 | tf_op jit(solution)/shard_map/pallas_call | solution.py:244
  12.2 4.3 %collective-permute-start.3 = (bf16[13,128,128]{2,1,0:T(8,128)(2,1)S(1)}, bf16[13,128,128]{2,1,0:T(8,128)(2,1)S(1)}, u32[]{:S(2)}, u32[]{:S(2)}) collective-permute-start(bf16[13,128,128]{2,1,0:T(8,128)(2,1)S(1)} %get-tuple-element.21), channel_id=1, source_target_pairs={{0,2},{2,4},{4,6},{6,8},{8,10},{10,12},{12,14},{1,3},{3,5},{5,7},{... | collective-permute-start | bytes 1277960 | tf_op jit(solution)/shard_map/ppermute | solution.py:258
  16.5 0.0 copy-start.2
  16.6 0.0 copy-start.3
  16.6 0.0 copy-start.5
  16.6 4.2 %shard_map.106 = (bf16[1280,1280]{1,0:T(8,128)(2,1)S(1)}, bf16[12,128,128]{2,1,0:T(8,128)(2,1)S(1)}) custom-call(s32[3,1,25]{2,1,0:T(1,128)S(1)} %bitcast.16, s32[3,2,25]{2,1,0:T(2,128)S(1)} %bitcast.14, s32[2,25]{1,0:T(2,128)S(1)} %collective-permute-done.corners, bf16[25,256,256]{2,1,0:T(8,128)(2,1)S(1)} %bitcast.12, ...), custom_call_target="tpu_custom_call" | custom-call | flops 2013265920 | bytes 5242880 | tf_op jit(solution)/shard_map/pallas_call | solution.py:244
  20.8 0.0 copy-start.4
  20.8 2.8 %collective-permute-start.2 = (bf16[12,128,128]{2,1,0:T(8,128)(2,1)S(1)}, bf16[12,128,128]{2,1,0:T(8,128)(2,1)S(1)}, u32[]{:S(2)}, u32[]{:S(2)}) collective-permute-start(bf16[12,128,128]{2,1,0:T(8,128)(2,1)S(1)} %get-tuple-element.18), channel_id=1, source_target_pairs={{0,2},{2,4},{4,6},{6,8},{8,10},{10,12},{12,14},{1,3},{3,5},{5,7},{... | collective-permute-start | bytes 1179656 | tf_op jit(solution)/shard_map/ppermute | solution.py:260
  23.7 4.0 %shard_map.107 = (f32[25,256,128]{2,1,0:T(8,128)S(1)}, f32[25,128]{1,0:T(8,128)S(1)}, bf16[1280,1280]{1,0:T(8,128)(2,1)}, s32[25]{0:T(128)S(1)}) custom-call(s32[2,25]{1,0:T(2,128)S(1)} %bitcast.18, bf16[1280,1280]{1,0:T(8,128)(2,1)S(1)} %get-tuple-element.15.picture, bf16[256,256]{1,0:T(8,128)(2,1)S(1)} %copy-done.3, f32[1,128]{1,0:T(1,128)S(1)} %copy-done.5, ...), custom_call_target="tpu_custom_call" | custom-call | flops 629145600 | bytes 3276800 | tf_op jit(solution)/shard_map/pallas_call | solution.py:262
  27.7 0.0 collective-permute-done.3.previous
  27.7 2.5 %shard_map.108.rest_0_ = f32[25,128,128]{2,1,0:T(8,128)} custom-call(s32[25]{0:T(128)S(1)} %get-tuple-element.17.order, bf16[13,128,128]{2,1,0:T(8,128)(2,1)S(1)} %collective-permute-done.3.previous, f32[25,256,128]{2,1,0:T(8,128)S(1)} %get-tuple-element.19.spectra, f32[25,128]{1,0:T(8,128)S(1)} %get-tuple-element.20.powers, bf16[256,256]{1,0:T(8,128)(2,1)S(1)} %copy-done.3, ...), custom_call_target="tpu_custom_call" | custom-call | flops 436207616 | bytes 2981888 | tf_op jit(solution)/shard_map/pallas_call | solution.py:284
  30.2 4.8 %collective-permute-done.2.previous = bf16[12,128,128]{2,1,0:T(8,128)(2,1)S(1)} collective-permute-done((bf16[12,128,128]{2,1,0:T(8,128)(2,1)S(1)}, bf16[12,128,128]{2,1,0:T(8,128)(2,1)S(1)}, u32[]{:S(2)}, u32[]{:S(2)}) %collective-permute-start.2) | collective-permute-done | bytes 393248 | tf_op jit(solution)/shard_map/ppermute | solution.py:260
  35.1 2.4 %shard_map.109 = f32[25,128,128]{2,1,0:T(8,128)} custom-call(s32[25]{0:T(128)S(1)} %get-tuple-element.17.order, bf16[12,128,128]{2,1,0:T(8,128)(2,1)S(1)} %collective-permute-done.2.previous, f32[25,256,128]{2,1,0:T(8,128)S(1)} %get-tuple-element.19.spectra, f32[25,128]{1,0:T(8,128)S(1)} %get-tuple-element.20.powers, ...), custom_call_target="tpu_custom_call", output_to_operand_aliasing={{}: (8, {})} | custom-call | flops 402653184 | bytes 2752512 | tf_op jit(solution)/shard_map/pallas_call | solution.py:284
  (8 shorter events, 0.0 us)
Async XLA Ops:
  0.6 0.7 %copy-start.8 = (s32[1,25,2]{1,2,0:T(2,128)S(1)}, s32[1,25,2]{1,2,0:T(2,128)}, u32[]{:S(2)}) copy-start(s32[1,25,2]{1,2,0:T(2,128)} %param.13) | copy-start | bytes 604
  0.6 6.4 %copy-start = (bf16[1,25,256,256]{3,2,1,0:T(8,128)(2,1)S(1)}, bf16[1,25,256,256]{3,2,1,0:T(8,128)(2,1)}, u32[]{:S(2)}) copy-start(bf16[1,25,256,256]{3,2,1,0:T(8,128)(2,1)} %param.9) | copy-start | bytes 9830404
  0.7 6.4 %copy-start.1 = (bf16[16,256,256]{2,1,0:T(8,128)(2,1)S(1)}, bf16[16,256,256]{2,1,0:T(8,128)(2,1)}, u32[]{:S(2)}) copy-start(bf16[16,256,256]{2,1,0:T(8,128)(2,1)} %table.3) | copy-start | bytes 6291460
  0.7 6.4 %copy-start.6 = (s32[1,25,3,2]{1,3,2,0:T(2,128)S(1)}, s32[1,25,3,2]{1,3,2,0:T(2,128)}, u32[]{:S(2)}) copy-start(s32[1,25,3,2]{1,3,2,0:T(2,128)} %param.11) | copy-start | bytes 1804
  0.7 6.4 %copy-start.7 = (s32[1,25,3]{1,0,2:T(1,128)S(1)}, s32[1,25,3]{1,0,2:T(1,128)}, u32[]{:S(2)}) copy-start(s32[1,25,3]{1,0,2:T(1,128)} %param.10) | copy-start | bytes 904
  0.7 6.3 %collective-permute-start.1 = (bf16[25,256,256]{2,1,0:T(8,128)(2,1)}, bf16[25,256,256]{2,1,0:T(8,128)(2,1)S(1)}, u32[]{:S(2)}, u32[]{:S(2)}) collective-permute-start(bf16[25,256,256]{2,1,0:T(8,128)(2,1)} %bitcast.10), channel_id=1, source_target_pairs={{0,1},{1,0},{2,3},{3,2},{4,5},{5,4},{6,7},{7,6},{8,9},{9,8},{10,11... | collective-permute-start | bytes 9830408 | tf_op jit(solution)/shard_map/ppermute | solution.py:230
  1.3 5.7 %collective-permute-start = (s32[2,25]{1,0:T(2,128)S(1)}, s32[2,25]{1,0:T(2,128)S(1)}, u32[]{:S(2)}, u32[]{:S(2)}) collective-permute-start(s32[2,25]{1,0:T(2,128)S(1)} %bitcast.17), channel_id=1, source_target_pairs={{2,0},{4,2},{6,4},{8,6},{10,8},{12,10},{14,12},{3,1},{5,3},{7,5},{... | collective-permute-start | bytes 608 | tf_op jit(solution)/shard_map/ppermute | solution.py:238
  12.2 15.5 %collective-permute-start.3 = (bf16[13,128,128]{2,1,0:T(8,128)(2,1)S(1)}, bf16[13,128,128]{2,1,0:T(8,128)(2,1)S(1)}, u32[]{:S(2)}, u32[]{:S(2)}) collective-permute-start(bf16[13,128,128]{2,1,0:T(8,128)(2,1)S(1)} %get-tuple-element.21), channel_id=1, source_target_pairs={{0,2},{2,4},{4,6},{6,8},{8,10},{10,12},{12,14},{1,3},{3,5},{5,7},{... | collective-permute-start | bytes 1277960 | tf_op jit(solution)/shard_map/ppermute | solution.py:258
  16.5 7.1 %copy-start.2 = (bf16[256,256]{1,0:T(8,128)(2,1)S(1)}, bf16[256,256]{1,0:T(8,128)(2,1)}, u32[]{:S(2)}) copy-start(bf16[256,256]{1,0:T(8,128)(2,1)} %constant.10.clone.down) | copy-start | bytes 393220
  16.6 7.1 %copy-start.3 = (bf16[256,256]{1,0:T(8,128)(2,1)S(1)}, bf16[256,256]{1,0:T(8,128)(2,1)}, u32[]{:S(2)}) copy-start(bf16[256,256]{1,0:T(8,128)(2,1)} %constant.8.clone.forward) | copy-start | bytes 393220
  16.6 7.1 %copy-start.5 = (f32[1,128]{1,0:T(1,128)S(1)}, f32[1,128]{1,0:T(1,128)}, u32[]{:S(2)}) copy-start(f32[1,128]{1,0:T(1,128)} %constant.9.clone.lowest) | copy-start | bytes 1540
  20.8 6.9 %copy-start.4 = (bf16[256,128]{1,0:T(8,128)(2,1)S(1)}, bf16[256,128]{1,0:T(8,128)(2,1)}, u32[]{:S(2)}) copy-start(bf16[256,128]{1,0:T(8,128)(2,1)} %constant.11.clone.back) | copy-start | bytes 196612
  20.8 14.3 %collective-permute-start.2 = (bf16[12,128,128]{2,1,0:T(8,128)(2,1)S(1)}, bf16[12,128,128]{2,1,0:T(8,128)(2,1)S(1)}, u32[]{:S(2)}, u32[]{:S(2)}) collective-permute-start(bf16[12,128,128]{2,1,0:T(8,128)(2,1)S(1)} %get-tuple-element.18), channel_id=1, source_target_pairs={{0,2},{2,4},{4,6},{6,8},{8,10},{10,12},{12,14},{1,3},{3,5},{5,7},{... | collective-permute-start | bytes 1179656 | tf_op jit(solution)/shard_map/ppermute | solution.py:260

commit v6 on v5

--- a/solution.py
+++ b/solution.py
@@ -12,6 +12,8 @@
 BS = 256
 PS = 128
 KP = 3
+CAP = 12
+LISTED = CAP + 1
 EPSILON = 1e-06
 ROWS = PS + 16
 COLS = 2 * PS
@@ -73,66 +75,104 @@
     return down
 
 
-def warp_block(block, low, count, ids, mats, source, other, table):
-    total = None
-    for k in range(KP):
-        local = ids[k, 0, block] - low
-        here = (local >= 0) & (local < count)
-        away = jnp.where(local < 0, local + count, local - count)
-        pulled = jnp.where(here, source[jnp.where(here, local, 0)], other[jnp.where(here, 0, away)])
-        left = dot(table[mats[k, 0, block]], pulled).astype(BF16)
-        term = lax.dot_general(
-            left, table[mats[k, 1, block]], (((1,), (1,)), ((), ())), preferred_element_type=F32
-        )
-        total = term if total is None else total + term
-    return total.astype(BF16)
-
-
-def window(picture, y, x):
-    top = pl.multiple_of(jnp.minimum(y // 16 * 16, picture.shape[0] - ROWS), 16)
-    left = pl.multiple_of(jnp.minimum(x // PS * PS, picture.shape[1] - COLS), PS)
-    area = picture[pl.ds(top, ROWS), pl.ds(left, COLS)]
+def near_kernel(count, grid, ids, mats, source, table, gate, lefts, plan):
+    low = lax.axis_index("tile") * count
+    pulls = count * KP
+    for r in range(2 * LISTED):
+        plan[pulls + r] = 0
+    found = jnp.int32(0)
+    for block in range(count):
+        for k in range(KP):
+            local = ids[k, 0, block] - low
+            here = (local >= 0) & (local < count)
+            plan[block * KP + k] = jnp.where(here, -1, found)
+            slot = jnp.minimum(found, CAP)
+            plan[pulls + slot] = jnp.where(here, 0, jnp.where(local < 0, local + count, local - count))
+            plan[pulls + LISTED + slot] = mats[k, 0, block]
+            found = found + jnp.where(here, 0, 1)
+            if grid <= block < count - grid:
+                left = dot(table[mats[k, 0, block]], source[jnp.where(here, local, 0)])
+                lefts[(block - grid) * KP + k] = left.astype(BF16)
+
+
+def warp_row(row, inner, low, grid, ids, mats, source, table, plan, lefts, others):
+    blocks = []
+    for column in range(grid):
+        block = row * grid + column
+        total = None
+        for k in range(KP):
+            slot = plan[block * KP + k]
+            if inner:
+                near = lefts[(block - grid) * KP + k]
+            else:
+                local = jnp.where(slot < 0, ids[k, 0, block] - low, 0)
+                near = dot(table[mats[k, 0, block]], source[local]).astype(BF16)
+            left = jnp.where(slot < 0, near, others[jnp.maximum(slot, 0)])
+            term = lax.dot_general(
+                left, table[mats[k, 1, block]], (((1,), (1,)), ((), ())), preferred_element_type=F32
+            )
+            total = term if total is None else total + term
+        blocks.append(total.astype(BF16))
+    return blocks
+
+
+def cut_windows(picture, corners, wanted, above, bands, out):
     i = lax.broadcasted_iota(jnp.int32, (PS, ROWS), 0)
     r = lax.broadcasted_iota(jnp.int32, (PS, ROWS), 1)
-    pick_rows = (r - i == y - top).astype(F32).astype(BF16)
     c = lax.broadcasted_iota(jnp.int32, (COLS, PS), 0)
     j = lax.broadcasted_iota(jnp.int32, (COLS, PS), 1)
-    pick_cols = (c - j == x - left).astype(F32).astype(BF16)
-    return dot(dot(pick_rows, area).astype(BF16), pick_cols).astype(BF16)
+    rests = []
+    for n, p in enumerate(wanted):
+        y, x = corners[0, p] - above, corners[1, p]
+        top = pl.multiple_of(jnp.minimum(y // 16 * 16, picture.shape[0] - ROWS), 16)
+        left = pl.multiple_of(jnp.minimum(x // PS * PS, picture.shape[1] - COLS), PS)
+        pick_rows = (r - i == y - top).astype(F32).astype(BF16)
+        bands[n] = dot(pick_rows, picture[pl.ds(top, ROWS), pl.ds(left, COLS)]).astype(BF16)
+        rests.append(x - left)
+    for n, rest in enumerate(rests):
+        pick_cols = (c - j == rest).astype(F32).astype(BF16)
+        out[n] = dot(bands[n], pick_cols).astype(BF16)
+
+
+def fill_row(picture, row, blocks):
+    for column, block in enumerate(blocks):
+        picture[pl.ds(pl.multiple_of(row * BS, BS), BS), pl.ds(column * BS, BS)] = block
 
 
 def early_kernel(
-    count, grid, patches, ids, mats, corners, source, other, table, gate, early, out, order
+    grid, patches, plan, ids, mats, corners, source, other, table, lefts, early, others, out, order, bands
 ):
-    low = lax.axis_index("tile") * count
+    pulls = grid * grid * KP
+    low = lax.axis_index("tile") * grid * grid
+    for r in range(CAP):
+        left = dot(table[plan[pulls + LISTED + r]], other[plan[pulls + r]])
+        others[r] = left.astype(BF16)
     down = window_order(corners, order, patches, grid)
-    for n in range(early_rows(grid) * grid):
-        block = down * grid + n
-        at = pl.ds(n // grid * BS, BS), pl.ds(n % grid * BS, BS)
-        early[at] = warp_block(block, low, count, ids, mats, source, other, table)
-    for n in range(out.shape[0]):
-        p = order[n]
-        out[n] = window(early, corners[0, p] - down * BS, corners[1, p])
+    above = jnp.where(down == 0, 1, 0)
+    given = ids, mats, source, table, plan, lefts, others
+    for n in range(early_rows(grid) - 1):
+        fill_row(early, n + above, warp_row(down + n + above, True, low, grid, *given))
+    outer = jnp.where(down == 0, 0, grid - 1)
+    fill_row(early, outer - down, warp_row(outer, False, low, grid, *given))
+    cut_windows(early, corners, [order[n] for n in range(out.shape[0])], down * BS, bands, out)
 
 
 def late_kernel(
-    count, grid, patches, ids, mats, corners, source, other, table, early, picture, out, order
+    grid, patches, plan, ids, mats, corners, source, table, lefts, others, early, picture, out, order, bands
 ):
-    low = lax.axis_index("tile") * count
     rows = early_rows(grid)
+    low = lax.axis_index("tile") * grid * grid
     down = window_order(corners, order, patches, grid)
+    given = ids, mats, source, table, plan, lefts, others
     for n in range(rows):
         picture[pl.ds(pl.multiple_of((down + n) * BS, BS), BS), :] = early[pl.ds(n * BS, BS), :]
-    after = lax.rem(down + rows, grid)
-    for n in range((grid - rows) * grid):
-        row = pl.multiple_of((after + n // grid) * BS, BS)
-        block = after * grid + n
-        picture[pl.ds(row, BS), pl.ds(n % grid * BS, BS)] = warp_block(
-            block, low, count, ids, mats, source, other, table
-        )
-    for n in range(out.shape[0]):
-        p = order[patches - out.shape[0] + n]
-        out[n] = window(picture, corners[0, p], corners[1, p])
+    for n in range(grid - rows - 1):
+        row = jnp.where(down == 0, rows + n, 1 + n)
+        fill_row(picture, row, warp_row(row, True, low, grid, *given))
+    outer = jnp.where(down == 0, grid - 1, 0)
+    fill_row(picture, outer, warp_row(outer, False, low, grid, *given))
+    wanted = [order[n] for n in range(patches - out.shape[0], patches)]
+    cut_windows(picture, corners, wanted, 0, bands, out)
 
 
 def spectrum_columns(patch, forward, lowest):
@@ -151,14 +191,12 @@
 
 
 def own_kernel(
-    patches, grid, corners, picture, forward, lowest, down, out, power_out, warped, order, bands, halves, sem
+    patches, grid, corners, picture, forward, lowest, down, out, power_out, warped, order, rows, bands, halves, sem
 ):
     write = pltpu.make_async_copy(picture, warped, sem)
     write.start()
     window_order(corners, order, patches, grid)
-    for n in range(patches):
-        p = order[n]
-        bands[n] = window(picture, corners[0, p], corners[1, p])
+    cut_windows(picture, corners, [order[n] for n in range(patches)], 0, rows, bands)
     for p in range(patches):
         halves[p, :PS], halves[p, PS:] = spectrum_columns(bands[p], forward, lowest)
     for p in range(patches):
@@ -190,14 +228,14 @@
             imag = one_real * two_imag - one_imag * two_real
             crosses[q, :PS, pl.ds(n * PS, PS)] = real.astype(BF16)
             crosses[q, PS:, pl.ds(n * PS, PS)] = imag.astype(BF16)
+    product = (powers[pl.ds(share[0], len(share)), :] + EPSILON) * (mean_square(scales[...]) + EPSILON)
+    scales[...] = lax.rsqrt(product) * (1.0 / (PS * PS * PS))
     for q, pair in enumerate(pairs):
         width = PS * len(pair)
         both = dot(down[...], crosses[q, :, :width]).astype(BF16)
         for n, p in enumerate(pair):
             mixed[2 * q + n, :, :PS] = both[:PS, n * PS : (n + 1) * PS]
             mixed[2 * q + n, :, PS:] = both[PS:, n * PS : (n + 1) * PS]
-    product = (powers[pl.ds(share[0], len(share)), :] + EPSILON) * (mean_square(scales[...]) + EPSILON)
-    scales[...] = lax.rsqrt(product) * (1.0 / (PS * PS * PS))
     fetch.wait()
     writes = []
     for n, p in enumerate(share):
@@ -240,23 +278,44 @@
 
     onward = [(i, i + 1) for i in range(sections - 1)]
 
-    def warp_and_cut(kernel, share, blocks_made, shape, last):
-        return pl.pallas_call(
-            functools.partial(kernel, count, grid, patches),
-            out_shape=(
-                jax.ShapeDtypeStruct(shape, BF16),
-                jax.ShapeDtypeStruct((len(share), PS, PS), BF16),
-            ),
-            in_specs=[SMEM] * 3 + [VMEM] * 3 + [ANY if kernel is early_kernel else VMEM],
-            out_specs=(VMEM, VMEM),
-            scratch_shapes=[pltpu.SMEM((patches,), jnp.int32)],
-            **params(16, blocks_made * KP * 4 * BS**3, blocks_made * (KP + 1) * BS * BS * 2),
-        )(ids, mats, wanted, blocks, other, interp_table, last)
+    pulls = count * KP
+    inner = pulls - 2 * grid * KP
+    lefts, plan = pl.pallas_call(
+        functools.partial(near_kernel, count, grid),
+        out_shape=(
+            jax.ShapeDtypeStruct((inner, BS, BS), BF16),
+            jax.ShapeDtypeStruct((pulls + 2 * LISTED,), jnp.int32),
+        ),
+        in_specs=[SMEM, SMEM, VMEM, VMEM, ANY],
+        out_specs=(VMEM, SMEM),
+        **params(16, inner * 2 * BS**3, (count + inner) * BS * BS * 2),
+    )(ids, mats, blocks, interp_table, gate)
 
     rows = early_rows(grid)
-    early, sent = warp_and_cut(early_kernel, shares[0], rows * grid, (rows * BS, side), gate)
+    early, others, sent = pl.pallas_call(
+        functools.partial(early_kernel, grid, patches),
+        out_shape=(
+            jax.ShapeDtypeStruct((rows * BS, side), BF16),
+            jax.ShapeDtypeStruct((CAP, BS, BS), BF16),
+            jax.ShapeDtypeStruct((len(shares[0]), PS, PS), BF16),
+        ),
+        in_specs=[SMEM] * 4 + [VMEM] * 4,
+        out_specs=[VMEM] * 3,
+        scratch_shapes=[pltpu.SMEM((patches,), jnp.int32), pltpu.VMEM((len(shares[0]), PS, COLS), BF16)],
+        **params(16, rows * grid * KP * 2 * BS**3, rows * grid * KP * BS * BS * 4),
+    )(plan, ids, mats, wanted, blocks, other, interp_table, lefts)
     arrivals = [lax.ppermute(sent, "sec", onward)]
-    picture, sent = warp_and_cut(late_kernel, shares[1], (grid - rows) * grid, (side, side), early)
+    picture, sent = pl.pallas_call(
+        functools.partial(late_kernel, grid, patches),
+        out_shape=(
+            jax.ShapeDtypeStruct((side, side), BF16),
+            jax.ShapeDtypeStruct((len(shares[1]), PS, PS), BF16),
+        ),
+        in_specs=[SMEM] * 4 + [VMEM] * 5,
+        out_specs=[VMEM] * 2,
+        scratch_shapes=[pltpu.SMEM((patches,), jnp.int32), pltpu.VMEM((len(shares[0]), PS, COLS), BF16)],
+        **params(16, (grid - rows) * grid * KP * 2 * BS**3, side * side * 4),
+    )(plan, ids, mats, wanted, blocks, interp_table, lefts, others, early)
     arrivals.append(lax.ppermute(sent, "sec", onward))
 
     spectra, powers, warped, order = pl.pallas_call(
@@ -270,6 +329,7 @@
         in_specs=[SMEM] + [VMEM] * 4,
         out_specs=(VMEM, VMEM, ANY, SMEM),
         scratch_shapes=[
+            pltpu.VMEM((patches, PS, COLS), BF16),
             pltpu.VMEM((patches, PS, PS), BF16),
             pltpu.VMEM((patches, 2 * PS, PS), BF16),
             pltpu.SemaphoreType.DMA,

time: 37.9 us -> 37.7 us (level)
  waiting for transfers between devices: 6.98 us -> 5.69 us
  Pallas kernels: 18.3 us -> 19.3 us
    ppermute x1, waiting for transfers between devices: 2.14 us -> 0.01 us  [shards(): lax.ppermute(asked, 'sec', [(i + 1, i) for i in range(sections - 1)])]
    pallas_call x2 -> x3, Pallas kernels: 9.34 us -> 10.6 us  [the longest x1 4.38 us: shards(): pl.pallas_call(functools.partial(early_kernel, grid, patches), out_shape=...]
    ppermute x1, waiting for transfers between devices: 0.03 us -> 1.13 us  [shards(): arrivals = [lax.ppermute(sent, 'sec', onward)]]
    ppermute x1, starting transfers between devices: 2.85 us -> 3.66 us  [shards(): arrivals.append(lax.ppermute(sent, 'sec', onward))]
    ppermute x1, starting transfers between devices: 4.33 us -> 3.52 us  [shards(): arrivals = [lax.ppermute(sent, 'sec', onward)]]
  transfers between devices with their start and end apart: 4 -> 4, of which waited for: 2 -> 2; matrix products, arithmetic and copies ran while one was open for 0% -> 0% of each run, Pallas kernels for 28% -> 33%
where the time goes in v6:
time: 37.7 us; the launch traced here: 37.4 us
  Pallas kernels  19.3 us (51%)
  starting transfers between devices  10.8 us (29%)
  waiting for transfers between devices  5.69 us (15%)
  between operations  1.01 us (3%)
  local copies, waits for them, and re-layouts  0.59 us (2%)
    pallas_call x2, Pallas kernels, shards(): pl.pallas_call(functools.partial(match_kernel, share), out_shape=jax.Shap...  4.96 us
    ppermute x1, waiting for transfers between devices, shards(): arrivals.append(lax.ppermute(sent, 'sec', onward))  4.55 us
    pallas_call x1, Pallas kernels, shards(): pl.pallas_call(functools.partial(early_kernel, grid, patches), out_shape=...  4.38 us
    pallas_call x1, Pallas kernels, shards(): pl.pallas_call(functools.partial(own_kernel, patches, grid), out_shape=(j...  3.75 us
    ppermute x1, starting transfers between devices, shards(): arrivals.append(lax.ppermute(sent, 'sec', onward))  3.66 us
    ppermute x1, starting transfers between devices, shards(): lax.ppermute(asked, 'sec', [(i + 1, i) for i in range(sections - 1)])  3.56 us
    ppermute x1, starting transfers between devices, shards(): arrivals = [lax.ppermute(sent, 'sec', onward)]  3.52 us
    pallas_call x1, Pallas kernels, shards(): pl.pallas_call(functools.partial(late_kernel, grid, patches), out_shape=(...  3.36 us
  transfers between devices with their start and end apart: 4, of which 2 were waited for; matrix products, arithmetic and copies ran while one was open for 0% of the time, Pallas kernels for 33%

profile of v6, /device:TPU:10, one launch (start us, length us, event | category | flops | bytes accessed | tf_op | source)
XLA Modules:
  0.0 37.4 jit_solution(9036355932811739985)
XLA Ops:
  0.6 0.0 copy-start.8
  0.6 0.0 copy-start
  0.7 0.1 collective-permute-start.1
  0.8 0.5 %copy-done.8 = s32[1,25,2]{1,2,0:T(2,128)S(1)} copy-done((s32[1,25,2]{1,2,0:T(2,128)S(1)}, s32[1,25,2]{1,2,0:T(2,128)}, u32[]{:S(2)}) %copy-start.8) | copy-done | bytes 224
  1.3 3.6 %collective-permute-start = (s32[2,25]{1,0:T(2,128)S(1)}, s32[2,25]{1,0:T(2,128)S(1)}, u32[]{:S(2)}, u32[]{:S(2)}) collective-permute-start(s32[2,25]{1,0:T(2,128)S(1)} %bitcast.20), channel_id=1, source_target_pairs={{2,0},{4,2},{6,4},{8,6},{10,8},{12,10},{14,12},{3,1},{5,3},{7,5},{... | collective-permute-start | bytes 608 | tf_op jit(solution)/shard_map/ppermute | solution.py:276
  4.9 2.9 %shard_map.105 = (bf16[45,256,256]{2,1,0:T(8,128)(2,1)S(1)}, s32[101]{0:T(128)S(1)}) custom-call(s32[3,1,25]{2,1,0:T(1,128)S(1)} %bitcast.17, s32[3,2,25]{2,1,0:T(2,128)S(1)} %bitcast.14, bf16[25,256,256]{2,1,0:T(8,128)(2,1)S(1)} %bitcast.11, bf16[16,256,256]{2,1,0:T(8,128)(2,1)S(1)} %copy-done.1, f32[8,128]{1,0:T(8,128)S(1)} %shard_map.104.gate), custom_call_target="tpu_custom_call" | custom-call | flops 1509949440 | bytes 9175040 | tf_op jit(solution)/shard_map/pallas_call | solution.py:283
  7.8 0.0 collective-permute-done.corners
  7.8 0.0 collective-permute-done.1.other
  7.8 4.4 %shard_map.106 = (bf16[768,1280]{1,0:T(8,128)(2,1)S(1)}, bf16[12,256,256]{2,1,0:T(8,128)(2,1)S(1)}, bf16[13,128,128]{2,1,0:T(8,128)(2,1)S(1)}) custom-call(s32[101]{0:T(128)S(1)} %get-tuple-element.16.plan, s32[3,1,25]{2,1,0:T(1,128)S(1)} %bitcast.18, s32[3,2,25]{2,1,0:T(2,128)S(1)} %bitcast.15, s32[2,25]{1,0:T(2,128)S(1)} %collective-permute-done.corners, ...), custom_call_target="tpu_custom_call" | custom-call | flops 1509949440 | bytes 11796480 | tf_op jit(solution)/shard_map/pallas_call | solution.py:295
  12.2 3.5 %collective-permute-start.3 = (bf16[13,128,128]{2,1,0:T(8,128)(2,1)S(1)}, bf16[13,128,128]{2,1,0:T(8,128)(2,1)S(1)}, u32[]{:S(2)}, u32[]{:S(2)}) collective-permute-start(bf16[13,128,128]{2,1,0:T(8,128)(2,1)S(1)} %get-tuple-element.27), channel_id=1, source_target_pairs={{0,2},{2,4},{4,6},{6,8},{8,10},{10,12},{12,14},{1,3},{3,5},{5,7},{... | collective-permute-start | bytes 1277960 | tf_op jit(solution)/shard_map/ppermute | solution.py:307
  15.7 0.0 copy-start.2
  15.8 0.0 copy-start.3
  15.8 0.0 copy-start.7
  15.8 3.4 %shard_map.107 = (bf16[1280,1280]{1,0:T(8,128)(2,1)S(1)}, bf16[12,128,128]{2,1,0:T(8,128)(2,1)S(1)}) custom-call(s32[101]{0:T(128)S(1)} %get-tuple-element.16.plan, s32[3,1,25]{2,1,0:T(1,128)S(1)} %bitcast.19, s32[3,2,25]{2,1,0:T(2,128)S(1)} %bitcast.16, s32[2,25]{1,0:T(2,128)S(1)} %collective-permute-done.corners, bf16[25,256,256]{2,1,0:T(8,128)(2,1)S(1)} %bitcast.13, ...), custom_call_target="tpu_custom_call" | custom-call | flops 1006632960 | bytes 6553600 | tf_op jit(solution)/shard_map/pallas_call | solution.py:308
  19.1 0.0 copy-start.4
  19.2 3.7 %collective-permute-start.2 = (bf16[12,128,128]{2,1,0:T(8,128)(2,1)S(1)}, bf16[12,128,128]{2,1,0:T(8,128)(2,1)S(1)}, u32[]{:S(2)}, u32[]{:S(2)}) collective-permute-start(bf16[12,128,128]{2,1,0:T(8,128)(2,1)S(1)} %get-tuple-element.24), channel_id=1, source_target_pairs={{0,2},{2,4},{4,6},{6,8},{8,10},{10,12},{12,14},{1,3},{3,5},{5,7},{... | collective-permute-start | bytes 1179656 | tf_op jit(solution)/shard_map/ppermute | solution.py:319
  22.8 0.0 copy-done.2
  22.8 0.0 copy-done.3
  22.8 0.0 copy-done.7
  22.9 3.7 %shard_map.108 = (f32[25,256,128]{2,1,0:T(8,128)S(1)}, f32[25,128]{1,0:T(8,128)S(1)}, bf16[1280,1280]{1,0:T(8,128)(2,1)}, s32[25]{0:T(128)S(1)}) custom-call(s32[2,25]{1,0:T(2,128)S(1)} %bitcast.21, bf16[1280,1280]{1,0:T(8,128)(2,1)S(1)} %get-tuple-element.21.picture, bf16[256,256]{1,0:T(8,128)(2,1)S(1)} %copy-done.3, f32[1,128]{1,0:T(1,128)S(1)} %copy-done.7, ...), custom_call_target="tpu_custom_call" | custom-call | flops 629145600 | bytes 3276800 | tf_op jit(solution)/shard_map/pallas_call | solution.py:321
  26.6 1.1 %collective-permute-done.3.previous = bf16[13,128,128]{2,1,0:T(8,128)(2,1)S(1)} collective-permute-done((bf16[13,128,128]{2,1,0:T(8,128)(2,1)S(1)}, bf16[13,128,128]{2,1,0:T(8,128)(2,1)S(1)}, u32[]{:S(2)}, u32[]{:S(2)}) %collective-permute-start.3) | collective-permute-done | bytes 426016 | tf_op jit(solution)/shard_map/ppermute | solution.py:307
  27.7 2.5 %shard_map.109.rest_0_ = f32[25,128,128]{2,1,0:T(8,128)} custom-call(s32[25]{0:T(128)S(1)} %get-tuple-element.23.order, bf16[13,128,128]{2,1,0:T(8,128)(2,1)S(1)} %collective-permute-done.3.previous, f32[25,256,128]{2,1,0:T(8,128)S(1)} %get-tuple-element.25.spectra, f32[25,128]{1,0:T(8,128)S(1)} %get-tuple-element.26.powers, bf16[256,256]{1,0:T(8,128)(2,1)S(1)} %copy-done.3, ...), custom_call_target="tpu_custom_call" | custom-call | flops 436207616 | bytes 2981888 | tf_op jit(solution)/shard_map/pallas_call | solution.py:344
  30.3 4.6 %collective-permute-done.2.previous = bf16[12,128,128]{2,1,0:T(8,128)(2,1)S(1)} collective-permute-done((bf16[12,128,128]{2,1,0:T(8,128)(2,1)S(1)}, bf16[12,128,128]{2,1,0:T(8,128)(2,1)S(1)}, u32[]{:S(2)}, u32[]{:S(2)}) %collective-permute-start.2) | collective-permute-done | bytes 393248 | tf_op jit(solution)/shard_map/ppermute | solution.py:319
  34.8 2.4 %shard_map.110 = f32[25,128,128]{2,1,0:T(8,128)} custom-call(s32[25]{0:T(128)S(1)} %get-tuple-element.23.order, bf16[12,128,128]{2,1,0:T(8,128)(2,1)S(1)} %collective-permute-done.2.previous, f32[25,256,128]{2,1,0:T(8,128)S(1)} %get-tuple-element.25.spectra, f32[25,128]{1,0:T(8,128)S(1)} %get-tuple-element.26.powers, ...), custom_call_target="tpu_custom_call", output_to_operand_aliasing={{}: (8, {})} | custom-call | flops 402653184 | bytes 2752512 | tf_op jit(solution)/shard_map/pallas_call | solution.py:344
  (9 shorter events, 0.0 us)
Async XLA Ops:
  0.6 0.7 %copy-start.8 = (s32[1,25,2]{1,2,0:T(2,128)S(1)}, s32[1,25,2]{1,2,0:T(2,128)}, u32[]{:S(2)}) copy-start(s32[1,25,2]{1,2,0:T(2,128)} %param.13) | copy-start | bytes 604
  0.6 4.2 %copy-start = (bf16[1,25,256,256]{3,2,1,0:T(8,128)(2,1)S(1)}, bf16[1,25,256,256]{3,2,1,0:T(8,128)(2,1)}, u32[]{:S(2)}) copy-start(bf16[1,25,256,256]{3,2,1,0:T(8,128)(2,1)} %param.9) | copy-start | bytes 9830404
  0.7 4.2 %copy-start.1 = (bf16[16,256,256]{2,1,0:T(8,128)(2,1)S(1)}, bf16[16,256,256]{2,1,0:T(8,128)(2,1)}, u32[]{:S(2)}) copy-start(bf16[16,256,256]{2,1,0:T(8,128)(2,1)} %table.5) | copy-start | bytes 6291460
  0.7 4.2 %copy-start.5 = (s32[1,25,3,2]{1,3,2,0:T(2,128)S(1)}, s32[1,25,3,2]{1,3,2,0:T(2,128)}, u32[]{:S(2)}) copy-start(s32[1,25,3,2]{1,3,2,0:T(2,128)} %param.11) | copy-start | bytes 1804
  0.7 4.2 %copy-start.6 = (s32[1,25,3]{1,0,2:T(1,128)S(1)}, s32[1,25,3]{1,0,2:T(1,128)}, u32[]{:S(2)}) copy-start(s32[1,25,3]{1,0,2:T(1,128)} %param.10) | copy-start | bytes 904
  0.7 7.1 %collective-permute-start.1 = (bf16[25,256,256]{2,1,0:T(8,128)(2,1)}, bf16[25,256,256]{2,1,0:T(8,128)(2,1)S(1)}, u32[]{:S(2)}, u32[]{:S(2)}) collective-permute-start(bf16[25,256,256]{2,1,0:T(8,128)(2,1)} %bitcast.10), channel_id=1, source_target_pairs={{0,1},{1,0},{2,3},{3,2},{4,5},{5,4},{6,7},{7,6},{8,9},{9,8},{10,11... | collective-permute-start | bytes 9830408 | tf_op jit(solution)/shard_map/ppermute | solution.py:268
  1.3 6.5 %collective-permute-start = (s32[2,25]{1,0:T(2,128)S(1)}, s32[2,25]{1,0:T(2,128)S(1)}, u32[]{:S(2)}, u32[]{:S(2)}) collective-permute-start(s32[2,25]{1,0:T(2,128)S(1)} %bitcast.20), channel_id=1, source_target_pairs={{2,0},{4,2},{6,4},{8,6},{10,8},{12,10},{14,12},{3,1},{5,3},{7,5},{... | collective-permute-start | bytes 608 | tf_op jit(solution)/shard_map/ppermute | solution.py:276
  12.2 15.5 %collective-permute-start.3 = (bf16[13,128,128]{2,1,0:T(8,128)(2,1)S(1)}, bf16[13,128,128]{2,1,0:T(8,128)(2,1)S(1)}, u32[]{:S(2)}, u32[]{:S(2)}) collective-permute-start(bf16[13,128,128]{2,1,0:T(8,128)(2,1)S(1)} %get-tuple-element.27), channel_id=1, source_target_pairs={{0,2},{2,4},{4,6},{6,8},{8,10},{10,12},{12,14},{1,3},{3,5},{5,7},{... | collective-permute-start | bytes 1277960 | tf_op jit(solution)/shard_map/ppermute | solution.py:307
  15.7 7.1 %copy-start.2 = (bf16[256,256]{1,0:T(8,128)(2,1)S(1)}, bf16[256,256]{1,0:T(8,128)(2,1)}, u32[]{:S(2)}) copy-start(bf16[256,256]{1,0:T(8,128)(2,1)} %constant.10.clone.down) | copy-start | bytes 393220
  15.8 7.1 %copy-start.3 = (bf16[256,256]{1,0:T(8,128)(2,1)S(1)}, bf16[256,256]{1,0:T(8,128)(2,1)}, u32[]{:S(2)}) copy-start(bf16[256,256]{1,0:T(8,128)(2,1)} %constant.8.clone.forward) | copy-start | bytes 393220
  15.8 7.1 %copy-start.7 = (f32[1,128]{1,0:T(1,128)S(1)}, f32[1,128]{1,0:T(1,128)}, u32[]{:S(2)}) copy-start(f32[1,128]{1,0:T(1,128)} %constant.9.clone.lowest) | copy-start | bytes 1540
  19.1 8.6 %copy-start.4 = (bf16[256,128]{1,0:T(8,128)(2,1)S(1)}, bf16[256,128]{1,0:T(8,128)(2,1)}, u32[]{:S(2)}) copy-start(bf16[256,128]{1,0:T(8,128)(2,1)} %constant.11.clone.back) | copy-start | bytes 196612
  19.2 15.7 %collective-permute-start.2 = (bf16[12,128,128]{2,1,0:T(8,128)(2,1)S(1)}, bf16[12,128,128]{2,1,0:T(8,128)(2,1)S(1)}, u32[]{:S(2)}, u32[]{:S(2)}) collective-permute-start(bf16[12,128,128]{2,1,0:T(8,128)(2,1)S(1)} %get-tuple-element.24), channel_id=1, source_target_pairs={{0,2},{2,4},{4,6},{6,8},{8,10},{10,12},{12,14},{1,3},{3,5},{5,7},{... | collective-permute-start | bytes 1179656 | tf_op jit(solution)/shard_map/ppermute | solution.py:319

commit v7 on v6

--- a/solution.py
+++ b/solution.py
@@ -14,9 +14,12 @@
 KP = 3
 CAP = 12
 LISTED = CAP + 1
+SHIFT = 8
+FIELD = 1 << SHIFT
 EPSILON = 1e-06
 ROWS = PS + 16
 COLS = 2 * PS
+LAG = 3
 
 SMEM = pl.BlockSpec(memory_space=pltpu.SMEM)
 VMEM = pl.BlockSpec(memory_space=pltpu.VMEM)
@@ -85,31 +88,37 @@
         for k in range(KP):
             local = ids[k, 0, block] - low
             here = (local >= 0) & (local < count)
-            plan[block * KP + k] = jnp.where(here, -1, found)
+            index = jnp.where(here, local, 0)
             slot = jnp.minimum(found, CAP)
+            plan[block * KP + k] = (
+                jnp.where(here, 0, slot + 1)
+                + mats[k, 1, block] * FIELD
+                + mats[k, 0, block] * FIELD**2
+                + index * FIELD**3
+            )
             plan[pulls + slot] = jnp.where(here, 0, jnp.where(local < 0, local + count, local - count))
             plan[pulls + LISTED + slot] = mats[k, 0, block]
             found = found + jnp.where(here, 0, 1)
             if grid <= block < count - grid:
-                left = dot(table[mats[k, 0, block]], source[jnp.where(here, local, 0)])
+                left = dot(table[mats[k, 0, block]], source[index])
                 lefts[(block - grid) * KP + k] = left.astype(BF16)
 
 
-def warp_row(row, inner, low, grid, ids, mats, source, table, plan, lefts, others):
+def warp_row(row, inner, grid, source, table, plan, lefts, others):
     blocks = []
     for column in range(grid):
         block = row * grid + column
         total = None
         for k in range(KP):
-            slot = plan[block * KP + k]
+            pull = plan[block * KP + k]
+            slot, column_matrix = pull & FIELD - 1, (pull >> SHIFT) & FIELD - 1
             if inner:
                 near = lefts[(block - grid) * KP + k]
             else:
-                local = jnp.where(slot < 0, ids[k, 0, block] - low, 0)
-                near = dot(table[mats[k, 0, block]], source[local]).astype(BF16)
-            left = jnp.where(slot < 0, near, others[jnp.maximum(slot, 0)])
+                near = dot(table[(pull >> 2 * SHIFT) & FIELD - 1], source[pull >> 3 * SHIFT]).astype(BF16)
+            left = jnp.where(slot == 0, near, others[jnp.maximum(slot - 1, 0)])
             term = lax.dot_general(
-                left, table[mats[k, 1, block]], (((1,), (1,)), ((), ())), preferred_element_type=F32
+                left, table[column_matrix], (((1,), (1,)), ((), ())), preferred_element_type=F32
             )
             total = term if total is None else total + term
         blocks.append(total.astype(BF16))
@@ -140,37 +149,35 @@
 
 
 def early_kernel(
-    grid, patches, plan, ids, mats, corners, source, other, table, lefts, early, others, out, order, bands
+    grid, patches, plan, corners, source, other, table, lefts, early, others, out, order, bands
 ):
     pulls = grid * grid * KP
-    low = lax.axis_index("tile") * grid * grid
     for r in range(CAP):
         left = dot(table[plan[pulls + LISTED + r]], other[plan[pulls + r]])
         others[r] = left.astype(BF16)
     down = window_order(corners, order, patches, grid)
     above = jnp.where(down == 0, 1, 0)
-    given = ids, mats, source, table, plan, lefts, others
+    given = source, table, plan, lefts, others
     for n in range(early_rows(grid) - 1):
-        fill_row(early, n + above, warp_row(down + n + above, True, low, grid, *given))
+        fill_row(early, n + above, warp_row(down + n + above, True, grid, *given))
     outer = jnp.where(down == 0, 0, grid - 1)
-    fill_row(early, outer - down, warp_row(outer, False, low, grid, *given))
+    fill_row(early, outer - down, warp_row(outer, False, grid, *given))
     cut_windows(early, corners, [order[n] for n in range(out.shape[0])], down * BS, bands, out)
 
 
 def late_kernel(
-    grid, patches, plan, ids, mats, corners, source, table, lefts, others, early, picture, out, order, bands
+    grid, patches, plan, corners, source, table, lefts, others, early, picture, out, order, bands
 ):
     rows = early_rows(grid)
-    low = lax.axis_index("tile") * grid * grid
     down = window_order(corners, order, patches, grid)
-    given = ids, mats, source, table, plan, lefts, others
+    given = source, table, plan, lefts, others
     for n in range(rows):
         picture[pl.ds(pl.multiple_of((down + n) * BS, BS), BS), :] = early[pl.ds(n * BS, BS), :]
     for n in range(grid - rows - 1):
         row = jnp.where(down == 0, rows + n, 1 + n)
-        fill_row(picture, row, warp_row(row, True, low, grid, *given))
+        fill_row(picture, row, warp_row(row, True, grid, *given))
     outer = jnp.where(down == 0, grid - 1, 0)
-    fill_row(picture, outer, warp_row(outer, False, low, grid, *given))
+    fill_row(picture, outer, warp_row(outer, False, grid, *given))
     wanted = [order[n] for n in range(patches - out.shape[0], patches)]
     cut_windows(picture, corners, wanted, 0, bands, out)
 
@@ -214,34 +221,47 @@
     fetch = pltpu.make_async_copy(order, slots, slots_sem)
     fetch.start()
     pairs = [share[start : start + 2] for start in range(0, len(share), 2)]
-    for n in range(len(share)):
-        at = pl.ds(n % 2 * PS, PS)
-        halves[n // 2, :PS, at], halves[n // 2, PS:, at] = spectrum_columns(previous[n], forward, lowest)
-    for q, pair in enumerate(pairs):
-        width = PS * len(pair)
-        second = dot(down[...], halves[q, :, :width])
+    writes = []
+
+    def columns(q):
+        for n in range(len(pairs[q])):
+            at = pl.ds(n * PS, PS)
+            halves[q, :PS, at], halves[q, PS:, at] = spectrum_columns(previous[2 * q + n], forward, lowest)
+
+    def cross(q):
+        pair = pairs[q]
+        second = dot(down[...], halves[q, :, : PS * len(pair)])
         for n, p in enumerate(pair):
             one_real, one_imag = spectra[p, :PS, :], spectra[p, PS:, :]
             two_real, two_imag = second[:PS, n * PS : (n + 1) * PS], second[PS:, n * PS : (n + 1) * PS]
-            scales[pl.ds(2 * q + n, 1), :] = energy(two_real, two_imag)
+            power = mean_square(energy(two_real, two_imag))
+            product = (powers[pl.ds(p, 1), :] + EPSILON) * (power + EPSILON)
+            scales[pl.ds(2 * q + n, 1), :] = lax.rsqrt(product) * (1.0 / (PS * PS * PS))
             real = one_real * two_real + one_imag * two_imag
             imag = one_real * two_imag - one_imag * two_real
             crosses[q, :PS, pl.ds(n * PS, PS)] = real.astype(BF16)
             crosses[q, PS:, pl.ds(n * PS, PS)] = imag.astype(BF16)
-    product = (powers[pl.ds(share[0], len(share)), :] + EPSILON) * (mean_square(scales[...]) + EPSILON)
-    scales[...] = lax.rsqrt(product) * (1.0 / (PS * PS * PS))
-    for q, pair in enumerate(pairs):
-        width = PS * len(pair)
-        both = dot(down[...], crosses[q, :, :width]).astype(BF16)
-        for n, p in enumerate(pair):
+
+    def mix(q):
+        pair = pairs[q]
+        both = dot(down[...], crosses[q, :, : PS * len(pair)]).astype(BF16)
+        for n in range(len(pair)):
             mixed[2 * q + n, :, :PS] = both[:PS, n * PS : (n + 1) * PS]
             mixed[2 * q + n, :, PS:] = both[PS:, n * PS : (n + 1) * PS]
-    fetch.wait()
-    writes = []
-    for n, p in enumerate(share):
-        done[n] = dot(mixed[n], back[...]) * scales[pl.ds(n, 1), :]
-        writes.append(pltpu.make_async_copy(done.at[n], out.at[slots[p]], sems.at[n]))
-        writes[-1].start()
+
+    def finish(q):
+        if q == 0:
+            fetch.wait()
+        for n, p in enumerate(pairs[q], 2 * q):
+            done[n] = dot(mixed[n], back[...]) * scales[pl.ds(n, 1), :]
+            writes.append(pltpu.make_async_copy(done.at[n], out.at[slots[p]], sems.at[n]))
+            writes[-1].start()
+
+    stages = columns, cross, mix, finish
+    for step in range(len(pairs) + LAG * (len(stages) - 1)):
+        for s, stage in enumerate(stages):
+            if 0 <= step - LAG * s < len(pairs):
+                stage(step - LAG * s)
     for write in writes:
         write.wait()
 
@@ -299,11 +319,11 @@
             jax.ShapeDtypeStruct((CAP, BS, BS), BF16),
             jax.ShapeDtypeStruct((len(shares[0]), PS, PS), BF16),
         ),
-        in_specs=[SMEM] * 4 + [VMEM] * 4,
+        in_specs=[SMEM] * 2 + [VMEM] * 4,
         out_specs=[VMEM] * 3,
         scratch_shapes=[pltpu.SMEM((patches,), jnp.int32), pltpu.VMEM((len(shares[0]), PS, COLS), BF16)],
         **params(16, rows * grid * KP * 2 * BS**3, rows * grid * KP * BS * BS * 4),
-    )(plan, ids, mats, wanted, blocks, other, interp_table, lefts)
+    )(plan, wanted, blocks, other, interp_table, lefts)
     arrivals = [lax.ppermute(sent, "sec", onward)]
     picture, sent = pl.pallas_call(
         functools.partial(late_kernel, grid, patches),
@@ -311,11 +331,11 @@
             jax.ShapeDtypeStruct((side, side), BF16),
             jax.ShapeDtypeStruct((len(shares[1]), PS, PS), BF16),
         ),
-        in_specs=[SMEM] * 4 + [VMEM] * 5,
+        in_specs=[SMEM] * 2 + [VMEM] * 5,
         out_specs=[VMEM] * 2,
         scratch_shapes=[pltpu.SMEM((patches,), jnp.int32), pltpu.VMEM((len(shares[0]), PS, COLS), BF16)],
         **params(16, (grid - rows) * grid * KP * 2 * BS**3, side * side * 4),
-    )(plan, ids, mats, wanted, blocks, interp_table, lefts, others, early)
+    )(plan, wanted, blocks, interp_table, lefts, others, early)
     arrivals.append(lax.ppermute(sent, "sec", onward))
 
     spectra, powers, warped, order = pl.pallas_call(

time: 37.7 us -> 37.5 us (level)
  no operation moved by 1% of the time
where the time goes in v7:
time: 37.5 us; the launch traced here: 37.3 us
  Pallas kernels  19.1 us (51%)
  starting transfers between devices  10.8 us (29%)
  waiting for transfers between devices  5.77 us (15%)
  between operations  1.01 us (3%)
  local copies, waits for them, and re-layouts  0.59 us (2%)
    pallas_call x2, Pallas kernels, shards(): pl.pallas_call(functools.partial(match_kernel, share), out_shape=jax.Shap...  4.87 us
    ppermute x1, waiting for transfers between devices, shards(): arrivals.append(lax.ppermute(sent, 'sec', onward))  4.56 us
    pallas_call x1, Pallas kernels, shards(): pl.pallas_call(functools.partial(early_kernel, grid, patches), out_shape=...  4.31 us
    pallas_call x1, Pallas kernels, shards(): pl.pallas_call(functools.partial(own_kernel, patches, grid), out_shape=(j...  3.74 us
    ppermute x1, starting transfers between devices, shards(): arrivals.append(lax.ppermute(sent, 'sec', onward))  3.67 us
    ppermute x1, starting transfers between devices, shards(): lax.ppermute(asked, 'sec', [(i + 1, i) for i in range(sections - 1)])  3.56 us
    ppermute x1, starting transfers between devices, shards(): arrivals = [lax.ppermute(sent, 'sec', onward)]  3.49 us
    pallas_call x1, Pallas kernels, shards(): pl.pallas_call(functools.partial(late_kernel, grid, patches), out_shape=(...  3.3 us
  transfers between devices with their start and end apart: 4, of which 2 were waited for; matrix products, arithmetic and copies ran while one was open for 0% of the time, Pallas kernels for 33%

profile of v7, /device:TPU:10, one launch (start us, length us, event | category | flops | bytes accessed | tf_op | source)
XLA Modules:
  0.0 37.3 jit_solution(15094595393947512909)
XLA Ops:
  0.6 0.0 copy-start.6
  0.7 0.1 collective-permute-start.1
  0.8 0.5 %copy-done.6 = s32[1,25,2]{1,2,0:T(2,128)S(1)} copy-done((s32[1,25,2]{1,2,0:T(2,128)S(1)}, s32[1,25,2]{1,2,0:T(2,128)}, u32[]{:S(2)}) %copy-start.6) | copy-done | bytes 224
  1.3 3.6 %collective-permute-start = (s32[2,25]{1,0:T(2,128)S(1)}, s32[2,25]{1,0:T(2,128)S(1)}, u32[]{:S(2)}, u32[]{:S(2)}) collective-permute-start(s32[2,25]{1,0:T(2,128)S(1)} %bitcast.14), channel_id=1, source_target_pairs={{2,0},{4,2},{6,4},{8,6},{10,8},{12,10},{14,12},{3,1},{5,3},{7,5},{... | collective-permute-start | bytes 608 | tf_op jit(solution)/shard_map/ppermute | solution.py:296
  4.9 0.0 copy-done
  4.9 0.0 copy-done.1
  4.9 0.0 copy-done.7
  4.9 0.0 copy-done.8
  4.9 2.9 %shard_map.105 = (bf16[45,256,256]{2,1,0:T(8,128)(2,1)S(1)}, s32[101]{0:T(128)S(1)}) custom-call(s32[3,1,25]{2,1,0:T(1,128)S(1)} %bitcast.17, s32[3,2,25]{2,1,0:T(2,128)S(1)} %bitcast.16, bf16[25,256,256]{2,1,0:T(8,128)(2,1)S(1)} %bitcast.11, bf16[16,256,256]{2,1,0:T(8,128)(2,1)S(1)} %copy-done.1, f32[8,128]{1,0:T(8,128)S(1)} %shard_map.104.gate), custom_call_target="tpu_custom_call" | custom-call | flops 1509949440 | bytes 9175040 | tf_op jit(solution)/shard_map/pallas_call | solution.py:303
  7.8 0.0 collective-permute-done.corners
  7.8 0.0 collective-permute-done.1.other
  7.8 4.3 %shard_map.106 = (bf16[768,1280]{1,0:T(8,128)(2,1)S(1)}, bf16[12,256,256]{2,1,0:T(8,128)(2,1)S(1)}, bf16[13,128,128]{2,1,0:T(8,128)(2,1)S(1)}) custom-call(s32[101]{0:T(128)S(1)} %get-tuple-element.16.plan, s32[2,25]{1,0:T(2,128)S(1)} %collective-permute-done.corners, bf16[25,256,256]{2,1,0:T(8,128)(2,1)S(1)} %bitcast.12, ...), custom_call_target="tpu_custom_call" | custom-call | flops 1509949440 | bytes 11796480 | tf_op jit(solution)/shard_map/pallas_call | solution.py:315
  12.2 3.5 %collective-permute-start.3 = (bf16[13,128,128]{2,1,0:T(8,128)(2,1)S(1)}, bf16[13,128,128]{2,1,0:T(8,128)(2,1)S(1)}, u32[]{:S(2)}, u32[]{:S(2)}) collective-permute-start(bf16[13,128,128]{2,1,0:T(8,128)(2,1)S(1)} %get-tuple-element.27), channel_id=1, source_target_pairs={{0,2},{2,4},{4,6},{6,8},{8,10},{10,12},{12,14},{1,3},{3,5},{5,7},{... | collective-permute-start | bytes 1277960 | tf_op jit(solution)/shard_map/ppermute | solution.py:327
  15.7 0.0 copy-start.2
  15.7 0.0 copy-start.3
  15.7 0.0 copy-start.5
  15.7 3.3 %shard_map.107 = (bf16[1280,1280]{1,0:T(8,128)(2,1)S(1)}, bf16[12,128,128]{2,1,0:T(8,128)(2,1)S(1)}) custom-call(s32[101]{0:T(128)S(1)} %get-tuple-element.16.plan, s32[2,25]{1,0:T(2,128)S(1)} %collective-permute-done.corners, bf16[25,256,256]{2,1,0:T(8,128)(2,1)S(1)} %bitcast.13, bf16[16,256,256]{2,1,0:T(8,128)(2,1)S(1)} %copy-done.1, ...), custom_call_target="tpu_custom_call" | custom-call | flops 1006632960 | bytes 6553600 | tf_op jit(solution)/shard_map/pallas_call | solution.py:328
  19.0 0.0 copy-start.4
  19.0 3.7 %collective-permute-start.2 = (bf16[12,128,128]{2,1,0:T(8,128)(2,1)S(1)}, bf16[12,128,128]{2,1,0:T(8,128)(2,1)S(1)}, u32[]{:S(2)}, u32[]{:S(2)}) collective-permute-start(bf16[12,128,128]{2,1,0:T(8,128)(2,1)S(1)} %get-tuple-element.24), channel_id=1, source_target_pairs={{0,2},{2,4},{4,6},{6,8},{8,10},{10,12},{12,14},{1,3},{3,5},{5,7},{... | collective-permute-start | bytes 1179656 | tf_op jit(solution)/shard_map/ppermute | solution.py:339
  22.7 3.7 %shard_map.108 = (f32[25,256,128]{2,1,0:T(8,128)S(1)}, f32[25,128]{1,0:T(8,128)S(1)}, bf16[1280,1280]{1,0:T(8,128)(2,1)}, s32[25]{0:T(128)S(1)}) custom-call(s32[2,25]{1,0:T(2,128)S(1)} %bitcast.15, bf16[1280,1280]{1,0:T(8,128)(2,1)S(1)} %get-tuple-element.21.picture, bf16[256,256]{1,0:T(8,128)(2,1)S(1)} %copy-done.3, f32[1,128]{1,0:T(1,128)S(1)} %copy-done.5, ...), custom_call_target="tpu_custom_call" | custom-call | flops 629145600 | bytes 3276800 | tf_op jit(solution)/shard_map/pallas_call | solution.py:341
  26.5 1.2 %collective-permute-done.3.previous = bf16[13,128,128]{2,1,0:T(8,128)(2,1)S(1)} collective-permute-done((bf16[13,128,128]{2,1,0:T(8,128)(2,1)S(1)}, bf16[13,128,128]{2,1,0:T(8,128)(2,1)S(1)}, u32[]{:S(2)}, u32[]{:S(2)}) %collective-permute-start.3) | collective-permute-done | bytes 426016 | tf_op jit(solution)/shard_map/ppermute | solution.py:327
  27.7 2.5 %shard_map.109.rest_0_ = f32[25,128,128]{2,1,0:T(8,128)} custom-call(s32[25]{0:T(128)S(1)} %get-tuple-element.23.order, bf16[13,128,128]{2,1,0:T(8,128)(2,1)S(1)} %collective-permute-done.3.previous, f32[25,256,128]{2,1,0:T(8,128)S(1)} %get-tuple-element.25.spectra, f32[25,128]{1,0:T(8,128)S(1)} %get-tuple-element.26.powers, bf16[256,256]{1,0:T(8,128)(2,1)S(1)} %copy-done.3, ...), custom_call_target="tpu_custom_call" | custom-call | flops 436207616 | bytes 2981888 | tf_op jit(solution)/shard_map/pallas_call | solution.py:364
  30.2 4.6 %collective-permute-done.2.previous = bf16[12,128,128]{2,1,0:T(8,128)(2,1)S(1)} collective-permute-done((bf16[12,128,128]{2,1,0:T(8,128)(2,1)S(1)}, bf16[12,128,128]{2,1,0:T(8,128)(2,1)S(1)}, u32[]{:S(2)}, u32[]{:S(2)}) %collective-permute-start.2) | collective-permute-done | bytes 393248 | tf_op jit(solution)/shard_map/ppermute | solution.py:339
  34.8 2.4 %shard_map.110 = f32[25,128,128]{2,1,0:T(8,128)} custom-call(s32[25]{0:T(128)S(1)} %get-tuple-element.23.order, bf16[12,128,128]{2,1,0:T(8,128)(2,1)S(1)} %collective-permute-done.2.previous, f32[25,256,128]{2,1,0:T(8,128)S(1)} %get-tuple-element.25.spectra, f32[25,128]{1,0:T(8,128)S(1)} %get-tuple-element.26.powers, ...), custom_call_target="tpu_custom_call", output_to_operand_aliasing={{}: (8, {})} | custom-call | flops 402653184 | bytes 2752512 | tf_op jit(solution)/shard_map/pallas_call | solution.py:364
  (9 shorter events, 0.0 us)
Async XLA Ops:
  0.6 0.7 %copy-start.6 = (s32[1,25,2]{1,2,0:T(2,128)S(1)}, s32[1,25,2]{1,2,0:T(2,128)}, u32[]{:S(2)}) copy-start(s32[1,25,2]{1,2,0:T(2,128)} %param.13) | copy-start | bytes 604
  0.6 4.2 %copy-start = (bf16[1,25,256,256]{3,2,1,0:T(8,128)(2,1)S(1)}, bf16[1,25,256,256]{3,2,1,0:T(8,128)(2,1)}, u32[]{:S(2)}) copy-start(bf16[1,25,256,256]{3,2,1,0:T(8,128)(2,1)} %param.9) | copy-start | bytes 9830404
  0.7 4.2 %copy-start.1 = (bf16[16,256,256]{2,1,0:T(8,128)(2,1)S(1)}, bf16[16,256,256]{2,1,0:T(8,128)(2,1)}, u32[]{:S(2)}) copy-start(bf16[16,256,256]{2,1,0:T(8,128)(2,1)} %table.5) | copy-start | bytes 6291460
  0.7 4.2 %copy-start.7 = (s32[1,25,3,2]{1,3,2,0:T(2,128)S(1)}, s32[1,25,3,2]{1,3,2,0:T(2,128)}, u32[]{:S(2)}) copy-start(s32[1,25,3,2]{1,3,2,0:T(2,128)} %param.11) | copy-start | bytes 1804
  0.7 4.2 %copy-start.8 = (s32[1,25,3]{1,0,2:T(1,128)S(1)}, s32[1,25,3]{1,0,2:T(1,128)}, u32[]{:S(2)}) copy-start(s32[1,25,3]{1,0,2:T(1,128)} %param.10) | copy-start | bytes 904
  0.7 7.2 %collective-permute-start.1 = (bf16[25,256,256]{2,1,0:T(8,128)(2,1)}, bf16[25,256,256]{2,1,0:T(8,128)(2,1)S(1)}, u32[]{:S(2)}, u32[]{:S(2)}) collective-permute-start(bf16[25,256,256]{2,1,0:T(8,128)(2,1)} %bitcast.10), channel_id=1, source_target_pairs={{0,1},{1,0},{2,3},{3,2},{4,5},{5,4},{6,7},{7,6},{8,9},{9,8},{10,11... | collective-permute-start | bytes 9830408 | tf_op jit(solution)/shard_map/ppermute | solution.py:288
  1.3 6.5 %collective-permute-start = (s32[2,25]{1,0:T(2,128)S(1)}, s32[2,25]{1,0:T(2,128)S(1)}, u32[]{:S(2)}, u32[]{:S(2)}) collective-permute-start(s32[2,25]{1,0:T(2,128)S(1)} %bitcast.14), channel_id=1, source_target_pairs={{2,0},{4,2},{6,4},{8,6},{10,8},{12,10},{14,12},{3,1},{5,3},{7,5},{... | collective-permute-start | bytes 608 | tf_op jit(solution)/shard_map/ppermute | solution.py:296
  12.2 15.5 %collective-permute-start.3 = (bf16[13,128,128]{2,1,0:T(8,128)(2,1)S(1)}, bf16[13,128,128]{2,1,0:T(8,128)(2,1)S(1)}, u32[]{:S(2)}, u32[]{:S(2)}) collective-permute-start(bf16[13,128,128]{2,1,0:T(8,128)(2,1)S(1)} %get-tuple-element.27), channel_id=1, source_target_pairs={{0,2},{2,4},{4,6},{6,8},{8,10},{10,12},{12,14},{1,3},{3,5},{5,7},{... | collective-permute-start | bytes 1277960 | tf_op jit(solution)/shard_map/ppermute | solution.py:327
  15.7 7.0 %copy-start.2 = (bf16[256,256]{1,0:T(8,128)(2,1)S(1)}, bf16[256,256]{1,0:T(8,128)(2,1)}, u32[]{:S(2)}) copy-start(bf16[256,256]{1,0:T(8,128)(2,1)} %constant.10.clone.down) | copy-start | bytes 393220
  15.7 7.0 %copy-start.3 = (bf16[256,256]{1,0:T(8,128)(2,1)S(1)}, bf16[256,256]{1,0:T(8,128)(2,1)}, u32[]{:S(2)}) copy-start(bf16[256,256]{1,0:T(8,128)(2,1)} %constant.8.clone.forward) | copy-start | bytes 393220
  15.7 7.0 %copy-start.5 = (f32[1,128]{1,0:T(1,128)S(1)}, f32[1,128]{1,0:T(1,128)}, u32[]{:S(2)}) copy-start(f32[1,128]{1,0:T(1,128)} %constant.9.clone.lowest) | copy-start | bytes 1540
  19.0 8.7 %copy-start.4 = (bf16[256,128]{1,0:T(8,128)(2,1)S(1)}, bf16[256,128]{1,0:T(8,128)(2,1)}, u32[]{:S(2)}) copy-start(bf16[256,128]{1,0:T(8,128)(2,1)} %constant.11.clone.back) | copy-start | bytes 196612
  19.0 15.8 %collective-permute-start.2 = (bf16[12,128,128]{2,1,0:T(8,128)(2,1)S(1)}, bf16[12,128,128]{2,1,0:T(8,128)(2,1)S(1)}, u32[]{:S(2)}, u32[]{:S(2)}) collective-permute-start(bf16[12,128,128]{2,1,0:T(8,128)(2,1)S(1)} %get-tuple-element.24), channel_id=1, source_target_pairs={{0,2},{2,4},{4,6},{6,8},{8,10},{10,12},{12,14},{1,3},{3,5},{5,7},{... | collective-permute-start | bytes 1179656 | tf_op jit(solution)/shard_map/ppermute | solution.py:339

commit v8 on v7

--- a/solution.py
+++ b/solution.py
@@ -55,6 +55,10 @@
 
 def early_rows(grid):
     return grid // 2 + 1
+
+
+def always_early(row, grid):
+    return grid - early_rows(grid) <= row < early_rows(grid)
 
 
 def from_top(corners, patches, grid):
@@ -99,9 +103,9 @@
             plan[pulls + slot] = jnp.where(here, 0, jnp.where(local < 0, local + count, local - count))
             plan[pulls + LISTED + slot] = mats[k, 0, block]
             found = found + jnp.where(here, 0, 1)
-            if grid <= block < count - grid:
+            if always_early(block // grid, grid):
                 left = dot(table[mats[k, 0, block]], source[index])
-                lefts[(block - grid) * KP + k] = left.astype(BF16)
+                lefts[(block - (grid - early_rows(grid)) * grid) * KP + k] = left.astype(BF16)
 
 
 def warp_row(row, inner, grid, source, table, plan, lefts, others):
@@ -113,7 +117,7 @@
             pull = plan[block * KP + k]
             slot, column_matrix = pull & FIELD - 1, (pull >> SHIFT) & FIELD - 1
             if inner:
-                near = lefts[(block - grid) * KP + k]
+                near = lefts[(block - (grid - early_rows(grid)) * grid) * KP + k]
             else:
                 near = dot(table[(pull >> 2 * SHIFT) & FIELD - 1], source[pull >> 3 * SHIFT]).astype(BF16)
             left = jnp.where(slot == 0, near, others[jnp.maximum(slot - 1, 0)])
@@ -156,12 +160,13 @@
         left = dot(table[plan[pulls + LISTED + r]], other[plan[pulls + r]])
         others[r] = left.astype(BF16)
     down = window_order(corners, order, patches, grid)
-    above = jnp.where(down == 0, 1, 0)
     given = source, table, plan, lefts, others
-    for n in range(early_rows(grid) - 1):
-        fill_row(early, n + above, warp_row(down + n + above, True, grid, *given))
-    outer = jnp.where(down == 0, 0, grid - 1)
-    fill_row(early, outer - down, warp_row(outer, False, grid, *given))
+    for row in range(grid):
+        if always_early(row, grid):
+            fill_row(early, row - down, warp_row(row, True, grid, *given))
+    outer = jnp.where(down == 0, 0, early_rows(grid))
+    for n in range(grid - early_rows(grid)):
+        fill_row(early, outer + n - down, warp_row(outer + n, False, grid, *given))
     cut_windows(early, corners, [order[n] for n in range(out.shape[0])], down * BS, bands, out)
 
 
@@ -173,11 +178,9 @@
     given = source, table, plan, lefts, others
     for n in range(rows):
         picture[pl.ds(pl.multiple_of((down + n) * BS, BS), BS), :] = early[pl.ds(n * BS, BS), :]
-    for n in range(grid - rows - 1):
-        row = jnp.where(down == 0, rows + n, 1 + n)
-        fill_row(picture, row, warp_row(row, True, grid, *given))
-    outer = jnp.where(down == 0, grid - 1, 0)
-    fill_row(picture, outer, warp_row(outer, False, grid, *given))
+    outer = jnp.where(down == 0, rows, 0)
+    for n in range(grid - rows):
+        fill_row(picture, outer + n, warp_row(outer + n, False, grid, *given))
     wanted = [order[n] for n in range(patches - out.shape[0], patches)]
     cut_windows(picture, corners, wanted, 0, bands, out)
 
@@ -299,7 +302,7 @@
     onward = [(i, i + 1) for i in range(sections - 1)]
 
     pulls = count * KP
-    inner = pulls - 2 * grid * KP
+    inner = (2 * early_rows(grid) - grid) * grid * KP
     lefts, plan = pl.pallas_call(
         functools.partial(near_kernel, count, grid),
         out_shape=(

time: 37.5 us -> 37.4 us (level)
    ppermute x1, starting transfers between devices: 3.49 us -> 4.22 us  [shards(): arrivals = [lax.ppermute(sent, 'sec', onward)]]
    ppermute x1, starting transfers between devices: 3.67 us -> 2.94 us  [shards(): arrivals.append(lax.ppermute(sent, 'sec', onward))]
    pallas_call x1, Pallas kernels: 2.9 us -> 2.18 us  [shards(): pl.pallas_call(functools.partial(near_kernel, count, grid), out_shape=(ja...]
    ppermute x1, waiting for transfers between devices: 1.21 us -> 0.71 us  [shards(): arrivals = [lax.ppermute(sent, 'sec', onward)]]
    pallas_call x1, Pallas kernels: 3.3 us -> 3.77 us  [shards(): pl.pallas_call(functools.partial(late_kernel, grid, patches), out_shape=(...]
    pallas_call x1, Pallas kernels: 4.31 us -> 4.76 us  [shards(): pl.pallas_call(functools.partial(early_kernel, grid, patches), out_shape=...]
where the time goes in v8:
time: 37.4 us; the launch traced here: 37.2 us
  Pallas kernels  19.3 us (52%)
  starting transfers between devices  10.8 us (29%)
  waiting for transfers between devices  5.44 us (15%)
  between operations  1.01 us (3%)
  local copies, waits for them, and re-layouts  0.59 us (2%)
    pallas_call x2, Pallas kernels, shards(): pl.pallas_call(functools.partial(match_kernel, share), out_shape=jax.Shap...  4.86 us
    pallas_call x1, Pallas kernels, shards(): pl.pallas_call(functools.partial(early_kernel, grid, patches), out_shape=...  4.76 us
    ppermute x1, waiting for transfers between devices, shards(): arrivals.append(lax.ppermute(sent, 'sec', onward))  4.73 us
    ppermute x1, starting transfers between devices, shards(): arrivals = [lax.ppermute(sent, 'sec', onward)]  4.22 us
    pallas_call x1, Pallas kernels, shards(): pl.pallas_call(functools.partial(late_kernel, grid, patches), out_shape=(...  3.77 us
    pallas_call x1, Pallas kernels, shards(): pl.pallas_call(functools.partial(own_kernel, patches, grid), out_shape=(j...  3.75 us
    ppermute x1, starting transfers between devices, shards(): lax.ppermute(asked, 'sec', [(i + 1, i) for i in range(sections - 1)])  3.56 us
    ppermute x1, starting transfers between devices, shards(): arrivals.append(lax.ppermute(sent, 'sec', onward))  2.94 us
  transfers between devices with their start and end apart: 4, of which 2 were waited for; matrix products, arithmetic and copies ran while one was open for 0% of the time, Pallas kernels for 33%

profile of v8, /device:TPU:10, one launch (start us, length us, event | category | flops | bytes accessed | tf_op | source)
XLA Modules:
  0.0 37.2 jit_solution(9164123492650682288)
XLA Ops:
  0.6 0.0 copy-start.8
  0.6 0.0 copy-start
  0.7 0.0 copy-start.1
  0.7 0.0 copy-start.6
  0.7 0.0 copy-start.7
  0.7 0.1 collective-permute-start.1
  0.8 0.5 %copy-done.8 = s32[1,25,2]{1,2,0:T(2,128)S(1)} copy-done((s32[1,25,2]{1,2,0:T(2,128)S(1)}, s32[1,25,2]{1,2,0:T(2,128)}, u32[]{:S(2)}) %copy-start.8) | copy-done | bytes 224
  1.3 3.6 %collective-permute-start = (s32[2,25]{1,0:T(2,128)S(1)}, s32[2,25]{1,0:T(2,128)S(1)}, u32[]{:S(2)}, u32[]{:S(2)}) collective-permute-start(s32[2,25]{1,0:T(2,128)S(1)} %bitcast.16), channel_id=1, source_target_pairs={{2,0},{4,2},{6,4},{8,6},{10,8},{12,10},{14,12},{3,1},{5,3},{7,5},{... | collective-permute-start | bytes 608 | tf_op jit(solution)/shard_map/ppermute | solution.py:299
  4.9 2.2 %shard_map.105 = (bf16[15,256,256]{2,1,0:T(8,128)(2,1)S(1)}, s32[101]{0:T(128)S(1)}) custom-call(s32[3,1,25]{2,1,0:T(1,128)S(1)} %bitcast.15, s32[3,2,25]{2,1,0:T(2,128)S(1)} %bitcast.14, bf16[25,256,256]{2,1,0:T(8,128)(2,1)S(1)} %bitcast.11, bf16[16,256,256]{2,1,0:T(8,128)(2,1)S(1)} %copy-done.1, f32[8,128]{1,0:T(8,128)S(1)} %shard_map.104.gate), custom_call_target="tpu_custom_call" | custom-call | flops 503316480 | bytes 5242880 | tf_op jit(solution)/shard_map/pallas_call | solution.py:306
  7.1 0.0 collective-permute-done.corners
  7.1 0.0 collective-permute-done.1.other
  7.1 4.8 %shard_map.106 = (bf16[768,1280]{1,0:T(8,128)(2,1)S(1)}, bf16[12,256,256]{2,1,0:T(8,128)(2,1)S(1)}, bf16[13,128,128]{2,1,0:T(8,128)(2,1)S(1)}) custom-call(s32[101]{0:T(128)S(1)} %get-tuple-element.16.plan, s32[2,25]{1,0:T(2,128)S(1)} %collective-permute-done.corners, bf16[25,256,256]{2,1,0:T(8,128)(2,1)S(1)} %bitcast.12, ...), custom_call_target="tpu_custom_call" | custom-call | flops 1509949440 | bytes 11796480 | tf_op jit(solution)/shard_map/pallas_call | solution.py:318
  11.9 4.2 %collective-permute-start.3 = (bf16[13,128,128]{2,1,0:T(8,128)(2,1)S(1)}, bf16[13,128,128]{2,1,0:T(8,128)(2,1)S(1)}, u32[]{:S(2)}, u32[]{:S(2)}) collective-permute-start(bf16[13,128,128]{2,1,0:T(8,128)(2,1)S(1)} %get-tuple-element.27), channel_id=1, source_target_pairs={{0,2},{2,4},{4,6},{6,8},{8,10},{10,12},{12,14},{1,3},{3,5},{5,7},{... | collective-permute-start | bytes 1277960 | tf_op jit(solution)/shard_map/ppermute | solution.py:330
  16.1 0.0 copy-start.2
  16.1 0.0 copy-start.3
  16.2 0.0 copy-start.5
  16.2 3.8 %shard_map.107 = (bf16[1280,1280]{1,0:T(8,128)(2,1)S(1)}, bf16[12,128,128]{2,1,0:T(8,128)(2,1)S(1)}) custom-call(s32[101]{0:T(128)S(1)} %get-tuple-element.16.plan, s32[2,25]{1,0:T(2,128)S(1)} %collective-permute-done.corners, bf16[25,256,256]{2,1,0:T(8,128)(2,1)S(1)} %bitcast.13, bf16[16,256,256]{2,1,0:T(8,128)(2,1)S(1)} %copy-done.1, ...), custom_call_target="tpu_custom_call" | custom-call | flops 1006632960 | bytes 6553600 | tf_op jit(solution)/shard_map/pallas_call | solution.py:331
  19.9 0.0 copy-start.4
  20.0 2.9 %collective-permute-start.2 = (bf16[12,128,128]{2,1,0:T(8,128)(2,1)S(1)}, bf16[12,128,128]{2,1,0:T(8,128)(2,1)S(1)}, u32[]{:S(2)}, u32[]{:S(2)}) collective-permute-start(bf16[12,128,128]{2,1,0:T(8,128)(2,1)S(1)} %get-tuple-element.24), channel_id=1, source_target_pairs={{0,2},{2,4},{4,6},{6,8},{8,10},{10,12},{12,14},{1,3},{3,5},{5,7},{... | collective-permute-start | bytes 1179656 | tf_op jit(solution)/shard_map/ppermute | solution.py:342
  22.9 3.8 %shard_map.108 = (f32[25,256,128]{2,1,0:T(8,128)S(1)}, f32[25,128]{1,0:T(8,128)S(1)}, bf16[1280,1280]{1,0:T(8,128)(2,1)}, s32[25]{0:T(128)S(1)}) custom-call(s32[2,25]{1,0:T(2,128)S(1)} %bitcast.17, bf16[1280,1280]{1,0:T(8,128)(2,1)S(1)} %get-tuple-element.21.picture, bf16[256,256]{1,0:T(8,128)(2,1)S(1)} %copy-done.3, f32[1,128]{1,0:T(1,128)S(1)} %copy-done.5, ...), custom_call_target="tpu_custom_call" | custom-call | flops 629145600 | bytes 3276800 | tf_op jit(solution)/shard_map/pallas_call | solution.py:344
  26.7 0.7 %collective-permute-done.3.previous = bf16[13,128,128]{2,1,0:T(8,128)(2,1)S(1)} collective-permute-done((bf16[13,128,128]{2,1,0:T(8,128)(2,1)S(1)}, bf16[13,128,128]{2,1,0:T(8,128)(2,1)S(1)}, u32[]{:S(2)}, u32[]{:S(2)}) %collective-permute-start.3) | collective-permute-done | bytes 426016 | tf_op jit(solution)/shard_map/ppermute | solution.py:330
  27.4 2.5 %shard_map.109.rest_0_ = f32[25,128,128]{2,1,0:T(8,128)} custom-call(s32[25]{0:T(128)S(1)} %get-tuple-element.23.order, bf16[13,128,128]{2,1,0:T(8,128)(2,1)S(1)} %collective-permute-done.3.previous, f32[25,256,128]{2,1,0:T(8,128)S(1)} %get-tuple-element.25.spectra, f32[25,128]{1,0:T(8,128)S(1)} %get-tuple-element.26.powers, bf16[256,256]{1,0:T(8,128)(2,1)S(1)} %copy-done.3, ...), custom_call_target="tpu_custom_call" | custom-call | flops 436207616 | bytes 2981888 | tf_op jit(solution)/shard_map/pallas_call | solution.py:367
  29.9 4.7 %collective-permute-done.2.previous = bf16[12,128,128]{2,1,0:T(8,128)(2,1)S(1)} collective-permute-done((bf16[12,128,128]{2,1,0:T(8,128)(2,1)S(1)}, bf16[12,128,128]{2,1,0:T(8,128)(2,1)S(1)}, u32[]{:S(2)}, u32[]{:S(2)}) %collective-permute-start.2) | collective-permute-done | bytes 393248 | tf_op jit(solution)/shard_map/ppermute | solution.py:342
  34.6 2.3 %shard_map.110 = f32[25,128,128]{2,1,0:T(8,128)} custom-call(s32[25]{0:T(128)S(1)} %get-tuple-element.23.order, bf16[12,128,128]{2,1,0:T(8,128)(2,1)S(1)} %collective-permute-done.2.previous, f32[25,256,128]{2,1,0:T(8,128)S(1)} %get-tuple-element.25.spectra, f32[25,128]{1,0:T(8,128)S(1)} %get-tuple-element.26.powers, ...), custom_call_target="tpu_custom_call", output_to_operand_aliasing={{}: (8, {})} | custom-call | flops 402653184 | bytes 2752512 | tf_op jit(solution)/shard_map/pallas_call | solution.py:367
  (9 shorter events, 0.0 us)
Async XLA Ops:
  0.6 0.7 %copy-start.8 = (s32[1,25,2]{1,2,0:T(2,128)S(1)}, s32[1,25,2]{1,2,0:T(2,128)}, u32[]{:S(2)}) copy-start(s32[1,25,2]{1,2,0:T(2,128)} %param.13) | copy-start | bytes 604
  0.6 4.2 %copy-start = (bf16[1,25,256,256]{3,2,1,0:T(8,128)(2,1)S(1)}, bf16[1,25,256,256]{3,2,1,0:T(8,128)(2,1)}, u32[]{:S(2)}) copy-start(bf16[1,25,256,256]{3,2,1,0:T(8,128)(2,1)} %param.9) | copy-start | bytes 9830404
  0.7 4.2 %copy-start.1 = (bf16[16,256,256]{2,1,0:T(8,128)(2,1)S(1)}, bf16[16,256,256]{2,1,0:T(8,128)(2,1)}, u32[]{:S(2)}) copy-start(bf16[16,256,256]{2,1,0:T(8,128)(2,1)} %table.5) | copy-start | bytes 6291460
  0.7 4.2 %copy-start.6 = (s32[1,25,3,2]{1,3,2,0:T(2,128)S(1)}, s32[1,25,3,2]{1,3,2,0:T(2,128)}, u32[]{:S(2)}) copy-start(s32[1,25,3,2]{1,3,2,0:T(2,128)} %param.11) | copy-start | bytes 1804
  0.7 4.2 %copy-start.7 = (s32[1,25,3]{1,0,2:T(1,128)S(1)}, s32[1,25,3]{1,0,2:T(1,128)}, u32[]{:S(2)}) copy-start(s32[1,25,3]{1,0,2:T(1,128)} %param.10) | copy-start | bytes 904
  0.7 6.4 %collective-permute-start.1 = (bf16[25,256,256]{2,1,0:T(8,128)(2,1)}, bf16[25,256,256]{2,1,0:T(8,128)(2,1)S(1)}, u32[]{:S(2)}, u32[]{:S(2)}) collective-permute-start(bf16[25,256,256]{2,1,0:T(8,128)(2,1)} %bitcast.10), channel_id=1, source_target_pairs={{0,1},{1,0},{2,3},{3,2},{4,5},{5,4},{6,7},{7,6},{8,9},{9,8},{10,11... | collective-permute-start | bytes 9830408 | tf_op jit(solution)/shard_map/ppermute | solution.py:291
  1.3 5.8 %collective-permute-start = (s32[2,25]{1,0:T(2,128)S(1)}, s32[2,25]{1,0:T(2,128)S(1)}, u32[]{:S(2)}, u32[]{:S(2)}) collective-permute-start(s32[2,25]{1,0:T(2,128)S(1)} %bitcast.16), channel_id=1, source_target_pairs={{2,0},{4,2},{6,4},{8,6},{10,8},{12,10},{14,12},{3,1},{5,3},{7,5},{... | collective-permute-start | bytes 608 | tf_op jit(solution)/shard_map/ppermute | solution.py:299
  11.9 15.5 %collective-permute-start.3 = (bf16[13,128,128]{2,1,0:T(8,128)(2,1)S(1)}, bf16[13,128,128]{2,1,0:T(8,128)(2,1)S(1)}, u32[]{:S(2)}, u32[]{:S(2)}) collective-permute-start(bf16[13,128,128]{2,1,0:T(8,128)(2,1)S(1)} %get-tuple-element.27), channel_id=1, source_target_pairs={{0,2},{2,4},{4,6},{6,8},{8,10},{10,12},{12,14},{1,3},{3,5},{5,7},{... | collective-permute-start | bytes 1277960 | tf_op jit(solution)/shard_map/ppermute | solution.py:330
  16.1 6.8 %copy-start.2 = (bf16[256,256]{1,0:T(8,128)(2,1)S(1)}, bf16[256,256]{1,0:T(8,128)(2,1)}, u32[]{:S(2)}) copy-start(bf16[256,256]{1,0:T(8,128)(2,1)} %constant.10.clone.down) | copy-start | bytes 393220
  16.1 6.8 %copy-start.3 = (bf16[256,256]{1,0:T(8,128)(2,1)S(1)}, bf16[256,256]{1,0:T(8,128)(2,1)}, u32[]{:S(2)}) copy-start(bf16[256,256]{1,0:T(8,128)(2,1)} %constant.8.clone.forward) | copy-start | bytes 393220
  16.2 6.8 %copy-start.5 = (f32[1,128]{1,0:T(1,128)S(1)}, f32[1,128]{1,0:T(1,128)}, u32[]{:S(2)}) copy-start(f32[1,128]{1,0:T(1,128)} %constant.9.clone.lowest) | copy-start | bytes 1540
  19.9 7.5 %copy-start.4 = (bf16[256,128]{1,0:T(8,128)(2,1)S(1)}, bf16[256,128]{1,0:T(8,128)(2,1)}, u32[]{:S(2)}) copy-start(bf16[256,128]{1,0:T(8,128)(2,1)} %constant.11.clone.back) | copy-start | bytes 196612
  20.0 14.7 %collective-permute-start.2 = (bf16[12,128,128]{2,1,0:T(8,128)(2,1)S(1)}, bf16[12,128,128]{2,1,0:T(8,128)(2,1)S(1)}, u32[]{:S(2)}, u32[]{:S(2)}) collective-permute-start(bf16[12,128,128]{2,1,0:T(8,128)(2,1)S(1)} %get-tuple-element.24), channel_id=1, source_target_pairs={{0,2},{2,4},{4,6},{6,8},{8,10},{10,12},{12,14},{1,3},{3,5},{5,7},{... | collective-permute-start | bytes 1179656 | tf_op jit(solution)/shard_map/ppermute | solution.py:342

commit v9 on v8

--- a/solution.py
+++ b/solution.py
@@ -161,12 +161,12 @@
         others[r] = left.astype(BF16)
     down = window_order(corners, order, patches, grid)
     given = source, table, plan, lefts, others
+    outer = jnp.where(down == 0, 0, early_rows(grid))
+    for n in range(grid - early_rows(grid)):
+        fill_row(early, outer + n - down, warp_row(outer + n, False, grid, *given))
     for row in range(grid):
         if always_early(row, grid):
             fill_row(early, row - down, warp_row(row, True, grid, *given))
-    outer = jnp.where(down == 0, 0, early_rows(grid))
-    for n in range(grid - early_rows(grid)):
-        fill_row(early, outer + n - down, warp_row(outer + n, False, grid, *given))
     cut_windows(early, corners, [order[n] for n in range(out.shape[0])], down * BS, bands, out)
 
 

time: 37.4 us -> 37.2 us (level)
  no operation moved by 1% of the time
where the time goes in v9:
time: 37.2 us; the launch traced here: 36.9 us
  Pallas kernels  19.1 us (51%)
  starting transfers between devices  10.8 us (29%)
  waiting for transfers between devices  5.42 us (15%)
  between operations  1.01 us (3%)
  local copies, waits for them, and re-layouts  0.59 us (2%)
    pallas_call x2, Pallas kernels, shards(): pl.pallas_call(functools.partial(match_kernel, share), out_shape=jax.Shap...  4.86 us
    ppermute x1, waiting for transfers between devices, shards(): arrivals.append(lax.ppermute(sent, 'sec', onward))  4.72 us
    pallas_call x1, Pallas kernels, shards(): pl.pallas_call(functools.partial(early_kernel, grid, patches), out_shape=...  4.54 us
    ppermute x1, starting transfers between devices, shards(): arrivals = [lax.ppermute(sent, 'sec', onward)]  4.22 us
    pallas_call x1, Pallas kernels, shards(): pl.pallas_call(functools.partial(late_kernel, grid, patches), out_shape=(...  3.78 us
    pallas_call x1, Pallas kernels, shards(): pl.pallas_call(functools.partial(own_kernel, patches, grid), out_shape=(j...  3.75 us
    ppermute x1, starting transfers between devices, shards(): lax.ppermute(asked, 'sec', [(i + 1, i) for i in range(sections - 1)])  3.56 us
    ppermute x1, starting transfers between devices, shards(): arrivals.append(lax.ppermute(sent, 'sec', onward))  2.94 us
  transfers between devices with their start and end apart: 4, of which 2 were waited for; matrix products, arithmetic and copies ran while one was open for 0% of the time, Pallas kernels for 33%

profile of v9, /device:TPU:10, one launch (start us, length us, event | category | flops | bytes accessed | tf_op | source)
XLA Modules:
  0.0 36.9 jit_solution(2845669547211142591)
XLA Ops:
  0.6 0.0 copy-start.8
  0.6 0.0 copy-start
  0.7 0.0 copy-start.1
  0.7 0.0 copy-start.6
  0.7 0.0 copy-start.7
  0.7 0.1 collective-permute-start.1
  0.8 0.5 %copy-done.8 = s32[1,25,2]{1,2,0:T(2,128)S(1)} copy-done((s32[1,25,2]{1,2,0:T(2,128)S(1)}, s32[1,25,2]{1,2,0:T(2,128)}, u32[]{:S(2)}) %copy-start.8) | copy-done | bytes 224
  1.3 3.6 %collective-permute-start = (s32[2,25]{1,0:T(2,128)S(1)}, s32[2,25]{1,0:T(2,128)S(1)}, u32[]{:S(2)}, u32[]{:S(2)}) collective-permute-start(s32[2,25]{1,0:T(2,128)S(1)} %bitcast.16), channel_id=1, source_target_pairs={{2,0},{4,2},{6,4},{8,6},{10,8},{12,10},{14,12},{3,1},{5,3},{7,5},{... | collective-permute-start | bytes 608 | tf_op jit(solution)/shard_map/ppermute | solution.py:299
  4.9 2.2 %shard_map.105 = (bf16[15,256,256]{2,1,0:T(8,128)(2,1)S(1)}, s32[101]{0:T(128)S(1)}) custom-call(s32[3,1,25]{2,1,0:T(1,128)S(1)} %bitcast.15, s32[3,2,25]{2,1,0:T(2,128)S(1)} %bitcast.14, bf16[25,256,256]{2,1,0:T(8,128)(2,1)S(1)} %bitcast.11, bf16[16,256,256]{2,1,0:T(8,128)(2,1)S(1)} %copy-done.1, f32[8,128]{1,0:T(8,128)S(1)} %shard_map.104.gate), custom_call_target="tpu_custom_call" | custom-call | flops 503316480 | bytes 5242880 | tf_op jit(solution)/shard_map/pallas_call | solution.py:306
  7.1 0.0 collective-permute-done.corners
  7.1 0.0 collective-permute-done.1.other
  7.1 4.5 %shard_map.106 = (bf16[768,1280]{1,0:T(8,128)(2,1)S(1)}, bf16[12,256,256]{2,1,0:T(8,128)(2,1)S(1)}, bf16[13,128,128]{2,1,0:T(8,128)(2,1)S(1)}) custom-call(s32[101]{0:T(128)S(1)} %get-tuple-element.16.plan, s32[2,25]{1,0:T(2,128)S(1)} %collective-permute-done.corners, bf16[25,256,256]{2,1,0:T(8,128)(2,1)S(1)} %bitcast.12, ...), custom_call_target="tpu_custom_call" | custom-call | flops 1509949440 | bytes 11796480 | tf_op jit(solution)/shard_map/pallas_call | solution.py:318
  11.7 4.2 %collective-permute-start.3 = (bf16[13,128,128]{2,1,0:T(8,128)(2,1)S(1)}, bf16[13,128,128]{2,1,0:T(8,128)(2,1)S(1)}, u32[]{:S(2)}, u32[]{:S(2)}) collective-permute-start(bf16[13,128,128]{2,1,0:T(8,128)(2,1)S(1)} %get-tuple-element.27), channel_id=1, source_target_pairs={{0,2},{2,4},{4,6},{6,8},{8,10},{10,12},{12,14},{1,3},{3,5},{5,7},{... | collective-permute-start | bytes 1277960 | tf_op jit(solution)/shard_map/ppermute | solution.py:330
  15.9 0.0 copy-start.2
  15.9 0.0 copy-start.3
  15.9 0.0 copy-start.5
  15.9 3.8 %shard_map.107 = (bf16[1280,1280]{1,0:T(8,128)(2,1)S(1)}, bf16[12,128,128]{2,1,0:T(8,128)(2,1)S(1)}) custom-call(s32[101]{0:T(128)S(1)} %get-tuple-element.16.plan, s32[2,25]{1,0:T(2,128)S(1)} %collective-permute-done.corners, bf16[25,256,256]{2,1,0:T(8,128)(2,1)S(1)} %bitcast.13, bf16[16,256,256]{2,1,0:T(8,128)(2,1)S(1)} %copy-done.1, ...), custom_call_target="tpu_custom_call" | custom-call | flops 1006632960 | bytes 6553600 | tf_op jit(solution)/shard_map/pallas_call | solution.py:331
  19.7 0.0 copy-start.4
  19.7 2.9 %collective-permute-start.2 = (bf16[12,128,128]{2,1,0:T(8,128)(2,1)S(1)}, bf16[12,128,128]{2,1,0:T(8,128)(2,1)S(1)}, u32[]{:S(2)}, u32[]{:S(2)}) collective-permute-start(bf16[12,128,128]{2,1,0:T(8,128)(2,1)S(1)} %get-tuple-element.24), channel_id=1, source_target_pairs={{0,2},{2,4},{4,6},{6,8},{8,10},{10,12},{12,14},{1,3},{3,5},{5,7},{... | collective-permute-start | bytes 1179656 | tf_op jit(solution)/shard_map/ppermute | solution.py:342
  22.7 3.8 %shard_map.108 = (f32[25,256,128]{2,1,0:T(8,128)S(1)}, f32[25,128]{1,0:T(8,128)S(1)}, bf16[1280,1280]{1,0:T(8,128)(2,1)}, s32[25]{0:T(128)S(1)}) custom-call(s32[2,25]{1,0:T(2,128)S(1)} %bitcast.17, bf16[1280,1280]{1,0:T(8,128)(2,1)S(1)} %get-tuple-element.21.picture, bf16[256,256]{1,0:T(8,128)(2,1)S(1)} %copy-done.3, f32[1,128]{1,0:T(1,128)S(1)} %copy-done.5, ...), custom_call_target="tpu_custom_call" | custom-call | flops 629145600 | bytes 3276800 | tf_op jit(solution)/shard_map/pallas_call | solution.py:344
  26.5 0.7 %collective-permute-done.3.previous = bf16[13,128,128]{2,1,0:T(8,128)(2,1)S(1)} collective-permute-done((bf16[13,128,128]{2,1,0:T(8,128)(2,1)S(1)}, bf16[13,128,128]{2,1,0:T(8,128)(2,1)S(1)}, u32[]{:S(2)}, u32[]{:S(2)}) %collective-permute-start.3) | collective-permute-done | bytes 426016 | tf_op jit(solution)/shard_map/ppermute | solution.py:330
  27.2 2.5 %shard_map.109.rest_0_ = f32[25,128,128]{2,1,0:T(8,128)} custom-call(s32[25]{0:T(128)S(1)} %get-tuple-element.23.order, bf16[13,128,128]{2,1,0:T(8,128)(2,1)S(1)} %collective-permute-done.3.previous, f32[25,256,128]{2,1,0:T(8,128)S(1)} %get-tuple-element.25.spectra, f32[25,128]{1,0:T(8,128)S(1)} %get-tuple-element.26.powers, bf16[256,256]{1,0:T(8,128)(2,1)S(1)} %copy-done.3, ...), custom_call_target="tpu_custom_call" | custom-call | flops 436207616 | bytes 2981888 | tf_op jit(solution)/shard_map/pallas_call | solution.py:367
  29.7 4.7 %collective-permute-done.2.previous = bf16[12,128,128]{2,1,0:T(8,128)(2,1)S(1)} collective-permute-done((bf16[12,128,128]{2,1,0:T(8,128)(2,1)S(1)}, bf16[12,128,128]{2,1,0:T(8,128)(2,1)S(1)}, u32[]{:S(2)}, u32[]{:S(2)}) %collective-permute-start.2) | collective-permute-done | bytes 393248 | tf_op jit(solution)/shard_map/ppermute | solution.py:342
  34.4 2.4 %shard_map.110 = f32[25,128,128]{2,1,0:T(8,128)} custom-call(s32[25]{0:T(128)S(1)} %get-tuple-element.23.order, bf16[12,128,128]{2,1,0:T(8,128)(2,1)S(1)} %collective-permute-done.2.previous, f32[25,256,128]{2,1,0:T(8,128)S(1)} %get-tuple-element.25.spectra, f32[25,128]{1,0:T(8,128)S(1)} %get-tuple-element.26.powers, ...), custom_call_target="tpu_custom_call", output_to_operand_aliasing={{}: (8, {})} | custom-call | flops 402653184 | bytes 2752512 | tf_op jit(solution)/shard_map/pallas_call | solution.py:367
  (9 shorter events, 0.0 us)
Async XLA Ops:
  0.6 0.7 %copy-start.8 = (s32[1,25,2]{1,2,0:T(2,128)S(1)}, s32[1,25,2]{1,2,0:T(2,128)}, u32[]{:S(2)}) copy-start(s32[1,25,2]{1,2,0:T(2,128)} %param.13) | copy-start | bytes 604
  0.6 4.2 %copy-start = (bf16[1,25,256,256]{3,2,1,0:T(8,128)(2,1)S(1)}, bf16[1,25,256,256]{3,2,1,0:T(8,128)(2,1)}, u32[]{:S(2)}) copy-start(bf16[1,25,256,256]{3,2,1,0:T(8,128)(2,1)} %param.9) | copy-start | bytes 9830404
  0.7 4.2 %copy-start.1 = (bf16[16,256,256]{2,1,0:T(8,128)(2,1)S(1)}, bf16[16,256,256]{2,1,0:T(8,128)(2,1)}, u32[]{:S(2)}) copy-start(bf16[16,256,256]{2,1,0:T(8,128)(2,1)} %table.5) | copy-start | bytes 6291460
  0.7 4.2 %copy-start.6 = (s32[1,25,3,2]{1,3,2,0:T(2,128)S(1)}, s32[1,25,3,2]{1,3,2,0:T(2,128)}, u32[]{:S(2)}) copy-start(s32[1,25,3,2]{1,3,2,0:T(2,128)} %param.11) | copy-start | bytes 1804
  0.7 4.2 %copy-start.7 = (s32[1,25,3]{1,0,2:T(1,128)S(1)}, s32[1,25,3]{1,0,2:T(1,128)}, u32[]{:S(2)}) copy-start(s32[1,25,3]{1,0,2:T(1,128)} %param.10) | copy-start | bytes 904
  0.7 6.4 %collective-permute-start.1 = (bf16[25,256,256]{2,1,0:T(8,128)(2,1)}, bf16[25,256,256]{2,1,0:T(8,128)(2,1)S(1)}, u32[]{:S(2)}, u32[]{:S(2)}) collective-permute-start(bf16[25,256,256]{2,1,0:T(8,128)(2,1)} %bitcast.10), channel_id=1, source_target_pairs={{0,1},{1,0},{2,3},{3,2},{4,5},{5,4},{6,7},{7,6},{8,9},{9,8},{10,11... | collective-permute-start | bytes 9830408 | tf_op jit(solution)/shard_map/ppermute | solution.py:291
  1.3 5.8 %collective-permute-start = (s32[2,25]{1,0:T(2,128)S(1)}, s32[2,25]{1,0:T(2,128)S(1)}, u32[]{:S(2)}, u32[]{:S(2)}) collective-permute-start(s32[2,25]{1,0:T(2,128)S(1)} %bitcast.16), channel_id=1, source_target_pairs={{2,0},{4,2},{6,4},{8,6},{10,8},{12,10},{14,12},{3,1},{5,3},{7,5},{... | collective-permute-start | bytes 608 | tf_op jit(solution)/shard_map/ppermute | solution.py:299
  11.7 15.5 %collective-permute-start.3 = (bf16[13,128,128]{2,1,0:T(8,128)(2,1)S(1)}, bf16[13,128,128]{2,1,0:T(8,128)(2,1)S(1)}, u32[]{:S(2)}, u32[]{:S(2)}) collective-permute-start(bf16[13,128,128]{2,1,0:T(8,128)(2,1)S(1)} %get-tuple-element.27), channel_id=1, source_target_pairs={{0,2},{2,4},{4,6},{6,8},{8,10},{10,12},{12,14},{1,3},{3,5},{5,7},{... | collective-permute-start | bytes 1277960 | tf_op jit(solution)/shard_map/ppermute | solution.py:330
  15.9 6.8 %copy-start.2 = (bf16[256,256]{1,0:T(8,128)(2,1)S(1)}, bf16[256,256]{1,0:T(8,128)(2,1)}, u32[]{:S(2)}) copy-start(bf16[256,256]{1,0:T(8,128)(2,1)} %constant.10.clone.down) | copy-start | bytes 393220
  15.9 6.8 %copy-start.3 = (bf16[256,256]{1,0:T(8,128)(2,1)S(1)}, bf16[256,256]{1,0:T(8,128)(2,1)}, u32[]{:S(2)}) copy-start(bf16[256,256]{1,0:T(8,128)(2,1)} %constant.8.clone.forward) | copy-start | bytes 393220
  15.9 6.8 %copy-start.5 = (f32[1,128]{1,0:T(1,128)S(1)}, f32[1,128]{1,0:T(1,128)}, u32[]{:S(2)}) copy-start(f32[1,128]{1,0:T(1,128)} %constant.9.clone.lowest) | copy-start | bytes 1540
  19.7 7.5 %copy-start.4 = (bf16[256,128]{1,0:T(8,128)(2,1)S(1)}, bf16[256,128]{1,0:T(8,128)(2,1)}, u32[]{:S(2)}) copy-start(bf16[256,128]{1,0:T(8,128)(2,1)} %constant.11.clone.back) | copy-start | bytes 196612
  19.7 14.7 %collective-permute-start.2 = (bf16[12,128,128]{2,1,0:T(8,128)(2,1)S(1)}, bf16[12,128,128]{2,1,0:T(8,128)(2,1)S(1)}, u32[]{:S(2)}, u32[]{:S(2)}) collective-permute-start(bf16[12,128,128]{2,1,0:T(8,128)(2,1)S(1)} %get-tuple-element.24), channel_id=1, source_target_pairs={{0,2},{2,4},{4,6},{6,8},{8,10},{10,12},{12,14},{1,3},{3,5},{5,7},{... | collective-permute-start | bytes 1179656 | tf_op jit(solution)/shard_map/ppermute | solution.py:342
